TPU v7x, 256 devices: a whole 4x4x8 slice. The times are simulated.
256 devices in a mesh: seq: 64 (over z, x, core), head: 4 (over y).
Axes of the slice: x: 4, y: 4, z: 8, core: 2. Of those that a mesh axis runs over, the one named last changes fastest.
Arguments:
- queries: bfloat16 [73728, 32, 128], P(('seq', 'head')), may hold values from -4 to 4
- key_states: bfloat16 [73728, 4, 128], P(('seq', 'head')), may hold values from -4 to 4
- value_states: bfloat16 [73728, 4, 128], P(('seq', 'head')), may hold values from -6 to 6
- outputs: bfloat16 [73728, 32, 128], P(('seq', 'head')), may hold values from -6 to 6
- output_grad: bfloat16 [73728, 32, 128], P(('seq', 'head')), may hold values from -96 to 96
- logsumexp: float32 [73728, 32], P(('seq', 'head')), may hold values from 6.8 to 7.8
- random_owner: int32 [576, 3], replicated, may hold values from 0 to 63, all different within a row; in each aligned block of 9 rows (0 to 8, 9 to 17, ...) no two rows name the same one
- random_slot: int32 [576, 3], replicated, may hold values from 0 to 8
Outputs:
- query_grad: bfloat16 [73728, 32, 128], P(('seq', 'head'))
- key_grad: bfloat16 [73728, 4, 128], P(('seq', 'head'))
- value_grad: bfloat16 [73728, 4, 128], P(('seq', 'head'))
Inputs may be any that keep to these rules, and one draw needn't show every extreme that they name: `random_owner`: each row names 3 different indices. Within the 9 rows of one index of seq (aligned blocks of 9 rows), no index of seq appears more than 1 times, and some index appears exactly 1 times in some block.
All inputs are finite; a program needn't handle non-finite values.
Results may differ from a plain program's by a relative error of at most 0.005.
Values may be sent and summed in bfloat16 or wider, within the bound.
No kernel may reach another device: no remote copies, remote signals or barrier semaphores. Data moves between devices by JAX's collectives and lax.ppermute only.
A program may use at most 128 MiB of HBM per device.

v0:
```python
import jax
import jax.numpy as jnp
from jax import lax
from jax.sharding import PartitionSpec as P

HD = 128
BLK = 128
G = 2
RND = 3


def extended_2(value, sides, width):
    for axis, dim in sides:
        devices, length = (lax.axis_size(axis), value.shape[dim])
        up = [(i, (i + 1) % devices) for i in range(devices - 1)]
        down = [(j, i) for i, j in up]
        last = lax.slice_in_dim(value, length - width, length, axis=dim)
        leading = lax.slice_in_dim(value, 0, width, axis=dim)
        before = lax.ppermute(last, axis, up)
        after = lax.ppermute(leading, axis, down)
        value = jnp.concatenate([before, value, after], axis=dim)
    return value


def broadcast(value, axis, source):
    kept = jnp.where(lax.axis_index(axis) == source, value, 0).astype(value.dtype)
    return lax.psum(kept, axis)


def from_behind(value, axis, steps):
    count = lax.axis_size(axis)
    leading, last = (max(0, -steps), min(count, count - steps))
    return lax.ppermute(value, axis, [(source, source + steps) for source in range(leading, last)])


def block_grads(
    query_block, grad_block, logsum_block, delta_block, key_blocks, value_blocks, validity
):
    scaling = 1.0 / HD**0.5
    scores = (
        jnp.einsum("ighd,mjgd->mghij", query_block, key_blocks, preferred_element_type=jnp.float32)
        * scaling
    )
    weights = (
        jnp.exp(scores - jnp.transpose(logsum_block, (1, 2, 0))[None, :, :, :, None])
        * validity[:, None, None, None, None]
    )
    weights_rounded = weights.astype(jnp.bfloat16)
    weight_grad = jnp.einsum(
        "ighd,mjgd->mghij", grad_block, value_blocks, preferred_element_type=jnp.float32
    )
    score_grad = (
        weights * (weight_grad - jnp.transpose(delta_block, (1, 2, 0))[None, :, :, :, None])
    ).astype(jnp.bfloat16)
    query_part = (
        jnp.einsum("mghij,mjgd->ighd", score_grad, key_blocks, preferred_element_type=jnp.float32)
        * scaling
    )
    key_part = (
        jnp.einsum("mghij,ighd->mjgd", score_grad, query_block, preferred_element_type=jnp.float32)
        * scaling
    )
    value_part = jnp.einsum(
        "mghij,ighd->mjgd", weights_rounded, grad_block, preferred_element_type=jnp.float32
    )
    return (query_part, jnp.stack([key_part, value_part], axis=2))


def local_grads(query_split, grad_split, logsum_split, delta_split, chosen_kv, validity):

    def single_block(items):
        return block_grads(*items)

    return lax.map(
        single_block,
        (
            query_split,
            grad_split,
            logsum_split,
            delta_split,
            chosen_kv[:, :, :, 0],
            chosen_kv[:, :, :, 1],
            validity,
        ),
    )


def pair_lists(block_ids, owners, slots, blocks_local, block_count):
    window_ids = block_ids[:, None] + jnp.arange(-1, 2, dtype=jnp.int32)[None, :]
    random_ids = owners * blocks_local + slots
    window_ok = (window_ids >= G) & (window_ids <= block_count - 1)
    random_ok = (random_ids >= G) & (jnp.abs(random_ids - block_ids[:, None]) >= 2)
    validity = jnp.concatenate(
        [
            jnp.ones((block_ids.shape[0], G), jnp.float32),
            window_ok.astype(jnp.float32),
            random_ok.astype(jnp.float32),
        ],
        axis=1,
    )
    return (window_ids, random_ids, validity)


def per_device(
    queries, key_states, value_states, outputs, output_grad, logsumexp, random_owner, random_slot
):
    query_loc, key_loc, value_loc, out_loc, grad_loc = (
        lax.all_to_all(queries, "head", split_axis=1, concat_axis=0, tiled=True),
        lax.all_to_all(key_states, "head", split_axis=1, concat_axis=0, tiled=True),
        lax.all_to_all(value_states, "head", split_axis=1, concat_axis=0, tiled=True),
        lax.all_to_all(outputs, "head", split_axis=1, concat_axis=0, tiled=True),
        lax.all_to_all(output_grad, "head", split_axis=1, concat_axis=0, tiled=True),
    )
    logsum_loc = lax.all_to_all(logsumexp, "head", split_axis=1, concat_axis=0, tiled=True)
    delta_loc = jnp.einsum("thd,thd->th", grad_loc, out_loc, preferred_element_type=jnp.float32)
    tok_count = query_loc.shape[0]
    heads_local = query_loc.shape[1]
    kv_heads = key_loc.shape[1]
    group = heads_local // kv_heads
    blocks_local = tok_count // BLK
    seq_count = lax.axis_size("seq")
    seq_index = lax.axis_index("seq")
    block_count = seq_count * blocks_local
    rows_each = blocks_local * RND
    most_slots = max(1, (rows_each + seq_count - 1) // seq_count)
    query_split = query_loc.reshape(blocks_local, BLK, kv_heads, group, HD)
    grad_split = grad_loc.reshape(blocks_local, BLK, kv_heads, group, HD)
    logsum_split = logsum_loc.reshape(blocks_local, BLK, kv_heads, group)
    delta_split = delta_loc.reshape(blocks_local, BLK, kv_heads, group)
    kv_loc = jnp.stack([key_loc, value_loc], axis=1)
    kv_blocks = kv_loc.reshape(blocks_local, BLK, 2, kv_heads, HD)
    block_ids = seq_index * blocks_local + jnp.arange(blocks_local, dtype=jnp.int32)
    my_owner = lax.dynamic_slice_in_dim(random_owner, seq_index * blocks_local, blocks_local, 0)
    my_slot = lax.dynamic_slice_in_dim(random_slot, seq_index * blocks_local, blocks_local, 0)
    window_ids, random_ids, validity = pair_lists(
        block_ids, my_owner, my_slot, blocks_local, block_count
    )
    owner_table = random_owner.reshape(seq_count, rows_each)
    slot_table = random_slot.reshape(seq_count, rows_each)
    entry_pos = jnp.arange(rows_each, dtype=jnp.int32)
    before_mask = entry_pos[None, :] < entry_pos[:, None]
    same_owner = owner_table[:, :, None] == owner_table[:, None, :]
    rank_table = jnp.sum((same_owner & before_mask[None, :, :]).astype(jnp.int32), axis=2)
    my_rank = lax.dynamic_slice_in_dim(rank_table, seq_index, 1, 0).reshape(blocks_local, RND)
    slot_ids = jnp.arange(most_slots, dtype=jnp.int32)
    local_ids = jnp.arange(blocks_local, dtype=jnp.int32)
    local_hits = (
        (owner_table == seq_index)[:, :, None, None]
        & (rank_table[:, :, None, None] == slot_ids[None, None, :, None])
        & (slot_table[:, :, None, None] == local_ids[None, None, None, :])
    )
    selector = jnp.sum(local_hits.astype(jnp.float32), axis=1)
    extended = extended_2(kv_loc, (("seq", 0),), BLK)
    ext_blocks = extended.reshape(blocks_local + 2, BLK, 2, kv_heads, HD)
    window_kv = jnp.stack(
        [ext_blocks[offset : offset + blocks_local] for offset in range(3)], axis=1
    )
    global_kv = broadcast(kv_loc[: G * BLK], "seq", 0).reshape(G, BLK, 2, kv_heads, HD)
    outgoing = jnp.einsum(
        "pml,lbtgd->pmbtgd",
        selector.astype(jnp.bfloat16),
        kv_blocks,
        preferred_element_type=jnp.float32,
    ).astype(jnp.bfloat16)
    fetched = lax.all_to_all(outgoing, "seq", split_axis=0, concat_axis=0, tiled=True)
    random_kv = fetched[my_owner, my_rank]
    global_wide = jnp.broadcast_to(global_kv[None], (blocks_local,) + global_kv.shape)
    chosen = jnp.concatenate([global_wide, window_kv, random_kv], axis=1)
    query_part, kv_part = local_grads(
        query_split, grad_split, logsum_split, delta_split, chosen, validity
    )
    global_part = jnp.sum(kv_part[:, :G], axis=0)
    window_part = kv_part[:, G : G + 3]
    random_part = kv_part[:, G + 3 :]
    global_total = lax.psum(global_part, "seq")
    padded_parts = [
        jnp.pad(window_part[:, offset], ((offset, 2 - offset), (0, 0), (0, 0), (0, 0), (0, 0)))
        for offset in range(3)
    ]
    ext_grad = padded_parts[0] + padded_parts[1] + padded_parts[2]
    own_grad = ext_grad[1 : blocks_local + 1]
    flat_target = (my_owner * most_slots + my_rank).reshape(-1)
    owner_onehot = (
        flat_target[None, :] == jnp.arange(seq_count * most_slots, dtype=jnp.int32)[:, None]
    ).astype(jnp.float32)
    returning = jnp.dot(
        owner_onehot,
        random_part.reshape(rows_each, -1),
        precision=lax.Precision.HIGHEST,
        preferred_element_type=jnp.float32,
    )
    returning = returning.reshape(seq_count, most_slots, BLK, 2, kv_heads, HD)
    from_upper = from_behind(ext_grad[0].astype(jnp.bfloat16), "seq", -1).astype(jnp.float32)
    from_lower = from_behind(ext_grad[blocks_local + 1].astype(jnp.bfloat16), "seq", 1).astype(
        jnp.float32
    )
    returned = lax.all_to_all(returning, "seq", split_axis=0, concat_axis=0, tiled=True)
    own_grad = own_grad.at[blocks_local - 1].add(from_upper)
    own_grad = own_grad.at[0].add(from_lower)
    own_grad = own_grad + jnp.einsum(
        "pml,pmbtgd->lbtgd",
        selector,
        returned,
        precision=lax.Precision.HIGHEST,
        preferred_element_type=jnp.float32,
    )
    global_here = jnp.where(seq_index == 0, global_total, jnp.zeros_like(global_total))
    own_grad = own_grad.at[:G].add(global_here)
    kv_grad = own_grad.reshape(tok_count, 2, kv_heads, HD)
    query_grad_loc = query_part.reshape(tok_count, heads_local, HD).astype(jnp.bfloat16)
    key_grad_loc = kv_grad[:, 0].astype(jnp.bfloat16)
    value_grad_loc = kv_grad[:, 1].astype(jnp.bfloat16)
    query_grad, key_grad, value_grad = (
        lax.all_to_all(query_grad_loc, "head", split_axis=0, concat_axis=1, tiled=True),
        lax.all_to_all(key_grad_loc, "head", split_axis=0, concat_axis=1, tiled=True),
        lax.all_to_all(value_grad_loc, "head", split_axis=0, concat_axis=1, tiled=True),
    )
    return (query_grad, key_grad, value_grad)


def solution(mesh):
    placed = (
        P(("seq", "head"), None, None),
        P(("seq", "head"), None, None),
        P(("seq", "head"), None, None),
        P(("seq", "head"), None, None),
        P(("seq", "head"), None, None),
        P(("seq", "head"), None),
        P(),
        P(),
    )
    return jax.shard_map(
        per_device,
        mesh=mesh,
        in_specs=placed,
        out_specs=(
            P(("seq", "head"), None, None),
            P(("seq", "head"), None, None),
            P(("seq", "head"), None, None),
        ),
        check_vma=False,
    )
```

profile of v0, /device:TPU:2, one launch (start us, length us, event | category | flops | bytes accessed | tf_op | source)
XLA Modules:
  0.0 798.1 jit_solution(15851126505593233173)
XLA Ops:
  7.2 4.5 all-to-all-start.4
  13.4 3.8 all-to-all-done.4
  17.2 3.5 all-to-all-start
  22.4 5.1 all-to-all-done
  27.5 3.5 all-to-all-start.1
  30.9 4.0 copy.270
  34.9 2.8 all-to-all-done.1
  37.7 4.6 all-to-all-start.3
  42.3 4.0 copy.278
  46.3 21.7 %all-to-all-done.3 = bf16[288,32,128]{2,0,1:T(8,128)(2,1)} async-done(((bf16[288,32,128]{2,0,1:T(8,128)(2,1)}), bf16[288,32,128]{2,0,1:T(8,128)(2,1)}, u32[]{:S(2)}, u32[]{:S(2)}) %all-to-all-start.3) | async-done | bytes 2359328 | tf_op jit(solution)/shard_map/all_to_all | solution.py:108
  68.0 4.5 all-to-all-start.6
  72.5 4.0 copy.274
  76.5 20.8 %all-to-all-done.6 = bf16[288,32,128]{2,0,1:T(8,128)(2,1)} async-done(((bf16[288,32,128]{2,0,1:T(8,128)(2,1)}), bf16[288,32,128]{2,0,1:T(8,128)(2,1)}, u32[]{:S(2)}, u32[]{:S(2)}) %all-to-all-start.6) | async-done | bytes 2359328 | tf_op jit(solution)/shard_map/all_to_all | solution.py:111
  97.4 4.5 all-to-all-start.5
  104.9 6.3 copy.262
  111.3 14.5 %all-to-all-done.5 = bf16[288,32,128]{2,0,1:T(8,128)(2,1)} async-done(((bf16[288,32,128]{2,0,1:T(8,128)(2,1)}), bf16[288,32,128]{2,0,1:T(8,128)(2,1)}, u32[]{:S(2)}, u32[]{:S(2)}) %all-to-all-start.5) | async-done | bytes 2359328 | tf_op jit(solution)/shard_map/all_to_all | solution.py:112
  125.8 12.2 %all-to-all-start.2 = ((bf16[64,1,128,2,1,128]{5,3,2,4,1,0:T(2,128)(2,1)}), bf16[64,1,128,2,1,128]{5,3,2,4,1,0:T(2,128)(2,1)}, u32[]{:S(2)}, u32[]{:S(2)}) async-start(bf16[64,1,128,2,1,128]{5,3,2,4,1,0:T(2,128)(2,1)} %copy.262), calls=%async_computation.2 | async-start | bytes 8388608 | tf_op jit(solution)/shard_map/all_to_all | solution.py:165
  143.0 2.3 collective-permute-start
  145.3 186.5 %all-reduce.6.cloned.1.call-done = bf16[2,128,2,128]{3,1,0,2:T(8,128)(2,1)} async-done(((bf16[2,128,2,128]{3,1,0,2:T(8,128)(2,1)}), bf16[2,128,2,128]{3,1,0,2:T(8,128)(2,1)}) %all-reduce.6.cloned.1.call-update) | async-done | bytes 131088 | tf_op jit(solution)/shard_map/psum | solution.py:27
  337.0 4.0 copy.272
  341.0 2.6 copy.280
  343.6 2.6 copy.276
  348.4 5.4 copy.368
  353.8 4.2 gather_fusion
  358.1 3.3 constant_dynamic-update-slice_fusion.1
  361.3 6.4 slice_bitcast_fusion
  367.7 109.1 %while.15 = (s32[]{:T(128)}, bf16[9,128,1,8,128]{4,3,1,0,2:T(8,128)(2,1)}, f32[9,8,128,2,1,128]{2,5,1,3,4,0:T(8,128)}, bf16[9,8,128,1,128]{4,2,1,3,0:T(8,128)(2,...) while((s32[]{:T(128)}, ...), condition=%wide.region_4.5_spmd, body=%wide.region_3.4_spmd.sunk | while | flops 1353318400 | bytes 26243352 | solution.py:74
  372.3 2.2 fusion.103
  384.4 2.2 fusion.103
  420.7 2.2 fusion.103
  432.8 2.2 fusion.103
  476.7 2.2 slice.179
  479.0 4.8 copy.296
  483.7 6.2 reshape.406
  489.9 4.9 reshape.407
  494.9 5.8 fusion.52
  500.7 9.8 %copy.298 = f32[64,1,128,2,1,128]{5,3,2,4,1,0:T(2,128)} copy(f32[64,1,128,2,1,128]{5,0,3,2,4,1:T(8,128)S(1)} %fusion.52) | data formatting | bytes 16777216 | tf_op jit(solution)/shard_map/dot_general | solution.py:186
  510.5 8.3 %all-to-all-start.8 = ((f32[64,1,128,2,1,128]{5,3,2,4,1,0:T(2,128)}), f32[64,1,128,2,1,128]{5,3,2,4,1,0:T(2,128)}, u32[]{:S(2)}, u32[]{:S(2)}) async-start(f32[64,1,128,2,1,128]{5,3,2,4,1,0:T(2,128)} %copy.298), calls=%async_computation.8 | async-start | bytes 16777216 | tf_op jit(solution)/shard_map/all_to_all | solution.py:197
  518.9 9.6 %copy.289 = f32[9,8,128,2,1,128]{5,2,3,0,4,1:T(8,128)} copy(f32[9,8,128,2,1,128]{2,5,1,3,4,0:T(8,128)} %get-tuple-element.93) | data formatting | bytes 18874368 | tf_op jit(solution)/shard_map/while | solution.py:74
  536.4 2.3 collective-permute-start.3
  538.8 168.1 %all-to-all-done.8 = f32[64,1,128,2,1,128]{5,3,2,4,1,0:T(2,128)} async-done(((f32[64,1,128,2,1,128]{5,3,2,4,1,0:T(2,128)}), f32[64,1,128,2,1,128]{5,3,2,4,1,0:T(2,128)}, u32[]{:S(2)}, u32[]{:S(2)}) %all-to-all-start.8) | async-done | bytes 8388640 | tf_op jit(solution)/shard_map/all_to_all | solution.py:197
  706.9 4.5 all-to-all-start.7
  713.3 12.3 %fusion.46 = f32[9,128,2,128]{3,0,2,1:T(8,128)S(1)} fusion(f32[64,1,128,2,1,128]{5,3,2,4,1,0:T(2,128)} %all-to-all-done.8, f32[64,9]{0,1:T(8,128)S(1)} %fusion.61), kind=kOutput, calls=%fused_computation.43 | convolution fusion | flops 226492416 | bytes 9570560 | tf_op jit(solution)/shard_map/pml,pmbtgd->lbtgd/dot_general | solution.py:200
  726.4 37.2 %all-reduce.8.cloned.1.call-done = f32[2,128,2,1,128]{4,1,3,2,0:T(8,128)} async-done(((f32[2,128,2,1,128]{4,1,3,2,0:T(8,128)}), f32[2,128,2,1,128]{4,1,3,2,0:T(8,128)}) %all-reduce.8.cloned.1.call-update) | async-done | bytes 262160 | tf_op jit(solution)/shard_map/psum | solution.py:175
  766.0 4.3 all-to-all-start.9
  771.9 6.7 all-to-all-done.9
  778.6 3.5 all-to-all-start.10
  785.1 4.5 all-to-all-done.10
  (196 shorter events, 137.3 us)
Async XLA Ops:
  7.2 10.0 %all-to-all-start.4 = ((f32[288,4,8]{0,2,1:T(8,128)}), f32[288,4,8]{0,2,1:T(8,128)S(1)}, u32[]{:S(2)}, u32[]{:S(2)}) async-start(f32[288,4,8]{0,2,1:T(8,128)} %bitcast.352), calls=%async_computation.4 | async-start | bytes 98304 | tf_op jit(solution)/shard_map/all_to_all | solution.py:114
  17.2 10.3 %all-to-all-start = ((bf16[288,4,128]{2,0,1:T(8,128)(2,1)}), bf16[288,4,128]{2,0,1:T(8,128)(2,1)S(1)}, u32[]{:S(2)}, u32[]{:S(2)}) async-start(bf16[288,4,128]{2,0,1:T(8,128)(2,1)} %copy.249), calls=%async_computation | async-start | bytes 589824 | tf_op jit(solution)/shard_map/all_to_all | solution.py:109
  27.5 10.3 %all-to-all-start.1 = ((bf16[288,4,128]{2,0,1:T(8,128)(2,1)}), bf16[288,4,128]{2,0,1:T(8,128)(2,1)S(1)}, u32[]{:S(2)}, u32[]{:S(2)}) async-start(bf16[288,4,128]{2,0,1:T(8,128)(2,1)} %copy.250), calls=%async_computation.1 | async-start | bytes 589824 | tf_op jit(solution)/shard_map/all_to_all | solution.py:110
  37.7 30.3 %all-to-all-start.3 = ((bf16[288,32,128]{2,0,1:T(8,128)(2,1)}), bf16[288,32,128]{2,0,1:T(8,128)(2,1)}, u32[]{:S(2)}, u32[]{:S(2)}) async-start(bf16[288,32,128]{2,0,1:T(8,128)(2,1)} %copy.270), calls=%async_computation.3 | async-start | bytes 4718592 | tf_op jit(solution)/shard_map/all_to_all | solution.py:108
  68.0 29.3 %all-to-all-start.6 = ((bf16[288,32,128]{2,0,1:T(8,128)(2,1)}), bf16[288,32,128]{2,0,1:T(8,128)(2,1)}, u32[]{:S(2)}, u32[]{:S(2)}) async-start(bf16[288,32,128]{2,0,1:T(8,128)(2,1)} %copy.278), calls=%async_computation.6 | async-start | bytes 4718592 | tf_op jit(solution)/shard_map/all_to_all | solution.py:111
  76.5 25.4 %copy-start.2 = (s32[576,3]{0,1:T(4,128)S(1)}, s32[576,3]{0,1:T(4,128)}, u32[]{:S(2)}) copy-start(s32[576,3]{0,1:T(4,128)} %param.23) | copy-start | bytes 20740
  76.5 25.8 %copy-start.1 = (s32[576,3]{0,1:T(4,128)S(1)}, s32[576,3]{0,1:T(4,128)}, u32[]{:S(2)}) copy-start(s32[576,3]{0,1:T(4,128)} %param.22) | copy-start | bytes 20740
  97.4 28.4 %all-to-all-start.5 = ((bf16[288,32,128]{2,0,1:T(8,128)(2,1)}), bf16[288,32,128]{2,0,1:T(8,128)(2,1)}, u32[]{:S(2)}, u32[]{:S(2)}) async-start(bf16[288,32,128]{2,0,1:T(8,128)(2,1)} %copy.274), calls=%async_computation.5 | async-start | bytes 4718592 | tf_op jit(solution)/shard_map/all_to_all | solution.py:112
  125.8 222.6 %all-to-all-start.2 = ((bf16[64,1,128,2,1,128]{5,3,2,4,1,0:T(2,128)(2,1)}), bf16[64,1,128,2,1,128]{5,3,2,4,1,0:T(2,128)(2,1)}, u32[]{:S(2)}, u32[]{:S(2)}) async-start(bf16[64,1,128,2,1,128]{5,3,2,4,1,0:T(2,128)(2,1)} %copy.262), calls=%async_computation.2 | async-start | bytes 8388608 | tf_op jit(solution)/shard_map/all_to_all | solution.py:165
  138.0 193.8 %all-reduce.6.cloned.1.call-start = ((), (), s32[]{:S(2)}) async-start(), calls=%async_computation.11 | async-start | bytes 262144 | tf_op jit(solution)/shard_map/psum | solution.py:27
  141.0 193.1 %collective-permute-start.1 = (bf16[128,2,1,128]{3,0,2,1:T(8,128)(2,1)S(1)}, bf16[128,2,1,128]{3,0,2,1:T(8,128)(2,1)S(1)}, u32[]{:S(2)}, u32[]{:S(2)}) collective-permute-start(bf16[128,2,1,128]{3,0,2,1:T(8,128)(2,1)S(1)} %get-tuple-element.194), channel_id=1, source_target_pairs={{4,0},{8,4},{12,8},{16,12},{20,16},{24,20},{28,24},{32,28},{36,32}... | collective-permute-start | bytes 196616 | tf_op jit(solution)/shard_map/ppermute | solution.py:20
  143.0 191.0 %collective-permute-start = (bf16[128,2,1,128]{3,0,2,1:T(8,128)(2,1)S(1)}, bf16[128,2,1,128]{3,0,2,1:T(8,128)(2,1)S(1)}, u32[]{:S(2)}, u32[]{:S(2)}) collective-permute-start(bf16[128,2,1,128]{3,0,2,1:T(8,128)(2,1)S(1)} %get-tuple-element.195), channel_id=1, source_target_pairs={{0,4},{4,8},{8,12},{12,16},{16,20},{20,24},{24,28},{28,32},{32,36}... | collective-permute-start | bytes 196616 | tf_op jit(solution)/shard_map/ppermute | solution.py:19
  489.9 4.9 copy-start.3
  510.5 196.4 %all-to-all-start.8 = ((f32[64,1,128,2,1,128]{5,3,2,4,1,0:T(2,128)}), f32[64,1,128,2,1,128]{5,3,2,4,1,0:T(2,128)}, u32[]{:S(2)}, u32[]{:S(2)}) async-start(f32[64,1,128,2,1,128]{5,3,2,4,1,0:T(2,128)} %copy.298), calls=%async_computation.8 | async-start | bytes 16777216 | tf_op jit(solution)/shard_map/all_to_all | solution.py:197
  518.8 244.7 %all-reduce.8.cloned.1.call-start = ((), (), s32[]{:S(2)}) async-start(), calls=%async_computation.12 | async-start | bytes 524288 | tf_op jit(solution)/shard_map/psum | solution.py:175
  531.0 7.8 copy-start
  531.7 179.7 %collective-permute-start.2 = (bf16[128,2,1,128]{3,0,1,2:T(8,128)(2,1)}, bf16[128,2,1,128]{3,0,1,2:T(8,128)(2,1)}, u32[]{:S(2)}, u32[]{:S(2)}) collective-permute-start(bf16[128,2,1,128]{3,0,1,2:T(8,128)(2,1)} %get-tuple-element.189), channel_id=1, source_target_pairs={{4,0},{8,4},{12,8},{16,12},{20,16},{24,20},{28,24},{32,28},{36,32}... | collective-permute-start | bytes 196616 | tf_op jit(solution)/shard_map/ppermute | solution.py:33
  536.4 176.0 %collective-permute-start.3 = (bf16[128,2,1,128]{3,0,1,2:T(8,128)(2,1)}, bf16[128,2,1,128]{3,0,1,2:T(8,128)(2,1)}, u32[]{:S(2)}, u32[]{:S(2)}) collective-permute-start(bf16[128,2,1,128]{3,0,1,2:T(8,128)(2,1)} %get-tuple-element.188), channel_id=1, source_target_pairs={{0,4},{4,8},{8,12},{12,16},{16,20},{20,24},{24,28},{28,32},{32,36}... | collective-permute-start | bytes 196616 | tf_op jit(solution)/shard_map/ppermute | solution.py:33
  706.9 59.0 %all-to-all-start.7 = ((bf16[1152,8,128]{2,1,0:T(8,128)(2,1)}), bf16[1152,8,128]{2,1,0:T(8,128)(2,1)S(1)}, u32[]{:S(2)}, u32[]{:S(2)}) async-start(bf16[1152,8,128]{2,1,0:T(8,128)(2,1)} %bitcast.339), calls=%async_computation.7 | async-start | bytes 4718592 | tf_op jit(solution)/shard_map/all_to_all | solution.py:214
  766.0 12.6 %all-to-all-start.9 = ((bf16[4,2,18432]{2,1,0:T(2,128)(2,1)}), bf16[4,2,18432]{2,1,0:T(2,128)(2,1)S(1)}, u32[]{:S(2)}, u32[]{:S(2)}) async-start(bf16[4,2,18432]{2,1,0:T(2,128)(2,1)} %reshape.445), calls=%async_computation.9 | async-start | bytes 589824 | tf_op jit(solution)/shard_map/all_to_all | solution.py:215
  778.6 11.0 %all-to-all-start.10 = ((bf16[4,2,18432]{2,1,0:T(2,128)(2,1)}), bf16[4,2,18432]{2,1,0:T(2,128)(2,1)S(1)}, u32[]{:S(2)}, u32[]{:S(2)}) async-start(bf16[4,2,18432]{2,1,0:T(2,128)(2,1)} %reshape.447), calls=%async_computation.10 | async-start | bytes 589824 | tf_op jit(solution)/shard_map/all_to_all | solution.py:216
Sparse Core Ops, SparseCore 0:
  142.9 188.8 all-reduce.5
  536.5 226.9 all-reduce.7
where the time goes:
time: 811 us; the launch traced here: 798 us
  waiting for transfers between devices  472 us (58%)
  local copies, waits for them, and re-layouts  122 us (15%)
  matrix products  91.8 us (11%)
  starting transfers between devices  66.5 us (8%)
  other arithmetic  30.1 us (4%)
  between operations  15 us (2%)
    psum x1, waiting for transfers between devices, broadcast(): return lax.psum(kept, axis)  186 us
    all_to_all x1, waiting for transfers between devices, per_device(): lax.all_to_all(returning, 'seq', split_axis=0, concat_axis=0, tiled=True)  168 us
    psum x1, waiting for transfers between devices, per_device(): global_total = lax.psum(global_part, 'seq')  37.2 us
    unnamed x27, local copies, waits for them, and re-layouts  23.9 us
    all_to_all x1, waiting for transfers between devices, per_device(): lax.all_to_all(queries, 'head', split_axis=1, concat_axis=0, tiled=True)  21.7 us
    all_to_all x1, waiting for transfers between devices, per_device(): lax.all_to_all(outputs, 'head', split_axis=1, concat_axis=0, tiled=True)  20.8 us
    dot_general x9, matrix products, block_grads(): jnp.einsum('ighd,mjgd->mghij', grad_block, value_blocks, preferred_elemen...  19.9 us
    dynamic_update_slice x9, other arithmetic, local_grads(): lax.map(single_block, (query_split, grad_split, logsum_split, delta_split...  19 us
  transfers between devices with their start and end apart: 17, of which 11 were waited for; matrix products, arithmetic and copies ran while one was open for 10% of the time, Pallas kernels for 0%

commit v1 on v0

v1 whole, which is shorter than its diff:
```python
import functools

import jax
import jax.numpy as jnp
import numpy as np
from jax import lax
from jax.experimental import pallas as pl
from jax.experimental.pallas import tpu as pltpu
from jax.sharding import Mesh, PartitionSpec as P

HD = 128
BLK = 128
G = 2
RND = 3
NZ, NX, NC, NH = 8, 4, 2, 4
NXC = NX * NC
SEQ = ("z", "x", "c")
NSEQ = NZ * NXC
QB = 9
NB = NSEQ * QB
HL = 8
ROWS = BLK * HL
TOK = 288
SCALE = 1.0 / HD**0.5
LOG2E = 1.4426950408889634
MASKED = 1e30
ENT = NB * RND
AT_SEQ, AT_Z, AT_HEAD, AT_WANT = 2 * ENT, 2 * ENT + 1, 2 * ENT + 2, 2 * ENT + 3
NEAR, FAR = (0, 1, 2, 6, 7), (3, 4, 5)
CUT = 5
PART = TOK * HL
BF = jnp.bfloat16
F32 = jnp.float32
ANY = pl.ANY


def dot(a, b, ca, cb):
    return lax.dot_general(a, b, (((ca,), (cb,)), ((), ())), preferred_element_type=F32)


def row_vector(tile):
    return jnp.concatenate([tile[i : i + 1, :] for i in range(HL)], axis=1)


def pair_grads(keys, values, biases, q, do, lse2, delta, key_scr, p_scr, ds_scr):
    n = len(keys)
    for t in range(n):
        rows = pl.ds(t * BLK, BLK)
        key_scr[rows, :] = keys[t]
        s = dot(keys[t], q, 1, 1)
        p = jnp.exp2(s * (SCALE * LOG2E) - (lse2 + biases[t]))
        dp = dot(values[t], do, 1, 1)
        p_scr[rows, :] = p.astype(BF)
        ds_scr[rows, :] = (p * (dp - delta)).astype(BF)
    dv = dot(p_scr[...], do, 1, 0)
    dk = dot(ds_scr[...], q, 1, 0) * SCALE
    dqt = dot(key_scr[...], ds_scr[...], 0, 0)
    return dk, dv, dqt


def load_parts(meta, parts, whole, sems):
    copies = []
    for i, (four, target) in enumerate(zip(parts, whole)):
        for k in range(NH):
            row = pl.multiple_of(((meta[AT_HEAD] - k) & (NH - 1)) * PART, PART)
            copies.append(
                pltpu.make_async_copy(four[k], target.at[pl.ds(row, PART)], sems.at[i, k])
            )
    for c in copies:
        c.start()
    for c in copies:
        c.wait()


def near_kernel(
    meta, q0, q1, q2, q3, d0, d1, d2, d3, ld_ref, kv_ref, gl_ref,
    dqt_ref, dkv_ref, dg_ref, q_scr, do_scr, key_scr, p_scr, ds_scr, sems,
):
    b = pl.program_id(0)

    @pl.when(b == 0)
    def _():
        load_parts(meta, ((q0, q1, q2, q3), (d0, d1, d2, d3)), (q_scr, do_scr), sems)
        dkv_ref[...] = jnp.zeros_like(dkv_ref)
        dg_ref[...] = jnp.zeros_like(dg_ref)

    block = meta[AT_SEQ] * QB + b
    keys = [gl_ref[0, 0], gl_ref[1, 0]] + [kv_ref[b + w, 0] for w in range(3)]
    values = [gl_ref[0, 1], gl_ref[1, 1]] + [kv_ref[b + w, 1] for w in range(3)]
    biases = [0.0, 0.0]
    for w in range(3):
        c = block + (w - 1)
        biases.append(jnp.where((c >= G) & (c <= NB - 1), 0.0, MASKED))
    lse2, delta = row_vector(ld_ref[0, 0]), row_vector(ld_ref[1, 0])
    rows = pl.ds(pl.multiple_of(b * ROWS, ROWS), ROWS)
    dk, dv, dqt = pair_grads(
        keys, values, biases, q_scr[rows, :], do_scr[rows, :], lse2, delta, key_scr, p_scr, ds_scr
    )
    dqt_ref[0] = dqt
    for t in range(G):
        dg_ref[t, 0] += dk[t * BLK : (t + 1) * BLK]
        dg_ref[t, 1] += dv[t * BLK : (t + 1) * BLK]
    for w in range(3):
        t = G + w
        dkv_ref[b + w, 0] += dk[t * BLK : (t + 1) * BLK]
        dkv_ref[b + w, 1] += dv[t * BLK : (t + 1) * BLK]


def place_of(meta, owner):
    r = ((owner >> 3) - meta[AT_Z]) & (NZ - 1)
    source = owner & (NXC - 1)
    far = (r >= FAR[0]) & (r <= FAR[-1])
    pos = jnp.where(r >= FAR[0], r - FAR[0], r)
    return far, source * jnp.where(far, len(FAR), len(NEAR)) + pos


def random_kernel(
    meta, q0, q1, q2, q3, d0, d1, d2, d3, ld_ref, near_ref, far_ref, dqt_ref,
    dq0, dq1, dq2, dq3, dnear_ref, dfar_ref,
    q_scr, do_scr, dq_scr, kv_scr, out_scr, key_scr, p_scr, ds_scr, sems, in_sems, out_sems, dq_sems,
):
    b = pl.program_id(0)
    start = meta[AT_SEQ] * (QB * RND)

    @pl.when(b == 0)
    def _():
        for e in range(QB * RND):
            far, at = place_of(meta, meta[start + e])

            @pl.when(far)
            def _():
                pltpu.make_async_copy(far_ref.at[at], kv_scr.at[e], in_sems.at[e]).start()

            @pl.when(jnp.logical_not(far))
            def _():
                pltpu.make_async_copy(near_ref.at[at], kv_scr.at[e], in_sems.at[e]).start()

        load_parts(meta, ((q0, q1, q2, q3), (d0, d1, d2, d3)), (q_scr, do_scr), sems)

    first = b * RND
    block = meta[AT_SEQ] * QB + b
    biases = []
    for j in range(RND):
        o = meta[start + first + j]
        r = o * QB + meta[ENT + start + first + j]
        biases.append(jnp.where((r >= G) & (jnp.abs(r - block) >= 2), 0.0, MASKED))
        pltpu.make_async_copy(near_ref.at[0], kv_scr.at[first + j], in_sems.at[first + j]).wait()
    lse2, delta = row_vector(ld_ref[0, 0]), row_vector(ld_ref[1, 0])
    rows = pl.ds(pl.multiple_of(b * ROWS, ROWS), ROWS)
    dk, dv, dqt = pair_grads(
        [kv_scr[first + j, 0] for j in range(RND)],
        [kv_scr[first + j, 1] for j in range(RND)],
        biases, q_scr[rows, :], do_scr[rows, :], lse2, delta, key_scr, p_scr, ds_scr,
    )
    dq_scr[rows, :] = ((dqt + dqt_ref[0]).T * SCALE).astype(BF)

    for j in range(RND):
        n = first + j
        out_scr[n, 0] = dk[j * BLK : (j + 1) * BLK].astype(BF)
        out_scr[n, 1] = dv[j * BLK : (j + 1) * BLK].astype(BF)
        far, at = place_of(meta, meta[start + n])

        @pl.when(far)
        def _():
            pltpu.make_async_copy(out_scr.at[n], dfar_ref.at[at], out_sems.at[n]).start()

        @pl.when(jnp.logical_not(far))
        def _():
            pltpu.make_async_copy(out_scr.at[n], dnear_ref.at[at], out_sems.at[n]).start()

    @pl.when(b == QB - 1)
    def _():
        copies = []
        for k, target in enumerate((dq0, dq1, dq2, dq3)):
            row = pl.multiple_of(((meta[AT_HEAD] + k) & (NH - 1)) * PART, PART)
            copies.append(
                pltpu.make_async_copy(dq_scr.at[pl.ds(row, PART)], target, dq_sems.at[k])
            )
        for c in copies:
            c.start()
        for c in copies:
            c.wait()
        for e in range(QB * RND):
            pltpu.make_async_copy(out_scr.at[e], dnear_ref.at[0], out_sems.at[e]).wait()


def select_kernel(steps, meta, *refs):
    sources, dst = refs[:-1], refs[-1]

    def lay(wanted, src, slot, at):
        @pl.when(wanted)
        def _():
            dst[at] = src[slot]

    for d in range(NXC):
        for i, r in enumerate(steps):
            slot = meta[AT_WANT + d * NZ + r]
            at = d * len(steps) + i
            if r == 4:
                lay((slot >= 0) & (slot < CUT), sources[i], slot, at)
                lay(slot >= CUT, sources[-1], slot - CUT, at)
            else:
                lay(slot >= 0, sources[i], slot, at)


def collect_kernel(steps, meta, got, *outs):
    for out in outs:
        out[...] = jnp.zeros_like(out)
    for d in range(NXC):
        for i, r in enumerate(steps):
            slot = meta[AT_WANT + d * NZ + r]

            @pl.when(slot >= 0)
            def _():
                outs[i][slot] += got[d * len(steps) + i].astype(F32)


TILE = (2, BLK, HD)
PARAMS = pltpu.CompilerParams(vmem_limit_bytes=50 << 20)


def full(*shape):
    return pl.BlockSpec(shape, lambda b, m: (0,) * len(shape))


def anywhere(n):
    return [pl.BlockSpec(memory_space=ANY)] * n


def work_scratch(n):
    return [
        pltpu.VMEM((n * BLK, HD), BF),
        pltpu.VMEM((n * BLK, ROWS), BF),
        pltpu.VMEM((n * BLK, ROWS), BF),
    ]


ROW_PAIR = pl.BlockSpec((2, 1, HL, BLK), lambda b, m: (0, b, 0, 0))
DQT = pl.BlockSpec((1, HD, ROWS), lambda b, m: (b, 0, 0))


def call_near(meta, q, do, ld, kvx, gl):
    return pl.pallas_call(
        near_kernel,
        grid_spec=pltpu.PrefetchScalarGridSpec(
            num_scalar_prefetch=1,
            grid=(QB,),
            in_specs=anywhere(2 * NH) + [ROW_PAIR, full(QB + 2, *TILE), full(G, *TILE)],
            out_specs=[DQT, full(QB + 2, *TILE), full(G, *TILE)],
            scratch_shapes=[pltpu.VMEM((QB * ROWS, HD), BF)] * 2
            + work_scratch(G + 3)
            + [pltpu.SemaphoreType.DMA((2, NH))],
        ),
        out_shape=[
            jax.ShapeDtypeStruct((QB, HD, ROWS), F32),
            jax.ShapeDtypeStruct((QB + 2, *TILE), F32),
            jax.ShapeDtypeStruct((G, *TILE), F32),
        ],
        compiler_params=PARAMS,
        name="near",
    )(meta, *q, *do, ld, kvx, gl)


def call_random(meta, q, do, ld, near, far, dqt):
    count = QB * RND
    return pl.pallas_call(
        random_kernel,
        grid_spec=pltpu.PrefetchScalarGridSpec(
            num_scalar_prefetch=1,
            grid=(QB,),
            in_specs=anywhere(2 * NH) + [ROW_PAIR] + anywhere(2) + [DQT],
            out_specs=anywhere(NH + 2),
            scratch_shapes=[pltpu.VMEM((QB * ROWS, HD), BF)] * 3
            + [pltpu.VMEM((count, *TILE), BF)] * 2
            + work_scratch(RND)
            + [
                pltpu.SemaphoreType.DMA((2, NH)),
                pltpu.SemaphoreType.DMA((count,)),
                pltpu.SemaphoreType.DMA((count,)),
                pltpu.SemaphoreType.DMA((NH,)),
            ],
        ),
        out_shape=[jax.ShapeDtypeStruct((PART, HD), BF)] * NH
        + [
            jax.ShapeDtypeStruct((NXC * len(NEAR), *TILE), BF),
            jax.ShapeDtypeStruct((NXC * len(FAR), *TILE), BF),
        ],
        compiler_params=PARAMS,
        name="random",
    )(meta, *q, *do, ld, near, far, dqt)


def call_select(meta, steps, sources):
    n = NXC * len(steps)
    return pl.pallas_call(
        functools.partial(select_kernel, steps),
        grid_spec=pltpu.PrefetchScalarGridSpec(
            num_scalar_prefetch=1,
            grid=(1,),
            in_specs=[full(*x.shape) for x in sources],
            out_specs=full(n, *TILE),
        ),
        out_shape=jax.ShapeDtypeStruct((n, *TILE), BF),
        compiler_params=PARAMS,
        name="select",
    )(meta, *sources)


def call_collect(meta, steps, got):
    return pl.pallas_call(
        functools.partial(collect_kernel, steps),
        grid_spec=pltpu.PrefetchScalarGridSpec(
            num_scalar_prefetch=1,
            grid=(1,),
            in_specs=[full(*got.shape)],
            out_specs=[full(QB, *TILE)] * len(steps),
        ),
        out_shape=[jax.ShapeDtypeStruct((QB, *TILE), F32)] * len(steps),
        compiler_params=PARAMS,
        name="collect",
    )(meta, got)


def join_kernel(head, p0, p1, p2, p3, out):
    for k, p in enumerate((p0, p1, p2, p3)):
        out[:, (head[0] - k) & (NH - 1)] = p[...]


def call_join(head, parts):
    rows = TOK // 3
    return pl.pallas_call(
        join_kernel,
        grid_spec=pltpu.PrefetchScalarGridSpec(
            num_scalar_prefetch=1,
            grid=(3,),
            in_specs=[pl.BlockSpec((rows, HL, HD), lambda b, m: (b, 0, 0))] * NH,
            out_specs=pl.BlockSpec((rows, NH, HL, HD), lambda b, m: (b, 0, 0, 0)),
        ),
        out_shape=jax.ShapeDtypeStruct((TOK, NH, HL, HD), BF),
        name="join",
    )(head, *[p.reshape(TOK, HL, HD) for p in parts])


def plain_a2a(value, axis):
    return lax.all_to_all(value, axis, split_axis=0, concat_axis=0, tiled=True)


def turn(value, k):
    return lax.ppermute(value, "head", [(i, (i + k) % NH) for i in range(NH)]) if k else value


def to_heads(value, head):
    parts = value.reshape(TOK, NH, HL, HD)
    return [
        turn(
            lax.dynamic_index_in_dim(parts, lax.rem(head + k, NH), axis=1, keepdims=False), k
        ).reshape(PART, HD)
        for k in range(NH)
    ]


def along_z(value, step):
    return lax.ppermute(value, "z", [(i, (i + step) % NZ) for i in range(NZ)])


def add(a, b):
    return (a.astype(F32) + b).astype(BF)


def spread(value, index):
    k = 1
    while k < NSEQ:
        got = lax.ppermute(value, SEQ, [(i, i + k) for i in range(k)])
        value = jnp.where((index >= k) & (index < 2 * k), got, value)
        k *= 2
    return value


def gather_sum(value):
    k = NSEQ // 2
    while k:
        value = value + lax.ppermute(value, SEQ, [(i + k, i) for i in range(k)])
        k //= 2
    return value


def per_device(q, k, v, o, do, lse, owner, slot):
    head, seq = lax.axis_index("head"), lax.axis_index(SEQ)
    z, xc = lax.axis_index("z"), lax.axis_index(("x", "c"))
    plane = NXC * QB
    owners = lax.dynamic_slice_in_dim(owner, z * plane, plane, 0).reshape(NXC, 1, QB * RND)
    slots = lax.dynamic_slice_in_dim(slot, z * plane, plane, 0).reshape(NXC, 1, QB * RND)
    column = ((z + jnp.arange(NZ, dtype=jnp.int32)) % NZ * NXC + xc)[None, :, None]
    want = jnp.max(jnp.where(owners == column, slots, -1), axis=2)
    spot = jnp.stack([seq, z, head]).astype(jnp.int32)
    meta = jnp.concatenate([owner.reshape(-1), slot.reshape(-1), spot, want.reshape(-1)])

    kv = jnp.stack([k, v]).transpose(2, 0, 1, 3)
    kv = plain_a2a(kv, "head")
    kv = kv.transpose(1, 0, 2, 3).reshape(2, QB, BLK, HD).transpose(1, 0, 2, 3)
    u1, d1 = along_z(kv, 1), along_z(kv, -1)
    u2, d2 = along_z(u1, 1), along_z(d1, -1)
    u3, d3 = along_z(u2, 1), along_z(d2, -1)
    u4, d4 = along_z(u3[:CUT], 1), along_z(d3[CUT:], -1)
    near = plain_a2a(call_select(meta, NEAR, [kv, d1, d2, u2, u1]), ("x", "c"))
    far = plain_a2a(call_select(meta, FAR, [d3, u4, u3, d4]), ("x", "c"))

    up = [(i, i + 1) for i in range(NSEQ - 1)]
    down = [(i + 1, i) for i in range(NSEQ - 1)]
    before = lax.ppermute(kv[QB - 1 :], SEQ, up)
    after = lax.ppermute(kv[:1], SEQ, down)
    kvx = jnp.concatenate([before, kv, after])
    gl = spread(kv[:G], seq)

    delta = jnp.sum(do.astype(F32) * o.astype(F32), axis=-1)
    ld = jnp.stack([lse * LOG2E, delta]).reshape(2, TOK, NH, HL).transpose(2, 0, 1, 3)
    ld = plain_a2a(ld.reshape(NH, 2, PART // BLK, BLK), "head")
    ld = ld.transpose(1, 0, 2, 3).reshape(2, QB, HL, BLK)

    ql, dol = to_heads(q, head), to_heads(do, head)
    dqt, dkvx, dg = call_near(meta, ql, dol, ld, kvx, gl)
    dq0, dq1, dq2, dq3, dnear, dfar = call_random(meta, ql, dol, ld, near, far, dqt)

    c3, c4, c5 = call_collect(meta, FAR, plain_a2a(dfar, ("x", "c")))
    c0, c1, c2, c6, c7 = call_collect(meta, NEAR, plain_a2a(dnear, ("x", "c")))
    up4 = along_z(c4[:CUT].astype(BF), 1)
    down4 = along_z(c4[CUT:].astype(BF), -1)
    up3 = along_z(jnp.concatenate([add(up4, c3[:CUT]), c3[CUT:].astype(BF)]), 1)
    down3 = along_z(jnp.concatenate([c5[:CUT].astype(BF), add(down4, c5[CUT:])]), -1)
    up2, down2 = along_z(add(up3, c2), 1), along_z(add(down3, c6), -1)
    up1, down1 = along_z(add(up2, c1), 1), along_z(add(down2, c7), -1)

    lower = lax.ppermute(dkvx[:1].astype(BF), SEQ, down)
    upper = lax.ppermute(dkvx[QB + 1 :].astype(BF), SEQ, up)
    dg = jnp.where(seq == 0, gather_sum(dg), 0.0)
    total = dkvx[1 : QB + 1] + c0 + up1.astype(F32) + down1.astype(F32)
    total = total.at[QB - 1 :].add(lower.astype(F32))
    total = total.at[:1].add(upper.astype(F32))
    total = total.at[:G].add(dg).astype(BF)
    dkv = total.transpose(1, 0, 2, 3).reshape(2, NH, TOK, HD).transpose(1, 0, 2, 3)
    dkv = plain_a2a(dkv, "head")
    dk = dkv[:, 0].transpose(1, 0, 2)
    dv = dkv[:, 1].transpose(1, 0, 2)
    dq = call_join(head.reshape(1), [turn(p, i) for i, p in enumerate((dq0, dq1, dq2, dq3))])
    return dq.reshape(TOK, NH * HL, HD), dk, dv


def solution(mesh):
    grid = Mesh(np.asarray(mesh.devices).reshape(NZ, NX, NC, NH), ("z", "x", "c", "head"))
    split = ("z", "x", "c", "head")
    wide = P(split, None, None)
    return jax.shard_map(
        per_device,
        mesh=grid,
        in_specs=(wide,) * 5 + (P(split, None), P(), P()),
        out_specs=(wide,) * 3,
        check_vma=False,
    )
```

time: 811 us -> 380 us (0.47); the launches traced: 798 us -> 378 us
  waiting for transfers between devices: 472 us -> 148 us
  local copies, waits for them, and re-layouts: 122 us -> 23.8 us
  matrix products: 91.8 us -> 0 us
  Pallas kernels: 0 us -> 55.9 us
  blocking collectives: 0 us -> 40 us
  starting transfers between devices: 66.5 us -> 93.2 us
  other arithmetic: 30.1 us -> 14.7 us
  between operations: 15 us -> 1.47 us
    all_to_all x11 -> x5, waiting for transfers between devices: 248 us -> 12.5 us  [plain_a2a(): return lax.all_to_all(value, axis, split_axis=0, concat_axis=0, tiled=True)]
    psum x2 -> x0, waiting for transfers between devices: 224 us -> none  [the longest x1 186 us: broadcast(): return lax.psum(kept, axis)]
    ppermute x4 -> x41, waiting for transfers between devices: 0.01 us -> 136 us  [the longest x9 53.5 us: turn(): lax.ppermute(value, 'head', [(i, (i + k) % NH) for i in range(NH)])]
    dot_general x48 -> x0, matrix products: 91.8 us -> none  [the longest x9 19.9 us: block_grads(): jnp.einsum('ighd,mjgd->mghij', grad_block, value_blocks, preferred_elemen...]
    ppermute x4 -> x41, starting transfers between devices: 8.64 us -> 70.5 us  [the longest x16 29.4 us: along_z(): return lax.ppermute(value, 'z', [(i, (i + step) % NZ) for i in range(NZ)])]
    pallas_call x0 -> x7, Pallas kernels: none -> 55.9 us  [the longest x1 21.6 us: call_near(): pl.pallas_call(near_kernel, grid_spec=pltpu.PrefetchScalarGridSpec(num_sc...]
    all_to_all x0 -> x2, blocking collectives: none -> 40 us  [plain_a2a(): return lax.all_to_all(value, axis, split_axis=0, concat_axis=0, tiled=True)]
    all_to_all x11 -> x5, starting transfers between devices: 57.6 us -> 22.7 us  [plain_a2a(): return lax.all_to_all(value, axis, split_axis=0, concat_axis=0, tiled=True)]
  transfers between devices with their start and end apart: 17 -> 46, of which waited for: 11 -> 13; matrix products, arithmetic and copies ran while one was open for 10% -> 9% of each run, Pallas kernels for 0% -> 10%
where the time goes in v1:
time: 380 us; the launch traced here: 378 us
  waiting for transfers between devices  148 us (39%)
  starting transfers between devices  93.2 us (25%)
  Pallas kernels  55.9 us (15%)
  blocking collectives  40 us (11%)
  local copies, waits for them, and re-layouts  23.8 us (6%)
  other arithmetic  14.7 us (4%)
    ppermute x9, waiting for transfers between devices, turn(): lax.ppermute(value, 'head', [(i, (i + k) % NH) for i in range(NH)])  53.5 us
    all_to_all x2, blocking collectives, plain_a2a(): return lax.all_to_all(value, axis, split_axis=0, concat_axis=0, tiled=True)  40 us
    ppermute x16, starting transfers between devices, along_z(): return lax.ppermute(value, 'z', [(i, (i + step) % NZ) for i in range(NZ)])  29.4 us
    ppermute x6, waiting for transfers between devices, spread(): got = lax.ppermute(value, SEQ, [(i, i + k) for i in range(k)])  27.1 us
    ppermute x6, waiting for transfers between devices, gather_sum(): value = value + lax.ppermute(value, SEQ, [(i + k, i) for i in range(k)])  25.4 us
    ppermute x16, waiting for transfers between devices, along_z(): return lax.ppermute(value, 'z', [(i, (i + step) % NZ) for i in range(NZ)])  22.9 us
    all_to_all x5, starting transfers between devices, plain_a2a(): return lax.all_to_all(value, axis, split_axis=0, concat_axis=0, tiled=True)  22.7 us
    pallas_call x1, Pallas kernels, call_near(): pl.pallas_call(near_kernel, grid_spec=pltpu.PrefetchScalarGridSpec(num_sc...  21.6 us
  transfers between devices with their start and end apart: 46, of which 13 were waited for; matrix products, arithmetic and copies ran while one was open for 9% of the time, Pallas kernels for 10%

profile of v1, /device:TPU:2, one launch (start us, length us, event | category | flops | bytes accessed | tf_op | source)
XLA Modules:
  0.0 377.6 jit_solution(11825092211548315101)
XLA Ops:
  1.8 14.6 %all_to_all.35 = bf16[4,2,288,128]{3,2,1,0:T(8,128)(2,1)S(1)} all-to-all(bf16[4,2,288,128]{3,2,1,0:T(8,128)(2,1)S(1)} %maximum_bitcast_fusion), channel_id=1, replica_groups=mesh['z'=8,'x'=4,'c'=2,'head'=4] {'head'}, dimensions={0} | all-to-all | bytes 1179648 | tf_op jit(solution)/shard_map/all_to_all | solution.py:345
  16.5 2.0 collective-permute-start.8
  18.5 4.0 %collective-permute-start.6 = (bf16[9,2,128,128]{3,2,1,0:T(8,128)(2,1)S(1)}, bf16[9,2,128,128]{3,2,1,0:T(8,128)(2,1)S(1)}, u32[]{:S(2)}, u32[]{:S(2)}) collective-permute-start(bf16[9,2,128,128]{3,2,1,0:T(8,128)(2,1)S(1)} %bitcast.72), channel_id=1, source_target_pairs={{0,224},{32,0},{64,32},{96,64},{128,96},{160,128},{192,160},{224,1... | collective-permute-start | bytes 1769480 | tf_op jit(solution)/shard_map/ppermute | solution.py:363
  24.0 10.3 %collective-permute-done.8.refs_4_ = bf16[9,2,128,128]{3,2,1,0:T(8,128)(2,1)S(1)} collective-permute-done((bf16[9,2,128,128]{3,2,1,0:T(8,128)(2,1)S(1)}, bf16[9,2,128,128]{3,2,1,0:T(8,128)(2,1)S(1)}, u32[]{:S(2)}, u32[]{:S(2)}) %collective-permute-start.8) | collective-permute-done | bytes 589856 | tf_op jit(solution)/shard_map/ppermute | solution.py:363
  34.3 3.2 collective-permute-start.7
  41.4 3.9 %all-to-all-start = ((f32[4,2,18,128]{3,1,2,0:T(2,128)}), f32[4,2,18,128]{3,1,2,0:T(2,128)}, u32[]{:S(2)}, u32[]{:S(2)}) async-start(f32[4,2,18,128]{3,1,2,0:T(2,128)} %copy.73), calls=%async_computation | async-start | bytes 147456 | tf_op jit(solution)/shard_map/all_to_all | solution.py:345
  50.3 2.6 select.24
  52.9 4.8 %all-to-all-start.2 = ((bf16[40,2,128,128]{3,2,1,0:T(8,128)(2,1)}), bf16[40,2,128,128]{3,2,1,0:T(8,128)(2,1)}, u32[]{:S(2)}, u32[]{:S(2)}) async-start(bf16[40,2,128,128]{3,2,1,0:T(8,128)(2,1)} %select.24), calls=%async_computation.2 | async-start | bytes 5242880 | tf_op jit(solution)/shard_map/all_to_all | solution.py:345
  58.5 3.2 collective-permute-start.10
  63.1 27.1 %collective-permute-done.17 = bf16[2,2,128,128]{3,2,1,0:T(8,128)(2,1)S(1)} collective-permute-done((bf16[2,2,128,128]{3,2,1,0:T(8,128)(2,1)S(1)}, bf16[2,2,128,128]{3,2,1,0:T(8,128)(2,1)S(1)}, u32[]{:S(2)}, u32[]{:S(2)}) %collective-permute-start.17) | collective-permute-done | bytes 131104 | tf_op jit(solution)/shard_map/ppermute | solution.py:373
  93.1 3.2 collective-permute-start.13
  97.0 1.9 collective-permute-start.19
  98.9 2.9 dynamic-slice_bitcast_fusion.4
  101.8 3.2 collective-permute-start.2
  105.8 3.1 select.25
  109.0 4.8 %all-to-all-start.3 = ((bf16[24,2,128,128]{3,2,1,0:T(8,128)(2,1)}), bf16[24,2,128,128]{3,2,1,0:T(8,128)(2,1)}, u32[]{:S(2)}, u32[]{:S(2)}) async-start(bf16[24,2,128,128]{3,2,1,0:T(8,128)(2,1)} %select.25), calls=%async_computation.3 | async-start | bytes 3145728 | tf_op jit(solution)/shard_map/all_to_all | solution.py:345
  116.0 2.1 collective-permute-start.14
  118.1 3.5 collective-permute-start.15
  122.9 2.9 dynamic-slice_bitcast_fusion
  125.9 7.0 %collective-permute-done.14 = bf16[1,2,128,128]{3,2,1,0:T(8,128)(2,1)S(1)} collective-permute-done((bf16[1,2,128,128]{3,2,1,0:T(8,128)(2,1)S(1)}, bf16[1,2,128,128]{3,2,1,0:T(8,128)(2,1)S(1)}, u32[]{:S(2)}, u32[]{:S(2)}) %collective-permute-start.14) | collective-permute-done | bytes 65568 | tf_op jit(solution)/shard_map/ppermute | solution.py:410
  134.4 2.4 collective-permute-start.5
  139.9 1.9 pad_maximum_fusion.kv_ref
  141.8 22.0 %collective-permute-done = bf16[288,8,128]{2,1,0:T(8,128)(2,1)S(1)} collective-permute-done((bf16[288,8,128]{2,1,0:T(8,128)(2,1)}, bf16[288,8,128]{2,1,0:T(8,128)(2,1)S(1)}, u32[]{:S(2)}, u32[]{:S(2)}) %collective-permute-start) | collective-permute-done | bytes 589856 | tf_op jit(solution)/shard_map/ppermute | solution.py:349
  163.9 10.8 %collective-permute-done.3 = bf16[288,8,128]{2,1,0:T(8,128)(2,1)} collective-permute-done((bf16[288,8,128]{2,1,0:T(8,128)(2,1)}, bf16[288,8,128]{2,1,0:T(8,128)(2,1)}, u32[]{:S(2)}, u32[]{:S(2)}) %collective-permute-start.3) | collective-permute-done | bytes 589856 | tf_op jit(solution)/shard_map/ppermute | solution.py:349
  174.7 21.6 %near.1 = (f32[9,128,1024]{2,1,0:T(8,128)}, f32[11,2,128,128]{3,2,1,0:T(8,128)}, f32[2,2,128,128]{3,2,1,0:T(8,128)}) custom-call(s32[3523]{0:T(1024)S(1)} %concatenate.19.meta, bf16[2304,128]{1,0:T(8,128)(2,1)S(1)} %get-tuple-element.92.q0, bf16[2304,128]{1,0:T(8,128)(2,1)S(1)} %bitcast.82, bf16[2304,128]{1,0:T(8,128)(2,1)S(1)} %bitcast.80, ...), custom_call_target="tpu_custom_call" | custom-call | tf_op jit(solution)/shard_map/near/pallas_call | solution.py:243
  197.2 17.1 %random.1 = (bf16[2304,128]{1,0:T(8,128)(2,1)S(1)}, bf16[2304,128]{1,0:T(8,128)(2,1)S(1)}, bf16[2304,128]{1,0:T(8,128)(2,1)S(1)}, bf16[2304,128]{1,0:T(8,128)(2,...) custom-call(s32[3523]{0:T(1024)S(1)} %concatenate.19.meta, ...), custom_call_target="tpu_custom_call" | custom-call | tf_op jit(solution)/shard_map/random/pallas_call | solution.py:266
  214.3 25.5 %all_to_all.36.got = bf16[24,2,128,128]{3,2,1,0:T(8,128)(2,1)} all-to-all(bf16[24,2,128,128]{3,2,1,0:T(8,128)(2,1)} %get-tuple-element.64), channel_id=1, replica_groups=mesh['z'=8,'x'=4,'c'=2,'head'=4] {'x','c'}, dimensions={0} | all-to-all | bytes 3145728 | tf_op jit(solution)/shard_map/all_to_all | solution.py:345
  239.8 5.8 %all-to-all-start.4 = ((bf16[40,2,128,128]{3,2,1,0:T(8,128)(2,1)}), bf16[40,2,128,128]{3,2,1,0:T(8,128)(2,1)}, u32[]{:S(2)}, u32[]{:S(2)}) async-start(bf16[40,2,128,128]{3,2,1,0:T(8,128)(2,1)} %get-tuple-element.62), calls=%async_computation.4 | async-start | bytes 5242880 | tf_op jit(solution)/shard_map/all_to_all | solution.py:345
  245.5 2.7 collect.3
  248.5 3.3 collective-permute-start.29
  251.8 7.6 %collective-permute-done.25 = bf16[5,2,128,128]{3,2,1,0:T(8,128)(2,1)S(1)} collective-permute-done((bf16[5,2,128,128]{3,2,1,0:T(8,128)(2,1)S(1)}, bf16[5,2,128,128]{3,2,1,0:T(8,128)(2,1)S(1)}, u32[]{:S(2)}, u32[]{:S(2)}) %collective-permute-start.25) | collective-permute-done | bytes 327712 | tf_op jit(solution)/shard_map/ppermute | solution.py:363
  259.8 3.5 collective-permute-start.30
  264.6 12.4 %all-to-all-done.4.got = bf16[40,2,128,128]{3,2,1,0:T(8,128)(2,1)} async-done(((bf16[40,2,128,128]{3,2,1,0:T(8,128)(2,1)}), bf16[40,2,128,128]{3,2,1,0:T(8,128)(2,1)}, u32[]{:S(2)}, u32[]{:S(2)}) %all-to-all-start.4) | async-done | bytes 2621472 | tf_op jit(solution)/shard_map/all_to_all | solution.py:345
  277.0 4.7 %collect.2 = (f32[9,2,128,128]{3,2,1,0:T(8,128)S(1)}, f32[9,2,128,128]{3,2,1,0:T(8,128)S(1)}, f32[9,2,128,128]{3,2,1,0:T(8,128)S(1)}, f32[9,2,128,128]{3,2,1,0:T(8,128)}, f32[9,2,128,128]{3,2,1,0:T(8,128)}) custom-call(s32[3523]{0:T(1024)S(1)} %concatenate.19.meta, bf16[40,2,128,128]{3,2,1,0:T(8,128)(2,1)} %all-to-all-done.4.got), custom_call_target="tpu_custom_call" | custom-call | tf_op jit(solution)/shard_map/collect/pallas_call | solution.py:310
  281.7 5.0 %collective-permute-done.26 = bf16[9,2,128,128]{3,2,1,0:T(8,128)(2,1)} collective-permute-done((bf16[9,2,128,128]{3,2,1,0:T(8,128)(2,1)S(1)}, bf16[9,2,128,128]{3,2,1,0:T(8,128)(2,1)}, u32[]{:S(2)}, u32[]{:S(2)}) %collective-permute-start.26) | collective-permute-done | bytes 589856 | tf_op jit(solution)/shard_map/ppermute | solution.py:363
  289.4 3.3 collective-permute-start.31
  295.0 12.3 %collective-permute-done.36 = f32[2,2,128,128]{3,2,1,0:T(8,128)S(1)} collective-permute-done((f32[2,2,128,128]{3,2,1,0:T(8,128)S(1)}, f32[2,2,128,128]{3,2,1,0:T(8,128)S(1)}, u32[]{:S(2)}, u32[]{:S(2)}) %collective-permute-start.36) | collective-permute-done | bytes 262176 | tf_op jit(solution)/shard_map/ppermute | solution.py:382
  309.7 2.7 collective-permute-start.28
  313.9 4.6 %collective-permute-done.37 = f32[2,2,128,128]{3,2,1,0:T(8,128)S(1)} collective-permute-done((f32[2,2,128,128]{3,2,1,0:T(8,128)S(1)}, f32[2,2,128,128]{3,2,1,0:T(8,128)S(1)}, u32[]{:S(2)}, u32[]{:S(2)}) %collective-permute-start.37) | collective-permute-done | bytes 262176 | tf_op jit(solution)/shard_map/ppermute | solution.py:382
  319.8 8.5 %collective-permute-done.38 = f32[2,2,128,128]{3,2,1,0:T(8,128)S(1)} collective-permute-done((f32[2,2,128,128]{3,2,1,0:T(8,128)S(1)}, f32[2,2,128,128]{3,2,1,0:T(8,128)S(1)}, u32[]{:S(2)}, u32[]{:S(2)}) %collective-permute-start.38) | collective-permute-done | bytes 262176 | tf_op jit(solution)/shard_map/ppermute | solution.py:382
  328.3 3.4 collective-permute-start.39
  333.4 1.9 collective-permute-start.34
  335.4 3.6 collective-permute-start.33
  339.9 2.2 collective-permute-start.23
  343.6 1.9 collective-permute-start.24
  346.9 3.5 all-to-all-start.6
  350.3 20.5 %collective-permute-done.22 = bf16[2304,128]{1,0:T(8,128)(2,1)S(1)} collective-permute-done((bf16[2304,128]{1,0:T(8,128)(2,1)S(1)}, bf16[2304,128]{1,0:T(8,128)(2,1)S(1)}, u32[]{:S(2)}, u32[]{:S(2)}) %collective-permute-start.22) | collective-permute-done | bytes 589856 | tf_op jit(solution)/shard_map/ppermute | solution.py:349
  371.7 4.1 %join.1 = bf16[288,4,8,128]{3,2,1,0:T(8,128)(2,1)} custom-call(s32[1]{0:T(128)} %bitcast.head, bf16[288,8,128]{2,1,0:T(8,128)(2,1)} %bitcast.84, bf16[288,8,128]{2,1,0:T(8,128)(2,1)} %bitcast.90, bf16[288,8,128]{2,1,0:T(8,128)(2,1)} %bitcast.32.p2, bf16[288,8,128]{2,1,0:T(8,128)(2,1)} %bitcast.33.p3), custom_call_target="tpu_custom_call" | custom-call | tf_op jit(solution)/shard_map/join/pallas_call | solution.py:331
  (165 shorter events, 46.9 us)
Async XLA Ops:
  16.5 17.8 %collective-permute-start.8 = (bf16[9,2,128,128]{3,2,1,0:T(8,128)(2,1)S(1)}, bf16[9,2,128,128]{3,2,1,0:T(8,128)(2,1)S(1)}, u32[]{:S(2)}, u32[]{:S(2)}) collective-permute-start(bf16[9,2,128,128]{3,2,1,0:T(8,128)(2,1)S(1)} %bitcast.71), channel_id=1, source_target_pairs={{0,32},{32,64},{64,96},{96,128},{128,160},{160,192},{192,224},{224... | collective-permute-start | bytes 1769480 | tf_op jit(solution)/shard_map/ppermute | solution.py:363
  18.5 15.8 %collective-permute-start.6 = (bf16[9,2,128,128]{3,2,1,0:T(8,128)(2,1)S(1)}, bf16[9,2,128,128]{3,2,1,0:T(8,128)(2,1)S(1)}, u32[]{:S(2)}, u32[]{:S(2)}) collective-permute-start(bf16[9,2,128,128]{3,2,1,0:T(8,128)(2,1)S(1)} %bitcast.72), channel_id=1, source_target_pairs={{0,224},{32,0},{64,32},{96,64},{128,96},{160,128},{192,160},{224,1... | collective-permute-start | bytes 1769480 | tf_op jit(solution)/shard_map/ppermute | solution.py:363
  34.3 16.0 %collective-permute-start.9 = (bf16[9,2,128,128]{3,2,1,0:T(8,128)(2,1)S(1)}, bf16[9,2,128,128]{3,2,1,0:T(8,128)(2,1)S(1)}, u32[]{:S(2)}, u32[]{:S(2)}) collective-permute-start(bf16[9,2,128,128]{3,2,1,0:T(8,128)(2,1)S(1)} %collective-permute-done.8.refs_4_), channel_id=1, source_target_pairs={{0,32},{32,64},{64,96},{96,128},{128,160},{160,192},{192,224},{224... | collective-permute-start | bytes 1769480 | tf_op jit(solution)/shard_map/ppermute | solution.py:363
  34.3 16.0 %collective-permute-start.7 = (bf16[9,2,128,128]{3,2,1,0:T(8,128)(2,1)S(1)}, bf16[9,2,128,128]{3,2,1,0:T(8,128)(2,1)S(1)}, u32[]{:S(2)}, u32[]{:S(2)}) collective-permute-start(bf16[9,2,128,128]{3,2,1,0:T(8,128)(2,1)S(1)} %collective-permute-done.6.refs_1_), channel_id=1, source_target_pairs={{0,224},{32,0},{64,32},{96,64},{128,96},{160,128},{192,160},{224,1... | collective-permute-start | bytes 1769480 | tf_op jit(solution)/shard_map/ppermute | solution.py:363
  41.4 11.5 %all-to-all-start = ((f32[4,2,18,128]{3,1,2,0:T(2,128)}), f32[4,2,18,128]{3,1,2,0:T(2,128)}, u32[]{:S(2)}, u32[]{:S(2)}) async-start(f32[4,2,18,128]{3,1,2,0:T(2,128)} %copy.73), calls=%async_computation | async-start | bytes 147456 | tf_op jit(solution)/shard_map/all_to_all | solution.py:345
  52.9 56.1 %all-to-all-start.2 = ((bf16[40,2,128,128]{3,2,1,0:T(8,128)(2,1)}), bf16[40,2,128,128]{3,2,1,0:T(8,128)(2,1)}, u32[]{:S(2)}, u32[]{:S(2)}) async-start(bf16[40,2,128,128]{3,2,1,0:T(8,128)(2,1)} %select.24), calls=%async_computation.2 | async-start | bytes 5242880 | tf_op jit(solution)/shard_map/all_to_all | solution.py:345
  57.8 4.0 %collective-permute-start.16 = (bf16[2,2,128,128]{3,2,1,0:T(8,128)(2,1)S(1)}, bf16[2,2,128,128]{3,2,1,0:T(8,128)(2,1)S(1)}, u32[]{:S(2)}, u32[]{:S(2)}) collective-permute-start(bf16[2,2,128,128]{3,2,1,0:T(8,128)(2,1)S(1)} %slice.164), channel_id=1, source_target_pairs={{0,4},{1,5},{2,6},{3,7}} | collective-permute-start | bytes 393224 | tf_op jit(solution)/shard_map/ppermute | solution.py:373
  58.5 33.1 %collective-permute-start.11 = (bf16[9,2,128,128]{3,2,1,0:T(8,128)(2,1)S(1)}, bf16[9,2,128,128]{3,2,1,0:T(8,128)(2,1)S(1)}, u32[]{:S(2)}, u32[]{:S(2)}) collective-permute-start(bf16[9,2,128,128]{3,2,1,0:T(8,128)(2,1)S(1)} %collective-permute-done.9.refs_3_), channel_id=1, source_target_pairs={{0,32},{32,64},{64,96},{96,128},{128,160},{160,192},{192,224},{224... | collective-permute-start | bytes 1769480 | tf_op jit(solution)/shard_map/ppermute | solution.py:363
  58.5 33.8 %collective-permute-start.10 = (bf16[9,2,128,128]{3,2,1,0:T(8,128)(2,1)S(1)}, bf16[9,2,128,128]{3,2,1,0:T(8,128)(2,1)S(1)}, u32[]{:S(2)}, u32[]{:S(2)}) collective-permute-start(bf16[9,2,128,128]{3,2,1,0:T(8,128)(2,1)S(1)} %collective-permute-done.7.refs_2_), channel_id=1, source_target_pairs={{0,224},{32,0},{64,32},{96,64},{128,96},{160,128},{192,160},{224,1... | collective-permute-start | bytes 1769480 | tf_op jit(solution)/shard_map/ppermute | solution.py:363
  61.8 28.4 %collective-permute-start.17 = (bf16[2,2,128,128]{3,2,1,0:T(8,128)(2,1)S(1)}, bf16[2,2,128,128]{3,2,1,0:T(8,128)(2,1)S(1)}, u32[]{:S(2)}, u32[]{:S(2)}) collective-permute-start(bf16[2,2,128,128]{3,2,1,0:T(8,128)(2,1)S(1)} %broadcast_select_fusion), channel_id=1, source_target_pairs={{0,8},{4,12},{1,9},{5,13},{2,10},{6,14},{3,11},{7,15}} | collective-permute-start | bytes 393224 | tf_op jit(solution)/shard_map/ppermute | solution.py:373
  90.2 6.1 %collective-permute-start.18 = (bf16[2,2,128,128]{3,2,1,0:T(8,128)(2,1)S(1)}, bf16[2,2,128,128]{3,2,1,0:T(8,128)(2,1)S(1)}, u32[]{:S(2)}, u32[]{:S(2)}) collective-permute-start(bf16[2,2,128,128]{3,2,1,0:T(8,128)(2,1)S(1)} %broadcast_select_fusion.1), channel_id=1, source_target_pairs={{0,16},{4,20},{8,24},{12,28},{1,17},{5,21},{9,25},{13,29},{2,18},{... | collective-permute-start | bytes 393224 | tf_op jit(solution)/shard_map/ppermute | solution.py:373
  92.3 13.5 %collective-permute-start.12 = (bf16[5,2,128,128]{3,2,1,0:T(8,128)(2,1)}, bf16[5,2,128,128]{3,2,1,0:T(8,128)(2,1)}, u32[]{:S(2)}, u32[]{:S(2)}) collective-permute-start(bf16[5,2,128,128]{3,2,1,0:T(8,128)(2,1)} %slice.160), channel_id=1, source_target_pairs={{0,32},{32,64},{64,96},{96,128},{128,160},{160,192},{192,224},{224... | collective-permute-start | bytes 983048 | tf_op jit(solution)/shard_map/ppermute | solution.py:363
  93.1 12.8 %collective-permute-start.13 = (bf16[4,2,128,128]{3,2,1,0:T(8,128)(2,1)}, bf16[4,2,128,128]{3,2,1,0:T(8,128)(2,1)}, u32[]{:S(2)}, u32[]{:S(2)}) collective-permute-start(bf16[4,2,128,128]{3,2,1,0:T(8,128)(2,1)} %slice.161), channel_id=1, source_target_pairs={{0,224},{32,0},{64,32},{96,64},{128,96},{160,128},{192,160},{224,1... | collective-permute-start | bytes 786440 | tf_op jit(solution)/shard_map/ppermute | solution.py:363
  97.0 16.8 %collective-permute-start.19 = (bf16[2,2,128,128]{3,2,1,0:T(8,128)(2,1)}, bf16[2,2,128,128]{3,2,1,0:T(8,128)(2,1)}, u32[]{:S(2)}, u32[]{:S(2)}) collective-permute-start(bf16[2,2,128,128]{3,2,1,0:T(8,128)(2,1)} %broadcast_select_fusion.2), channel_id=1, source_target_pairs={{0,32},{4,36},{8,40},{12,44},{16,48},{20,52},{24,56},{28,60},{1,33... | collective-permute-start | bytes 393224 | tf_op jit(solution)/shard_map/ppermute | solution.py:373
  101.8 35.0 %collective-permute-start.2 = (bf16[288,8,128]{2,1,0:T(8,128)(2,1)}, bf16[288,8,128]{2,1,0:T(8,128)(2,1)S(1)}, u32[]{:S(2)}, u32[]{:S(2)}) collective-permute-start(bf16[288,8,128]{2,1,0:T(8,128)(2,1)} %get-tuple-element.89), channel_id=1, source_target_pairs={{0,3},{1,0},{2,1},{3,2},{4,7},{5,4},{6,5},{7,6},{8,11},{9,8},{10,9... | collective-permute-start | bytes 1769480 | tf_op jit(solution)/shard_map/ppermute | solution.py:349
  105.0 36.8 %collective-permute-start.1 = (bf16[288,8,128]{2,1,0:T(8,128)(2,1)}, bf16[288,8,128]{2,1,0:T(8,128)(2,1)S(1)}, u32[]{:S(2)}, u32[]{:S(2)}) collective-permute-start(bf16[288,8,128]{2,1,0:T(8,128)(2,1)} %get-tuple-element.90), channel_id=1, source_target_pairs={{0,2},{1,3},{2,0},{3,1},{4,6},{5,7},{6,4},{7,5},{8,10},{9,11},{10,... | collective-permute-start | bytes 1769480 | tf_op jit(solution)/shard_map/ppermute | solution.py:349
  109.0 87.3 %all-to-all-start.3 = ((bf16[24,2,128,128]{3,2,1,0:T(8,128)(2,1)}), bf16[24,2,128,128]{3,2,1,0:T(8,128)(2,1)}, u32[]{:S(2)}, u32[]{:S(2)}) async-start(bf16[24,2,128,128]{3,2,1,0:T(8,128)(2,1)} %select.25), calls=%async_computation.3 | async-start | bytes 3145728 | tf_op jit(solution)/shard_map/all_to_all | solution.py:345
  114.7 6.9 %collective-permute-start.20 = (bf16[2,2,128,128]{3,2,1,0:T(8,128)(2,1)S(1)}, bf16[2,2,128,128]{3,2,1,0:T(8,128)(2,1)S(1)}, u32[]{:S(2)}, u32[]{:S(2)}) collective-permute-start(bf16[2,2,128,128]{3,2,1,0:T(8,128)(2,1)S(1)} %broadcast_select_fusion.3), channel_id=1, source_target_pairs={{0,64},{4,68},{8,72},{12,76},{16,80},{20,84},{24,88},{28,92},{32,9... | collective-permute-start | bytes 393224 | tf_op jit(solution)/shard_map/ppermute | solution.py:373
  116.0 16.9 %collective-permute-start.14 = (bf16[1,2,128,128]{3,2,1,0:T(8,128)(2,1)S(1)}, bf16[1,2,128,128]{3,2,1,0:T(8,128)(2,1)S(1)}, u32[]{:S(2)}, u32[]{:S(2)}) collective-permute-start(bf16[1,2,128,128]{3,2,1,0:T(8,128)(2,1)S(1)} %get-tuple-element.97), channel_id=1, source_target_pairs={{0,4},{4,8},{8,12},{12,16},{16,20},{20,24},{24,28},{28,32},{32,36}... | collective-permute-start | bytes 196616 | tf_op jit(solution)/shard_map/ppermute | solution.py:410
  118.1 16.3 %collective-permute-start.15 = (bf16[1,2,128,128]{3,2,1,0:T(8,128)(2,1)S(1)}, bf16[1,2,128,128]{3,2,1,0:T(8,128)(2,1)S(1)}, u32[]{:S(2)}, u32[]{:S(2)}) collective-permute-start(bf16[1,2,128,128]{3,2,1,0:T(8,128)(2,1)S(1)} %get-tuple-element.98), channel_id=1, source_target_pairs={{4,0},{8,4},{12,8},{16,12},{20,16},{24,20},{28,24},{32,28},{36,32}... | collective-permute-start | bytes 196616 | tf_op jit(solution)/shard_map/ppermute | solution.py:411
  121.6 16.6 %collective-permute-start.21 = (bf16[2,2,128,128]{3,2,1,0:T(8,128)(2,1)S(1)}, bf16[2,2,128,128]{3,2,1,0:T(8,128)(2,1)S(1)}, u32[]{:S(2)}, u32[]{:S(2)}) collective-permute-start(bf16[2,2,128,128]{3,2,1,0:T(8,128)(2,1)S(1)} %broadcast_select_fusion.4), channel_id=1, source_target_pairs={{0,128},{4,132},{8,136},{12,140},{16,144},{20,148},{24,152},{28,15... | collective-permute-start | bytes 393224 | tf_op jit(solution)/shard_map/ppermute | solution.py:373
  125.9 70.4 %copy-start = (bf16[2304,128]{1,0:T(8,128)(2,1)}, bf16[2304,128]{1,0:T(8,128)(2,1)S(1)}, u32[]{:S(2)}) copy-start(bf16[2304,128]{1,0:T(8,128)(2,1)S(1)} %get-tuple-element.88.d0) | copy-start | bytes 1769476
  133.5 30.3 %collective-permute-start = (bf16[288,8,128]{2,1,0:T(8,128)(2,1)}, bf16[288,8,128]{2,1,0:T(8,128)(2,1)S(1)}, u32[]{:S(2)}, u32[]{:S(2)}) collective-permute-start(bf16[288,8,128]{2,1,0:T(8,128)(2,1)} %get-tuple-element.91), channel_id=1, source_target_pairs={{0,1},{1,2},{2,3},{3,0},{4,5},{5,6},{6,7},{7,4},{8,9},{9,10},{10,1... | collective-permute-start | bytes 1769480 | tf_op jit(solution)/shard_map/ppermute | solution.py:349
  134.4 29.5 %collective-permute-start.5 = (bf16[288,8,128]{2,1,0:T(8,128)(2,1)}, bf16[288,8,128]{2,1,0:T(8,128)(2,1)}, u32[]{:S(2)}, u32[]{:S(2)}) collective-permute-start(bf16[288,8,128]{2,1,0:T(8,128)(2,1)} %get-tuple-element.85), channel_id=1, source_target_pairs={{0,3},{1,0},{2,1},{3,2},{4,7},{5,4},{6,5},{7,6},{8,11},{9,8},{10,9... | collective-permute-start | bytes 1769480 | tf_op jit(solution)/shard_map/ppermute | solution.py:349
  136.8 59.5 %copy-start.1 = (bf16[288,8,128]{2,1,0:T(8,128)(2,1)}, bf16[288,8,128]{2,1,0:T(8,128)(2,1)S(1)}, u32[]{:S(2)}) copy-start(bf16[288,8,128]{2,1,0:T(8,128)(2,1)S(1)} %collective-permute-done.2) | copy-start | bytes 1769476
  136.8 27.1 %collective-permute-start.4 = (bf16[288,8,128]{2,1,0:T(8,128)(2,1)}, bf16[288,8,128]{2,1,0:T(8,128)(2,1)}, u32[]{:S(2)}, u32[]{:S(2)}) collective-permute-start(bf16[288,8,128]{2,1,0:T(8,128)(2,1)} %get-tuple-element.86), channel_id=1, source_target_pairs={{0,2},{1,3},{2,0},{3,1},{4,6},{5,7},{6,4},{7,5},{8,10},{9,11},{10,... | collective-permute-start | bytes 1769480 | tf_op jit(solution)/shard_map/ppermute | solution.py:349
  138.9 35.7 %collective-permute-start.3 = (bf16[288,8,128]{2,1,0:T(8,128)(2,1)}, bf16[288,8,128]{2,1,0:T(8,128)(2,1)}, u32[]{:S(2)}, u32[]{:S(2)}) collective-permute-start(bf16[288,8,128]{2,1,0:T(8,128)(2,1)} %get-tuple-element.87), channel_id=1, source_target_pairs={{0,1},{1,2},{2,3},{3,0},{4,5},{5,6},{6,7},{7,4},{8,9},{9,10},{10,1... | collective-permute-start | bytes 1769480 | tf_op jit(solution)/shard_map/ppermute | solution.py:349
  239.8 37.3 %all-to-all-start.4 = ((bf16[40,2,128,128]{3,2,1,0:T(8,128)(2,1)}), bf16[40,2,128,128]{3,2,1,0:T(8,128)(2,1)}, u32[]{:S(2)}, u32[]{:S(2)}) async-start(bf16[40,2,128,128]{3,2,1,0:T(8,128)(2,1)} %get-tuple-element.62), calls=%async_computation.4 | async-start | bytes 5242880 | tf_op jit(solution)/shard_map/all_to_all | solution.py:345
  248.3 11.1 %collective-permute-start.25 = (bf16[5,2,128,128]{3,2,1,0:T(8,128)(2,1)S(1)}, bf16[5,2,128,128]{3,2,1,0:T(8,128)(2,1)S(1)}, u32[]{:S(2)}, u32[]{:S(2)}) collective-permute-start(bf16[5,2,128,128]{3,2,1,0:T(8,128)(2,1)S(1)} %slice.165), channel_id=1, source_target_pairs={{0,32},{32,64},{64,96},{96,128},{128,160},{160,192},{192,224},{224... | collective-permute-start | bytes 983048 | tf_op jit(solution)/shard_map/ppermute | solution.py:363
  248.5 11.1 %collective-permute-start.29 = (bf16[4,2,128,128]{3,2,1,0:T(8,128)(2,1)S(1)}, bf16[4,2,128,128]{3,2,1,0:T(8,128)(2,1)S(1)}, u32[]{:S(2)}, u32[]{:S(2)}) collective-permute-start(bf16[4,2,128,128]{3,2,1,0:T(8,128)(2,1)S(1)} %slice.168), channel_id=1, source_target_pairs={{0,224},{32,0},{64,32},{96,64},{128,96},{160,128},{192,160},{224,1... | collective-permute-start | bytes 786440 | tf_op jit(solution)/shard_map/ppermute | solution.py:363
  259.5 27.2 %collective-permute-start.26 = (bf16[9,2,128,128]{3,2,1,0:T(8,128)(2,1)S(1)}, bf16[9,2,128,128]{3,2,1,0:T(8,128)(2,1)}, u32[]{:S(2)}, u32[]{:S(2)}) collective-permute-start(bf16[9,2,128,128]{3,2,1,0:T(8,128)(2,1)S(1)} %pad_maximum_fusion.1), channel_id=1, source_target_pairs={{0,32},{32,64},{64,96},{96,128},{128,160},{160,192},{192,224},{224... | collective-permute-start | bytes 1769480 | tf_op jit(solution)/shard_map/ppermute | solution.py:363
  259.8 28.4 %collective-permute-start.30 = (bf16[9,2,128,128]{3,2,1,0:T(8,128)(2,1)S(1)}, bf16[9,2,128,128]{3,2,1,0:T(8,128)(2,1)}, u32[]{:S(2)}, u32[]{:S(2)}) collective-permute-start(bf16[9,2,128,128]{3,2,1,0:T(8,128)(2,1)S(1)} %pad_maximum_fusion.2), channel_id=1, source_target_pairs={{0,224},{32,0},{64,32},{96,64},{128,96},{160,128},{192,160},{224,1... | collective-permute-start | bytes 1769480 | tf_op jit(solution)/shard_map/ppermute | solution.py:363
  263.3 29.4 %collective-permute-start.35 = (f32[2,2,128,128]{3,2,1,0:T(8,128)}, f32[2,2,128,128]{3,2,1,0:T(8,128)}, u32[]{:S(2)}, u32[]{:S(2)}) collective-permute-start(f32[2,2,128,128]{3,2,1,0:T(8,128)} %get-tuple-element.72), channel_id=1, source_target_pairs={{128,0},{132,4},{136,8},{140,12},{144,16},{148,20},{152,24},{156,2... | collective-permute-start | bytes 786440 | tf_op jit(solution)/shard_map/ppermute | solution.py:382
  288.1 20.6 %collective-permute-start.27 = (bf16[9,2,128,128]{3,2,1,0:T(8,128)(2,1)S(1)}, bf16[9,2,128,128]{3,2,1,0:T(8,128)(2,1)S(1)}, u32[]{:S(2)}, u32[]{:S(2)}) collective-permute-start(bf16[9,2,128,128]{3,2,1,0:T(8,128)(2,1)S(1)} %add_convert_fusion.3), channel_id=1, source_target_pairs={{0,32},{32,64},{64,96},{96,128},{128,160},{160,192},{192,224},{224... | collective-permute-start | bytes 1769480 | tf_op jit(solution)/shard_map/ppermute | solution.py:363
  289.4 23.0 %collective-permute-start.31 = (bf16[9,2,128,128]{3,2,1,0:T(8,128)(2,1)S(1)}, bf16[9,2,128,128]{3,2,1,0:T(8,128)(2,1)S(1)}, u32[]{:S(2)}, u32[]{:S(2)}) collective-permute-start(bf16[9,2,128,128]{3,2,1,0:T(8,128)(2,1)S(1)} %add_convert_fusion.1), channel_id=1, source_target_pairs={{0,224},{32,0},{64,32},{96,64},{128,96},{160,128},{192,160},{224,1... | collective-permute-start | bytes 1769480 | tf_op jit(solution)/shard_map/ppermute | solution.py:363
  293.7 13.6 %collective-permute-start.36 = (f32[2,2,128,128]{3,2,1,0:T(8,128)S(1)}, f32[2,2,128,128]{3,2,1,0:T(8,128)S(1)}, u32[]{:S(2)}, u32[]{:S(2)}) collective-permute-start(f32[2,2,128,128]{3,2,1,0:T(8,128)S(1)} %add.162), channel_id=1, source_target_pairs={{64,0},{68,4},{72,8},{76,12},{80,16},{84,20},{88,24},{92,28},{96,3... | collective-permute-start | bytes 786440 | tf_op jit(solution)/shard_map/ppermute | solution.py:382
  307.4 11.1 %collective-permute-start.37 = (f32[2,2,128,128]{3,2,1,0:T(8,128)S(1)}, f32[2,2,128,128]{3,2,1,0:T(8,128)S(1)}, u32[]{:S(2)}, u32[]{:S(2)}) collective-permute-start(f32[2,2,128,128]{3,2,1,0:T(8,128)S(1)} %add.163), channel_id=1, source_target_pairs={{32,0},{36,4},{40,8},{44,12},{48,16},{52,20},{56,24},{60,28},{33,1... | collective-permute-start | bytes 786440 | tf_op jit(solution)/shard_map/ppermute | solution.py:382
  309.7 30.0 %collective-permute-start.28 = (bf16[9,2,128,128]{3,2,1,0:T(8,128)(2,1)}, bf16[9,2,128,128]{3,2,1,0:T(8,128)(2,1)}, u32[]{:S(2)}, u32[]{:S(2)}) collective-permute-start(bf16[9,2,128,128]{3,2,1,0:T(8,128)(2,1)} %add_convert_fusion.2), channel_id=1, source_target_pairs={{0,32},{32,64},{64,96},{96,128},{128,160},{160,192},{192,224},{224... | collective-permute-start | bytes 1769480 | tf_op jit(solution)/shard_map/ppermute | solution.py:363
  313.4 26.5 %collective-permute-start.32 = (bf16[9,2,128,128]{3,2,1,0:T(8,128)(2,1)}, bf16[9,2,128,128]{3,2,1,0:T(8,128)(2,1)}, u32[]{:S(2)}, u32[]{:S(2)}) collective-permute-start(bf16[9,2,128,128]{3,2,1,0:T(8,128)(2,1)} %add_convert_fusion), channel_id=1, source_target_pairs={{0,224},{32,0},{64,32},{96,64},{128,96},{160,128},{192,160},{224,1... | collective-permute-start | bytes 1769480 | tf_op jit(solution)/shard_map/ppermute | solution.py:363
  318.5 9.8 %collective-permute-start.38 = (f32[2,2,128,128]{3,2,1,0:T(8,128)S(1)}, f32[2,2,128,128]{3,2,1,0:T(8,128)S(1)}, u32[]{:S(2)}, u32[]{:S(2)}) collective-permute-start(f32[2,2,128,128]{3,2,1,0:T(8,128)S(1)} %add.164), channel_id=1, source_target_pairs={{16,0},{20,4},{24,8},{28,12},{17,1},{21,5},{25,9},{29,13},{18,2},{... | collective-permute-start | bytes 786440 | tf_op jit(solution)/shard_map/ppermute | solution.py:382
  328.3 10.7 %collective-permute-start.39 = (f32[2,2,128,128]{3,2,1,0:T(8,128)S(1)}, f32[2,2,128,128]{3,2,1,0:T(8,128)S(1)}, u32[]{:S(2)}, u32[]{:S(2)}) collective-permute-start(f32[2,2,128,128]{3,2,1,0:T(8,128)S(1)} %add.165), channel_id=1, source_target_pairs={{8,0},{12,4},{9,1},{13,5},{10,2},{14,6},{11,3},{15,7}} | collective-permute-start | bytes 786440 | tf_op jit(solution)/shard_map/ppermute | solution.py:382
  333.4 12.2 %collective-permute-start.34 = (bf16[1,2,128,128]{3,2,1,0:T(8,128)(2,1)S(1)}, bf16[1,2,128,128]{3,2,1,0:T(8,128)(2,1)S(1)}, u32[]{:S(2)}, u32[]{:S(2)}) collective-permute-start(bf16[1,2,128,128]{3,2,1,0:T(8,128)(2,1)S(1)} %get-tuple-element.93), channel_id=1, source_target_pairs={{0,4},{4,8},{8,12},{12,16},{16,20},{20,24},{24,28},{28,32},{32,36}... | collective-permute-start | bytes 196616 | tf_op jit(solution)/shard_map/ppermute | solution.py:434
  335.4 8.3 %collective-permute-start.33 = (bf16[1,2,128,128]{3,2,1,0:T(8,128)(2,1)S(1)}, bf16[1,2,128,128]{3,2,1,0:T(8,128)(2,1)S(1)}, u32[]{:S(2)}, u32[]{:S(2)}) collective-permute-start(bf16[1,2,128,128]{3,2,1,0:T(8,128)(2,1)S(1)} %get-tuple-element.94), channel_id=1, source_target_pairs={{4,0},{8,4},{12,8},{16,12},{20,16},{24,20},{28,24},{32,28},{36,32}... | collective-permute-start | bytes 196616 | tf_op jit(solution)/shard_map/ppermute | solution.py:433
  339.1 6.6 %collective-permute-start.40 = (f32[2,2,128,128]{3,2,1,0:T(8,128)S(1)}, f32[2,2,128,128]{3,2,1,0:T(8,128)S(1)}, u32[]{:S(2)}, u32[]{:S(2)}) collective-permute-start(f32[2,2,128,128]{3,2,1,0:T(8,128)S(1)} %add.166), channel_id=1, source_target_pairs={{4,0},{5,1},{6,2},{7,3}} | collective-permute-start | bytes 786440 | tf_op jit(solution)/shard_map/ppermute | solution.py:382
  339.8 31.1 %collective-permute-start.22 = (bf16[2304,128]{1,0:T(8,128)(2,1)S(1)}, bf16[2304,128]{1,0:T(8,128)(2,1)S(1)}, u32[]{:S(2)}, u32[]{:S(2)}) collective-permute-start(bf16[2304,128]{1,0:T(8,128)(2,1)S(1)} %copy-done.7), channel_id=1, source_target_pairs={{0,1},{1,2},{2,3},{3,0},{4,5},{5,6},{6,7},{7,4},{8,9},{9,10},{10,1... | collective-permute-start | bytes 1769480 | tf_op jit(solution)/shard_map/ppermute | solution.py:349
  339.9 31.0 %collective-permute-start.23 = (bf16[2304,128]{1,0:T(8,128)(2,1)S(1)}, bf16[2304,128]{1,0:T(8,128)(2,1)}, u32[]{:S(2)}, u32[]{:S(2)}) collective-permute-start(bf16[2304,128]{1,0:T(8,128)(2,1)S(1)} %get-tuple-element.59), channel_id=1, source_target_pairs={{0,2},{1,3},{2,0},{3,1},{4,6},{5,7},{6,4},{7,5},{8,10},{9,11},{10,... | collective-permute-start | bytes 1769480 | tf_op jit(solution)/shard_map/ppermute | solution.py:349
  343.6 27.3 %collective-permute-start.24 = (bf16[2304,128]{1,0:T(8,128)(2,1)S(1)}, bf16[2304,128]{1,0:T(8,128)(2,1)}, u32[]{:S(2)}, u32[]{:S(2)}) collective-permute-start(bf16[2304,128]{1,0:T(8,128)(2,1)S(1)} %get-tuple-element.60), channel_id=1, source_target_pairs={{0,3},{1,0},{2,1},{3,2},{4,7},{5,4},{6,5},{7,6},{8,11},{9,8},{10,9... | collective-permute-start | bytes 1769480 | tf_op jit(solution)/shard_map/ppermute | solution.py:349
  346.9 29.0 %all-to-all-start.6 = ((bf16[4,2,288,128]{3,2,1,0:T(8,128)(2,1)}), bf16[4,2,288,128]{3,2,1,0:T(8,128)(2,1)S(1)}, u32[]{:S(2)}, u32[]{:S(2)}) async-start(bf16[4,2,288,128]{3,2,1,0:T(8,128)(2,1)} %copy.81), calls=%async_computation.6 | async-start | bytes 1179648 | tf_op jit(solution)/shard_map/all_to_all | solution.py:345
  (20 other events, 236.7 us)

commit v2 on v1

v2 whole, which is shorter than its diff:
```python
import functools

import jax
import jax.numpy as jnp
import numpy as np
from jax import lax
from jax.experimental import pallas as pl
from jax.experimental.pallas import tpu as pltpu
from jax.sharding import Mesh, PartitionSpec as P

HD = 128
BLK = 128
G = 2
RND = 3
NZ, NX, NC, NH = 8, 4, 2, 4
SEQ = ("z", "x", "c")
NSEQ = NZ * NX * NC
QB = 9
NB = NSEQ * QB
HL = 8
ROWS = BLK * HL
TOK = 288
SCALE = 1.0 / HD**0.5
LOG2E = 1.4426950408889634
MASKED = 1e30
ENT = QB * RND
AT_SEQ, AT_HEAD, AT_WANT = ENT, ENT + 1, ENT + 2
STEP = 8
PART = TOK * HL
BF = jnp.bfloat16
F32 = jnp.float32
ANY = pl.ANY


def dot(a, b, ca, cb):
    return lax.dot_general(a, b, (((ca,), (cb,)), ((), ())), preferred_element_type=F32)


def row_vector(tile):
    return jnp.concatenate([tile[i : i + 1, :] for i in range(HL)], axis=1)


def pair_grads(keys, values, biases, q, do, lse2, delta, key_scr, p_scr, ds_scr):
    n = len(keys)
    for t in range(n):
        rows = pl.ds(t * BLK, BLK)
        key_scr[rows, :] = keys[t]
        s = dot(keys[t], q, 1, 1)
        p = jnp.exp2(s * (SCALE * LOG2E) - (lse2 + biases[t]))
        dp = dot(values[t], do, 1, 1)
        p_scr[rows, :] = p.astype(BF)
        ds_scr[rows, :] = (p * (dp - delta)).astype(BF)
    dv = dot(p_scr[...], do, 1, 0)
    dk = dot(ds_scr[...], q, 1, 0) * SCALE
    dqt = dot(key_scr[...], ds_scr[...], 0, 0)
    return dk, dv, dqt


def load_parts(meta, parts, whole, sems):
    copies = []
    for i, (four, target) in enumerate(zip(parts, whole)):
        for k in range(NH):
            row = pl.multiple_of(((meta[AT_HEAD] - k) & (NH - 1)) * PART, PART)
            copies.append(
                pltpu.make_async_copy(four[k], target.at[pl.ds(row, PART)], sems.at[i, k])
            )
    for c in copies:
        c.start()
    for c in copies:
        c.wait()


def near_kernel(
    meta, q0, q1, q2, q3, d0, d1, d2, d3, ld_ref, kv_ref, gl_ref,
    dqt_ref, dkv_ref, dg_ref, q_scr, do_scr, key_scr, p_scr, ds_scr, sems,
):
    b = pl.program_id(0)

    @pl.when(b == 0)
    def _():
        load_parts(meta, ((q0, q1, q2, q3), (d0, d1, d2, d3)), (q_scr, do_scr), sems)
        dkv_ref[...] = jnp.zeros_like(dkv_ref)
        dg_ref[...] = jnp.zeros_like(dg_ref)

    block = meta[AT_SEQ] * QB + b
    keys = [gl_ref[0, 0], gl_ref[1, 0]] + [kv_ref[b + w, 0] for w in range(3)]
    values = [gl_ref[0, 1], gl_ref[1, 1]] + [kv_ref[b + w, 1] for w in range(3)]
    biases = [0.0, 0.0]
    for w in range(3):
        c = block + (w - 1)
        biases.append(jnp.where((c >= G) & (c <= NB - 1), 0.0, MASKED))
    lse2, delta = row_vector(ld_ref[0, 0]), row_vector(ld_ref[1, 0])
    rows = pl.ds(pl.multiple_of(b * ROWS, ROWS), ROWS)
    dk, dv, dqt = pair_grads(
        keys, values, biases, q_scr[rows, :], do_scr[rows, :], lse2, delta, key_scr, p_scr, ds_scr
    )
    dqt_ref[0] = dqt
    for t in range(G):
        dg_ref[t, 0] += dk[t * BLK : (t + 1) * BLK]
        dg_ref[t, 1] += dv[t * BLK : (t + 1) * BLK]
    for w in range(3):
        t = G + w
        dkv_ref[b + w, 0] += dk[t * BLK : (t + 1) * BLK]
        dkv_ref[b + w, 1] += dv[t * BLK : (t + 1) * BLK]


def random_kernel(
    meta, q0, q1, q2, q3, d0, d1, d2, d3, ld_ref, got_ref, dqt_ref,
    dq0, dq1, dq2, dq3, dkv_ref,
    q_scr, do_scr, dq_scr, kv_scr, out_scr, key_scr, p_scr, ds_scr, sems, in_sems, out_sems, dq_sems,
):
    b = pl.program_id(0)

    def fetch(e):
        return pltpu.make_async_copy(got_ref.at[meta[e] >> 4], kv_scr.at[e], in_sems.at[e])

    def give(e):
        return pltpu.make_async_copy(out_scr.at[e], dkv_ref.at[meta[e] >> 4], out_sems.at[e])

    @pl.when(b == 0)
    def _():
        for e in range(ENT):
            fetch(e).start()
        load_parts(meta, ((q0, q1, q2, q3), (d0, d1, d2, d3)), (q_scr, do_scr), sems)

    first = b * RND
    block = meta[AT_SEQ] * QB + b
    biases = []
    for j in range(RND):
        named = meta[first + j]
        r = (named >> 4) * QB + (named & 15)
        biases.append(jnp.where((r >= G) & (jnp.abs(r - block) >= 2), 0.0, MASKED))
        fetch(first + j).wait()
    lse2, delta = row_vector(ld_ref[0, 0]), row_vector(ld_ref[1, 0])
    rows = pl.ds(pl.multiple_of(b * ROWS, ROWS), ROWS)
    dk, dv, dqt = pair_grads(
        [kv_scr[first + j, 0] for j in range(RND)],
        [kv_scr[first + j, 1] for j in range(RND)],
        biases, q_scr[rows, :], do_scr[rows, :], lse2, delta, key_scr, p_scr, ds_scr,
    )
    dq_scr[rows, :] = ((dqt + dqt_ref[0]).T * SCALE).astype(BF)
    for j in range(RND):
        n = first + j
        out_scr[n, 0] = dk[j * BLK : (j + 1) * BLK].astype(BF)
        out_scr[n, 1] = dv[j * BLK : (j + 1) * BLK].astype(BF)
        give(n).start()

    @pl.when(b == QB - 1)
    def _():
        copies = []
        for k, target in enumerate((dq0, dq1, dq2, dq3)):
            row = pl.multiple_of(((meta[AT_HEAD] + k) & (NH - 1)) * PART, PART)
            copies.append(
                pltpu.make_async_copy(dq_scr.at[pl.ds(row, PART)], target, dq_sems.at[k])
            )
        for c in copies:
            c.start()
        for c in copies:
            c.wait()
        for e in range(ENT):
            give(e).wait()


def select_kernel(meta, kv_ref, out_ref):
    base = pl.program_id(0) * STEP
    for i in range(STEP):
        slot = meta[AT_WANT + base + i]

        @pl.when(slot >= 0)
        def _():
            out_ref[i] = kv_ref[slot]


def collect_kernel(meta, got, ext, lower, upper, dg, out, acc):
    step = pl.program_id(0)

    @pl.when(step == 0)
    def _():
        acc[...] = ext[1 : QB + 1]
        acc[QB - 1] += lower[0].astype(F32)
        acc[0] += upper[0].astype(F32)

        @pl.when(meta[AT_SEQ] == 0)
        def _():
            for t in range(G):
                acc[t] += dg[t]

    for i in range(STEP):
        slot = meta[AT_WANT + step * STEP + i]

        @pl.when(slot >= 0)
        def _():
            acc[slot] += got[i].astype(F32)

    @pl.when(step == NSEQ // STEP - 1)
    def _():
        out[...] = acc[...].astype(BF)


TILE = (2, BLK, HD)
PARAMS = pltpu.CompilerParams(vmem_limit_bytes=50 << 20)


def full(*shape):
    return pl.BlockSpec(shape, lambda b, m: (0,) * len(shape))


def anywhere(n):
    return [pl.BlockSpec(memory_space=ANY)] * n


def work_scratch(n):
    return [
        pltpu.VMEM((n * BLK, HD), BF),
        pltpu.VMEM((n * BLK, ROWS), BF),
        pltpu.VMEM((n * BLK, ROWS), BF),
    ]


ROW_PAIR = pl.BlockSpec((2, 1, HL, BLK), lambda b, m: (0, b, 0, 0))
DQT = pl.BlockSpec((1, HD, ROWS), lambda b, m: (b, 0, 0))


def call_near(meta, q, do, ld, kvx, gl):
    return pl.pallas_call(
        near_kernel,
        grid_spec=pltpu.PrefetchScalarGridSpec(
            num_scalar_prefetch=1,
            grid=(QB,),
            in_specs=anywhere(2 * NH) + [ROW_PAIR, full(QB + 2, *TILE), full(G, *TILE)],
            out_specs=[DQT, full(QB + 2, *TILE), full(G, *TILE)],
            scratch_shapes=[pltpu.VMEM((QB * ROWS, HD), BF)] * 2
            + work_scratch(G + 3)
            + [pltpu.SemaphoreType.DMA((2, NH))],
        ),
        out_shape=[
            jax.ShapeDtypeStruct((QB, HD, ROWS), F32),
            jax.ShapeDtypeStruct((QB + 2, *TILE), F32),
            jax.ShapeDtypeStruct((G, *TILE), F32),
        ],
        compiler_params=PARAMS,
        name="near",
    )(meta, *q, *do, ld, kvx, gl)


def call_random(meta, q, do, ld, got, dqt):
    return pl.pallas_call(
        random_kernel,
        grid_spec=pltpu.PrefetchScalarGridSpec(
            num_scalar_prefetch=1,
            grid=(QB,),
            in_specs=anywhere(2 * NH) + [ROW_PAIR] + anywhere(1) + [DQT],
            out_specs=anywhere(NH + 1),
            scratch_shapes=[pltpu.VMEM((QB * ROWS, HD), BF)] * 3
            + [pltpu.VMEM((ENT, *TILE), BF)] * 2
            + work_scratch(RND)
            + [
                pltpu.SemaphoreType.DMA((2, NH)),
                pltpu.SemaphoreType.DMA((ENT,)),
                pltpu.SemaphoreType.DMA((ENT,)),
                pltpu.SemaphoreType.DMA((NH,)),
            ],
        ),
        out_shape=[jax.ShapeDtypeStruct((PART, HD), BF)] * NH
        + [jax.ShapeDtypeStruct((NSEQ, *TILE), BF)],
        compiler_params=PARAMS,
        name="random",
    )(meta, *q, *do, ld, got, dqt)


STEP_TILES = pl.BlockSpec((STEP, *TILE), lambda b, m: (b, 0, 0, 0))


def call_select(meta, kv):
    return pl.pallas_call(
        select_kernel,
        grid_spec=pltpu.PrefetchScalarGridSpec(
            num_scalar_prefetch=1,
            grid=(NSEQ // STEP,),
            in_specs=[full(QB, *TILE)],
            out_specs=STEP_TILES,
        ),
        out_shape=jax.ShapeDtypeStruct((NSEQ, *TILE), BF),
        compiler_params=PARAMS,
        name="select",
    )(meta, kv)


def call_collect(meta, got, ext, lower, upper, dg):
    return pl.pallas_call(
        collect_kernel,
        grid_spec=pltpu.PrefetchScalarGridSpec(
            num_scalar_prefetch=1,
            grid=(NSEQ // STEP,),
            in_specs=[STEP_TILES, full(QB + 2, *TILE), full(1, *TILE), full(1, *TILE), full(G, *TILE)],
            out_specs=full(QB, *TILE),
            scratch_shapes=[pltpu.VMEM((QB, *TILE), F32)],
        ),
        out_shape=jax.ShapeDtypeStruct((QB, *TILE), BF),
        compiler_params=PARAMS,
        name="collect",
    )(meta, got, ext, lower, upper, dg)


def join_kernel(head, p0, p1, p2, p3, out):
    for k, p in enumerate((p0, p1, p2, p3)):
        out[:, (head[0] - k) & (NH - 1)] = p[...]


def call_join(head, parts):
    rows = TOK // 3
    return pl.pallas_call(
        join_kernel,
        grid_spec=pltpu.PrefetchScalarGridSpec(
            num_scalar_prefetch=1,
            grid=(3,),
            in_specs=[pl.BlockSpec((rows, HL, HD), lambda b, m: (b, 0, 0))] * NH,
            out_specs=pl.BlockSpec((rows, NH, HL, HD), lambda b, m: (b, 0, 0, 0)),
        ),
        out_shape=jax.ShapeDtypeStruct((TOK, NH, HL, HD), BF),
        name="join",
    )(head, *[p.reshape(TOK, HL, HD) for p in parts])


def plain_a2a(value, axis):
    return lax.all_to_all(value, axis, split_axis=0, concat_axis=0, tiled=True)


def turn(value, k):
    return lax.ppermute(value, "head", [(i, (i + k) % NH) for i in range(NH)]) if k else value


def head_parts(value, head):
    parts = value.reshape(TOK, NH, HL, HD)
    return [
        lax.dynamic_index_in_dim(parts, lax.rem(head + k, NH), axis=1, keepdims=False).reshape(PART, HD)
        for k in range(NH)
    ]


def tie(*values):
    return lax.optimization_barrier(values)


def spread(value, index):
    k = 1
    while k < NSEQ:
        got = lax.ppermute(value, SEQ, [(i, i + k) for i in range(k)])
        value = jnp.where((index >= k) & (index < 2 * k), got, value)
        k *= 2
    return value


def gather_sum(value):
    k = NSEQ // 2
    while k:
        value = value + lax.ppermute(value, SEQ, [(i + k, i) for i in range(k)])
        k //= 2
    return value


def per_device(q, k, v, o, do, lse, owner, slot):
    head, seq = lax.axis_index("head"), lax.axis_index(SEQ)
    named = (owner * 16 + slot).reshape(NSEQ, ENT)
    mine = lax.dynamic_index_in_dim(named, seq, 0, keepdims=False)
    want = jnp.max(jnp.where(named >> 4 == seq, named & 15, -1), axis=1)
    meta = jnp.concatenate([mine, jnp.stack([seq, head]).astype(jnp.int32), want])

    kv = jnp.stack([k, v]).transpose(2, 0, 1, 3)
    kv = plain_a2a(kv, "head")
    kv = kv.transpose(1, 0, 2, 3).reshape(2, QB, BLK, HD).transpose(1, 0, 2, 3)
    got = plain_a2a(call_select(meta, kv), SEQ)

    up = [(i, i + 1) for i in range(NSEQ - 1)]
    down = [(i + 1, i) for i in range(NSEQ - 1)]
    qp, dop = head_parts(q, head), head_parts(do, head)
    ql = [turn(p, i) for i, p in enumerate(qp)]
    dol = [turn(p, i) for i, p in enumerate(dop)]
    before = lax.ppermute(kv[QB - 1 :], SEQ, up)
    after = lax.ppermute(kv[:1], SEQ, down)
    kvx = jnp.concatenate([before, kv, after])
    gl = spread(kv[:G], seq)
    delta = jnp.sum(do.astype(F32) * o.astype(F32), axis=-1)
    ld = jnp.stack([lse * LOG2E, delta]).reshape(2, TOK, NH, HL).transpose(2, 0, 1, 3)
    ld = ld.reshape(NH, 2, PART // BLK, BLK)
    ld = jnp.stack([turn(lax.dynamic_index_in_dim(ld, lax.rem(head + i, NH), 0, keepdims=False), i) for i in range(NH)])
    ld = jnp.roll(ld[::-1], head + 1, axis=0)
    ld = ld.transpose(1, 0, 2, 3).reshape(2, QB, HL, BLK)

    dqt, dkvx, dg = call_near(meta, ql, dol, ld, kvx, gl)
    *dq, back = call_random(meta, ql, dol, ld, got, dqt)

    back = plain_a2a(back, SEQ)
    dq = call_join(head.reshape(1), [turn(p, i) for i, p in enumerate(dq)])
    lower = lax.ppermute(dkvx[:1].astype(BF), SEQ, down)
    upper = lax.ppermute(dkvx[QB + 1 :].astype(BF), SEQ, up)
    back, dq = tie(back, dq)
    total = call_collect(meta, back, dkvx, lower, upper, gather_sum(dg))
    dkv = total.transpose(1, 0, 2, 3).reshape(2, NH, TOK, HD).transpose(1, 0, 2, 3)
    dkv = plain_a2a(dkv, "head")
    dk = dkv[:, 0].transpose(1, 0, 2)
    dv = dkv[:, 1].transpose(1, 0, 2)
    return dq.reshape(TOK, NH * HL, HD), dk, dv


def solution(mesh):
    grid = Mesh(np.asarray(mesh.devices).reshape(NZ, NX, NC, NH), ("z", "x", "c", "head"))
    split = ("z", "x", "c", "head")
    wide = P(split, None, None)
    return jax.shard_map(
        per_device,
        mesh=grid,
        in_specs=(wide,) * 5 + (P(split, None), P(), P()),
        out_specs=(wide,) * 3,
        check_vma=False,
    )
```

time: 380 us -> 440 us (1.16)
  waiting for transfers between devices: 148 us -> 267 us
  blocking collectives: 40 us -> 13 us
  starting transfers between devices: 93.2 us -> 72.4 us
  local copies, waits for them, and re-layouts: 23.8 us -> 19 us
    ppermute x6, waiting for transfers between devices: 25.4 us -> 135 us  [gather_sum(): value = value + lax.ppermute(value, SEQ, [(i + k, i) for i in range(k)])]
    ppermute x6, waiting for transfers between devices: 27.1 us -> 77.1 us  [spread(): got = lax.ppermute(value, SEQ, [(i, i + k) for i in range(k)])]
    ppermute x16 -> x0, starting transfers between devices: 29.4 us -> none  [along_z(): return lax.ppermute(value, 'z', [(i, (i + step) % NZ) for i in range(NZ)])]
    all_to_all x2 -> x1, blocking collectives: 40 us -> 13 us  [plain_a2a(): return lax.all_to_all(value, axis, split_axis=0, concat_axis=0, tiled=True)]
    ppermute x16 -> x0, waiting for transfers between devices: 22.9 us -> none  [along_z(): return lax.ppermute(value, 'z', [(i, (i + step) % NZ) for i in range(NZ)])]
    ppermute x9 -> x12, waiting for transfers between devices: 53.5 us -> 45.8 us  [turn(): lax.ppermute(value, 'head', [(i, (i + k) % NH) for i in range(NH)])]
    ppermute x1, waiting for transfers between devices: 7.04 us -> 0.01 us  [per_device(): before = lax.ppermute(kv[QB - 1:], SEQ, up)]
    squeeze x2 -> x1, local copies, waits for them, and re-layouts: 5.82 us -> 0.01 us  [per_device(): mine = lax.dynamic_index_in_dim(named, seq, 0, keepdims=False)]
  transfers between devices with their start and end apart: 46 -> 31, of which waited for: 13 -> 16; matrix products, arithmetic and copies ran while one was open for 9% -> 5% of each run, Pallas kernels for 10% -> 6%
where the time goes in v2:
time: 440 us; the launch traced here: 437 us
  waiting for transfers between devices  267 us (61%)
  starting transfers between devices  72.4 us (16%)
  Pallas kernels  53.1 us (12%)
  local copies, waits for them, and re-layouts  19 us (4%)
  blocking collectives  13 us (3%)
  other arithmetic  10.6 us (2%)
    ppermute x6, waiting for transfers between devices, gather_sum(): value = value + lax.ppermute(value, SEQ, [(i + k, i) for i in range(k)])  135 us
    ppermute x6, waiting for transfers between devices, spread(): got = lax.ppermute(value, SEQ, [(i, i + k) for i in range(k)])  77.1 us
    ppermute x12, waiting for transfers between devices, turn(): lax.ppermute(value, 'head', [(i, (i + k) % NH) for i in range(NH)])  45.8 us
    all_to_all x3, starting transfers between devices, plain_a2a(): return lax.all_to_all(value, axis, split_axis=0, concat_axis=0, tiled=True)  28.4 us
    pallas_call x1, Pallas kernels, call_near(): pl.pallas_call(near_kernel, grid_spec=pltpu.PrefetchScalarGridSpec(num_sc...  21.7 us
    pallas_call x1, Pallas kernels, call_random(): pl.pallas_call(random_kernel, grid_spec=pltpu.PrefetchScalarGridSpec(num_...  17.5 us
    ppermute x12, starting transfers between devices, turn(): lax.ppermute(value, 'head', [(i, (i + k) % NH) for i in range(NH)])  14.4 us
    all_to_all x1, blocking collectives, plain_a2a(): return lax.all_to_all(value, axis, split_axis=0, concat_axis=0, tiled=True)  13 us
  transfers between devices with their start and end apart: 31, of which 16 were waited for; matrix products, arithmetic and copies ran while one was open for 5% of the time, Pallas kernels for 6%

profile of v2, /device:TPU:2, one launch (start us, length us, event | category | flops | bytes accessed | tf_op | source)
XLA Modules:
  0.0 436.7 jit_solution(10779316791692027526)
XLA Ops:
  2.7 4.5 %all-to-all-start = ((bf16[4,2,288,128]{3,2,1,0:T(8,128)(2,1)}), bf16[4,2,288,128]{3,2,1,0:T(8,128)(2,1)S(1)}, u32[]{:S(2)}, u32[]{:S(2)}) async-start(bf16[4,2,288,128]{3,2,1,0:T(8,128)(2,1)} %maximum_bitcast_fusion), calls=%async_computation | async-start | bytes 1179648 | tf_op jit(solution)/shard_map/all_to_all | solution.py:326
  7.8 9.5 %all-to-all-done = bf16[4,2,288,128]{3,2,1,0:T(8,128)(2,1)S(1)} async-done(((bf16[4,2,288,128]{3,2,1,0:T(8,128)(2,1)}), bf16[4,2,288,128]{3,2,1,0:T(8,128)(2,1)S(1)}, u32[]{:S(2)}, u32[]{:S(2)}) %all-to-all-start) | async-done | bytes 589856 | tf_op jit(solution)/shard_map/all_to_all | solution.py:326
  17.4 4.2 select.11
  21.6 12.3 %all-to-all-start.1 = ((bf16[64,2,128,128]{3,2,1,0:T(8,128)(2,1)}), bf16[64,2,128,128]{3,2,1,0:T(8,128)(2,1)}, u32[]{:S(2)}, u32[]{:S(2)}) async-start(bf16[64,2,128,128]{3,2,1,0:T(8,128)(2,1)} %select.11), calls=%async_computation.1 | async-start | bytes 8388608 | tf_op jit(solution)/shard_map/all_to_all | solution.py:326
  34.8 3.2 multiply_reduce_fusion
  38.2 1.3 collective-permute-start.12
  39.5 9.5 %collective-permute-done.12 = bf16[2,2,128,128]{3,2,1,0:T(8,128)(2,1)S(1)} collective-permute-done((bf16[2,2,128,128]{3,2,1,0:T(8,128)(2,1)S(1)}, bf16[2,2,128,128]{3,2,1,0:T(8,128)(2,1)S(1)}, u32[]{:S(2)}, u32[]{:S(2)}) %collective-permute-start.12) | collective-permute-done | bytes 131104 | tf_op jit(solution)/shard_map/ppermute | solution.py:348
  49.0 1.3 collective-permute-start.13
  53.1 1.5 collective-permute-start.7
  55.5 1.3 collective-permute-start.14
  56.8 2.9 dynamic-slice_bitcast_fusion.4
  59.7 2.3 collective-permute-start.2
  62.1 64.8 %collective-permute-done.14 = bf16[2,2,128,128]{3,2,1,0:T(8,128)(2,1)S(1)} collective-permute-done((bf16[2,2,128,128]{3,2,1,0:T(8,128)(2,1)S(1)}, bf16[2,2,128,128]{3,2,1,0:T(8,128)(2,1)S(1)}, u32[]{:S(2)}, u32[]{:S(2)}) %collective-permute-start.14) | collective-permute-done | bytes 131104 | tf_op jit(solution)/shard_map/ppermute | solution.py:348
  126.9 1.3 collective-permute-start.15
  128.9 1.9 collective-permute-done.15
  130.7 1.9 collective-permute-start.9
  133.3 3.6 collective-permute-start.10
  137.0 1.9 collective-permute-start.16
  138.9 2.9 dynamic-slice_bitcast_fusion
  143.7 1.5 collective-permute-start
  145.1 1.8 collective-permute-start.5
  146.9 1.8 collective-permute-start.4
  149.3 1.4 pad_maximum_fusion.1
  150.7 1.5 rev.3
  153.2 1.9 pad_maximum_fusion.kv_ref
  156.0 4.5 %collective-permute-done.1.q2 = bf16[2304,128]{1,0:T(8,128)(2,1)S(1)} collective-permute-done((bf16[2304,128]{1,0:T(8,128)(2,1)}, bf16[2304,128]{1,0:T(8,128)(2,1)S(1)}, u32[]{:S(2)}, u32[]{:S(2)}) %collective-permute-start.1) | collective-permute-done | bytes 589856 | tf_op jit(solution)/shard_map/ppermute | solution.py:330
  160.5 12.7 %collective-permute-done.q1 = bf16[2304,128]{1,0:T(8,128)(2,1)S(1)} collective-permute-done((bf16[2304,128]{1,0:T(8,128)(2,1)}, bf16[2304,128]{1,0:T(8,128)(2,1)S(1)}, u32[]{:S(2)}, u32[]{:S(2)}) %collective-permute-start) | collective-permute-done | bytes 589856 | tf_op jit(solution)/shard_map/ppermute | solution.py:330
  173.2 12.7 %collective-permute-done.4.d2 = bf16[2304,128]{1,0:T(8,128)(2,1)} collective-permute-done((bf16[2304,128]{1,0:T(8,128)(2,1)}, bf16[2304,128]{1,0:T(8,128)(2,1)}, u32[]{:S(2)}, u32[]{:S(2)}) %collective-permute-start.4) | collective-permute-done | bytes 589856 | tf_op jit(solution)/shard_map/ppermute | solution.py:330
  185.9 11.4 %collective-permute-done.3.d1 = bf16[2304,128]{1,0:T(8,128)(2,1)} collective-permute-done((bf16[2304,128]{1,0:T(8,128)(2,1)}, bf16[2304,128]{1,0:T(8,128)(2,1)}, u32[]{:S(2)}, u32[]{:S(2)}) %collective-permute-start.3) | collective-permute-done | bytes 589856 | tf_op jit(solution)/shard_map/ppermute | solution.py:330
  197.3 21.7 %near.1 = (f32[9,128,1024]{2,1,0:T(8,128)}, f32[11,2,128,128]{3,2,1,0:T(8,128)}, f32[2,2,128,128]{3,2,1,0:T(8,128)S(1)}) custom-call(s32[93]{0:T(128)S(1)} %pad_add_fusion.meta, bf16[2304,128]{1,0:T(8,128)(2,1)S(1)} %get-tuple-element.41.q0, bf16[2304,128]{1,0:T(8,128)(2,1)S(1)} %collective-permute-done.q1, bf16[2304,128]{1,0:T(8,128)(2,1)S(1)} %collective-permute-done.1.q2, ...), custom_call_target="tpu_custom_call" | custom-call | tf_op jit(solution)/shard_map/near/pallas_call | solution.py:225
  220.7 17.5 %random.1 = (bf16[2304,128]{1,0:T(8,128)(2,1)S(1)}, bf16[2304,128]{1,0:T(8,128)(2,1)}, bf16[2304,128]{1,0:T(8,128)(2,1)S(1)}, bf16[2304,128]{1,0:T(8,128)(2,1)S(1)}, bf16[64,2,128,128]{3,2,1,0:T(8,128)(2,1)}) custom-call(s32[93]{0:T(128)S(1)} %pad_add_fusion.meta, bf16[2304,128]{1,0:T(8,128)(2,1)S(1)} %get-tuple-element.41.q0, ...), custom_call_target="tpu_custom_call" | custom-call | tf_op jit(solution)/shard_map/random/pallas_call | solution.py:247
  239.9 11.6 %all-to-all-start.2 = ((bf16[64,2,128,128]{3,2,1,0:T(8,128)(2,1)}), bf16[64,2,128,128]{3,2,1,0:T(8,128)(2,1)}, u32[]{:S(2)}, u32[]{:S(2)}) async-start(bf16[64,2,128,128]{3,2,1,0:T(8,128)(2,1)} %get-tuple-element.14), calls=%async_computation.2 | async-start | bytes 8388608 | tf_op jit(solution)/shard_map/all_to_all | solution.py:326
  251.5 1.4 collective-permute-start.22
  253.0 100.3 %collective-permute-done.22 = f32[2,2,128,128]{3,2,1,0:T(8,128)S(1)} collective-permute-done((f32[2,2,128,128]{3,2,1,0:T(8,128)S(1)}, f32[2,2,128,128]{3,2,1,0:T(8,128)S(1)}, u32[]{:S(2)}, u32[]{:S(2)}) %collective-permute-start.22) | collective-permute-done | bytes 262176 | tf_op jit(solution)/shard_map/ppermute | solution.py:357
  354.6 17.9 %collective-permute-done.23 = f32[2,2,128,128]{3,2,1,0:T(8,128)S(1)} collective-permute-done((f32[2,2,128,128]{3,2,1,0:T(8,128)S(1)}, f32[2,2,128,128]{3,2,1,0:T(8,128)S(1)}, u32[]{:S(2)}, u32[]{:S(2)}) %collective-permute-start.23) | collective-permute-done | bytes 262176 | tf_op jit(solution)/shard_map/ppermute | solution.py:357
  372.5 1.3 collective-permute-start.24
  373.8 7.9 %collective-permute-done.24 = f32[2,2,128,128]{3,2,1,0:T(8,128)S(1)} collective-permute-done((f32[2,2,128,128]{3,2,1,0:T(8,128)S(1)}, f32[2,2,128,128]{3,2,1,0:T(8,128)S(1)}, u32[]{:S(2)}, u32[]{:S(2)}) %collective-permute-start.24) | collective-permute-done | bytes 262176 | tf_op jit(solution)/shard_map/ppermute | solution.py:357
  381.7 1.3 collective-permute-start.25
  383.1 2.1 collective-permute-start.18
  386.3 5.1 %collective-permute-done.25 = f32[2,2,128,128]{3,2,1,0:T(8,128)S(1)} collective-permute-done((f32[2,2,128,128]{3,2,1,0:T(8,128)S(1)}, f32[2,2,128,128]{3,2,1,0:T(8,128)S(1)}, u32[]{:S(2)}, u32[]{:S(2)}) %collective-permute-start.25) | collective-permute-done | bytes 262176 | tf_op jit(solution)/shard_map/ppermute | solution.py:357
  391.5 2.5 collective-permute-start.26
  394.0 3.9 collective-permute-done.26
  398.7 1.9 collective-permute-start.21
  400.6 5.7 %collective-permute-start.20 = (bf16[1,2,128,128]{3,2,1,0:T(8,128)(2,1)S(1)}, bf16[1,2,128,128]{3,2,1,0:T(8,128)(2,1)S(1)}, u32[]{:S(2)}, u32[]{:S(2)}) collective-permute-start(bf16[1,2,128,128]{3,2,1,0:T(8,128)(2,1)S(1)} %get-tuple-element.43), channel_id=1, source_target_pairs={{4,0},{8,4},{12,8},{16,12},{20,16},{24,20},{28,24},{32,28},{36,32}... | collective-permute-start | bytes 196616 | tf_op jit(solution)/shard_map/ppermute | solution.py:395
  406.4 4.1 collective-permute-done.17
  412.2 4.1 join.1
  416.3 5.5 %collect.1 = bf16[9,2,128,128]{3,2,1,0:T(8,128)(2,1)S(1)} custom-call(s32[93]{0:T(128)S(1)} %pad_add_fusion.meta, bf16[64,2,128,128]{3,2,1,0:T(8,128)(2,1)} %all-to-all-done.2.got, f32[11,2,128,128]{3,2,1,0:T(8,128)S(1)} %copy-done, bf16[1,2,128,128]{3,2,1,0:T(8,128)(2,1)S(1)} %collective-permute-done.20.lower, ...), custom_call_target="tpu_custom_call" | custom-call | tf_op jit(solution)/shard_map/collect/pallas_call | solution.py:290
  421.9 13.0 %all_to_all.20 = bf16[4,2,288,128]{3,2,1,0:T(8,128)(2,1)S(1)} all-to-all(bf16[4,2,288,128]{3,2,1,0:T(8,128)(2,1)S(1)} %copy.77), channel_id=1, replica_groups=mesh['z'=8,'x'=4,'c'=2,'head'=4] {'head'}, dimensions={0} | all-to-all | bytes 1179648 | tf_op jit(solution)/shard_map/all_to_all | solution.py:326
  (111 shorter events, 23.3 us)
Async XLA Ops:
  0.6 6.5 %copy-start.20 = (s32[576,3]{0,1:T(4,128)S(1)}, s32[576,3]{0,1:T(4,128)}, u32[]{:S(2)}) copy-start(s32[576,3]{0,1:T(4,128)} %param.15) | copy-start | bytes 20740
  0.6 6.5 %copy-start.21 = (s32[576,3]{0,1:T(4,128)S(1)}, s32[576,3]{0,1:T(4,128)}, u32[]{:S(2)}) copy-start(s32[576,3]{0,1:T(4,128)} %param.14) | copy-start | bytes 20740
  2.7 14.6 %all-to-all-start = ((bf16[4,2,288,128]{3,2,1,0:T(8,128)(2,1)}), bf16[4,2,288,128]{3,2,1,0:T(8,128)(2,1)S(1)}, u32[]{:S(2)}, u32[]{:S(2)}) async-start(bf16[4,2,288,128]{3,2,1,0:T(8,128)(2,1)} %maximum_bitcast_fusion), calls=%async_computation | async-start | bytes 1179648 | tf_op jit(solution)/shard_map/all_to_all | solution.py:326
  21.6 13.2 %copy-start.11 = (bf16[288,32,128]{2,1,0:T(8,128)(2,1)S(1)}, bf16[288,32,128]{2,1,0:T(8,128)(2,1)}, u32[]{:S(2)}) copy-start(bf16[288,32,128]{2,1,0:T(8,128)(2,1)} %param.12) | copy-start | bytes 7077892
  21.6 198.2 %all-to-all-start.1 = ((bf16[64,2,128,128]{3,2,1,0:T(8,128)(2,1)}), bf16[64,2,128,128]{3,2,1,0:T(8,128)(2,1)}, u32[]{:S(2)}, u32[]{:S(2)}) async-start(bf16[64,2,128,128]{3,2,1,0:T(8,128)(2,1)} %select.11), calls=%async_computation.1 | async-start | bytes 8388608 | tf_op jit(solution)/shard_map/all_to_all | solution.py:326
  34.0 5.5 %copy-start.16 = (f32[288,32]{0,1:T(8,128)S(1)}, f32[288,32]{0,1:T(8,128)}, u32[]{:S(2)}) copy-start(f32[288,32]{0,1:T(8,128)} %param.13) | copy-start | bytes 110596
  34.0 4.2 collective-permute-start.11
  38.2 10.8 %collective-permute-start.12 = (bf16[2,2,128,128]{3,2,1,0:T(8,128)(2,1)S(1)}, bf16[2,2,128,128]{3,2,1,0:T(8,128)(2,1)S(1)}, u32[]{:S(2)}, u32[]{:S(2)}) collective-permute-start(bf16[2,2,128,128]{3,2,1,0:T(8,128)(2,1)S(1)} %broadcast_select_fusion), channel_id=1, source_target_pairs={{0,8},{4,12},{1,9},{5,13},{2,10},{6,14},{3,11},{7,15}} | collective-permute-start | bytes 393224 | tf_op jit(solution)/shard_map/ppermute | solution.py:348
  49.0 6.4 %collective-permute-start.13 = (bf16[2,2,128,128]{3,2,1,0:T(8,128)(2,1)S(1)}, bf16[2,2,128,128]{3,2,1,0:T(8,128)(2,1)S(1)}, u32[]{:S(2)}, u32[]{:S(2)}) collective-permute-start(bf16[2,2,128,128]{3,2,1,0:T(8,128)(2,1)S(1)} %broadcast_select_fusion.1), channel_id=1, source_target_pairs={{0,16},{4,20},{8,24},{12,28},{1,17},{5,21},{9,25},{13,29},{2,18},{... | collective-permute-start | bytes 393224 | tf_op jit(solution)/shard_map/ppermute | solution.py:348
  51.9 81.4 %collective-permute-start.8 = (f32[2,18,128]{2,1,0:T(8,128)S(1)}, f32[2,18,128]{2,1,0:T(8,128)S(1)}, u32[]{:S(2)}, u32[]{:S(2)}) collective-permute-start(f32[2,18,128]{2,1,0:T(8,128)S(1)} %get-tuple-element.49), channel_id=1, source_target_pairs={{0,3},{1,0},{2,1},{3,2},{4,7},{5,4},{6,5},{7,6},{8,11},{9,8},{10,9... | collective-permute-start | bytes 55304 | tf_op jit(solution)/shard_map/ppermute | solution.py:330
  53.1 83.9 %collective-permute-start.7 = (f32[2,18,128]{2,1,0:T(8,128)S(1)}, f32[2,18,128]{2,1,0:T(8,128)S(1)}, u32[]{:S(2)}, u32[]{:S(2)}) collective-permute-start(f32[2,18,128]{2,1,0:T(8,128)S(1)} %get-tuple-element.50), channel_id=1, source_target_pairs={{0,2},{1,3},{2,0},{3,1},{4,6},{5,7},{6,4},{7,5},{8,10},{9,11},{10,... | collective-permute-start | bytes 55304 | tf_op jit(solution)/shard_map/ppermute | solution.py:330
  54.6 87.3 %collective-permute-start.6 = (f32[2,18,128]{2,1,0:T(8,128)S(1)}, f32[2,18,128]{2,1,0:T(8,128)S(1)}, u32[]{:S(2)}, u32[]{:S(2)}) collective-permute-start(f32[2,18,128]{2,1,0:T(8,128)S(1)} %get-tuple-element.51), channel_id=1, source_target_pairs={{0,1},{1,2},{2,3},{3,0},{4,5},{5,6},{6,7},{7,4},{8,9},{9,10},{10,1... | collective-permute-start | bytes 55304 | tf_op jit(solution)/shard_map/ppermute | solution.py:330
  55.5 71.4 %collective-permute-start.14 = (bf16[2,2,128,128]{3,2,1,0:T(8,128)(2,1)S(1)}, bf16[2,2,128,128]{3,2,1,0:T(8,128)(2,1)S(1)}, u32[]{:S(2)}, u32[]{:S(2)}) collective-permute-start(bf16[2,2,128,128]{3,2,1,0:T(8,128)(2,1)S(1)} %broadcast_select_fusion.2), channel_id=1, source_target_pairs={{0,32},{4,36},{8,40},{12,44},{16,48},{20,52},{24,56},{28,60},{1,33... | collective-permute-start | bytes 393224 | tf_op jit(solution)/shard_map/ppermute | solution.py:348
  59.7 87.2 %collective-permute-start.2 = (bf16[2304,128]{1,0:T(8,128)(2,1)}, bf16[2304,128]{1,0:T(8,128)(2,1)S(1)}, u32[]{:S(2)}, u32[]{:S(2)}) collective-permute-start(bf16[2304,128]{1,0:T(8,128)(2,1)} %get-tuple-element.38), channel_id=1, source_target_pairs={{0,3},{1,0},{2,1},{3,2},{4,7},{5,4},{6,5},{7,6},{8,11},{9,8},{10,9... | collective-permute-start | bytes 1769480 | tf_op jit(solution)/shard_map/ppermute | solution.py:330
  126.9 3.8 collective-permute-start.15
  130.7 12.3 %collective-permute-start.9 = (bf16[1,2,128,128]{3,2,1,0:T(8,128)(2,1)S(1)}, bf16[1,2,128,128]{3,2,1,0:T(8,128)(2,1)S(1)}, u32[]{:S(2)}, u32[]{:S(2)}) collective-permute-start(bf16[1,2,128,128]{3,2,1,0:T(8,128)(2,1)S(1)} %get-tuple-element.46), channel_id=1, source_target_pairs={{0,4},{4,8},{8,12},{12,16},{16,20},{20,24},{24,28},{28,32},{32,36}... | collective-permute-start | bytes 196616 | tf_op jit(solution)/shard_map/ppermute | solution.py:379
  133.3 5.6 %copy-start.17 = (f32[2,18,128]{2,1,0:T(8,128)}, f32[2,18,128]{2,1,0:T(8,128)S(1)}, u32[]{:S(2)}) copy-start(f32[2,18,128]{2,1,0:T(8,128)S(1)} %collective-permute-done.8) | copy-start | bytes 55300
  133.3 11.8 %collective-permute-start.10 = (bf16[1,2,128,128]{3,2,1,0:T(8,128)(2,1)}, bf16[1,2,128,128]{3,2,1,0:T(8,128)(2,1)}, u32[]{:S(2)}, u32[]{:S(2)}) collective-permute-start(bf16[1,2,128,128]{3,2,1,0:T(8,128)(2,1)} %get-tuple-element.47), channel_id=1, source_target_pairs={{4,0},{8,4},{12,8},{16,12},{20,16},{24,20},{28,24},{32,28},{36,32}... | collective-permute-start | bytes 196616 | tf_op jit(solution)/shard_map/ppermute | solution.py:380
  137.0 2.0 copy-start.18
  137.0 11.7 %collective-permute-start.16 = (bf16[2,2,128,128]{3,2,1,0:T(8,128)(2,1)}, bf16[2,2,128,128]{3,2,1,0:T(8,128)(2,1)}, u32[]{:S(2)}, u32[]{:S(2)}) collective-permute-start(bf16[2,2,128,128]{3,2,1,0:T(8,128)(2,1)} %broadcast_select_fusion.4), channel_id=1, source_target_pairs={{0,128},{4,132},{8,136},{12,140},{16,144},{20,148},{24,152},{28,15... | collective-permute-start | bytes 393224 | tf_op jit(solution)/shard_map/ppermute | solution.py:348
  141.8 77.2 %copy-start.1 = (bf16[2304,128]{1,0:T(8,128)(2,1)}, bf16[2304,128]{1,0:T(8,128)(2,1)S(1)}, u32[]{:S(2)}) copy-start(bf16[2304,128]{1,0:T(8,128)(2,1)S(1)} %get-tuple-element.37.d0) | copy-start | bytes 1769476
  142.5 18.0 %collective-permute-start.1 = (bf16[2304,128]{1,0:T(8,128)(2,1)}, bf16[2304,128]{1,0:T(8,128)(2,1)S(1)}, u32[]{:S(2)}, u32[]{:S(2)}) collective-permute-start(bf16[2304,128]{1,0:T(8,128)(2,1)} %get-tuple-element.39), channel_id=1, source_target_pairs={{0,2},{1,3},{2,0},{3,1},{4,6},{5,7},{6,4},{7,5},{8,10},{9,11},{10,... | collective-permute-start | bytes 1769480 | tf_op jit(solution)/shard_map/ppermute | solution.py:330
  143.7 29.5 %collective-permute-start = (bf16[2304,128]{1,0:T(8,128)(2,1)}, bf16[2304,128]{1,0:T(8,128)(2,1)S(1)}, u32[]{:S(2)}, u32[]{:S(2)}) collective-permute-start(bf16[2304,128]{1,0:T(8,128)(2,1)} %get-tuple-element.40), channel_id=1, source_target_pairs={{0,1},{1,2},{2,3},{3,0},{4,5},{5,6},{6,7},{7,4},{8,9},{9,10},{10,1... | collective-permute-start | bytes 1769480 | tf_op jit(solution)/shard_map/ppermute | solution.py:330
  145.1 28.0 %collective-permute-start.5 = (bf16[2304,128]{1,0:T(8,128)(2,1)}, bf16[2304,128]{1,0:T(8,128)(2,1)}, u32[]{:S(2)}, u32[]{:S(2)}) collective-permute-start(bf16[2304,128]{1,0:T(8,128)(2,1)} %get-tuple-element.34), channel_id=1, source_target_pairs={{0,3},{1,0},{2,1},{3,2},{4,7},{5,4},{6,5},{7,6},{8,11},{9,8},{10,9... | collective-permute-start | bytes 1769480 | tf_op jit(solution)/shard_map/ppermute | solution.py:330
  146.9 72.2 %copy-start.2 = (bf16[2304,128]{1,0:T(8,128)(2,1)}, bf16[2304,128]{1,0:T(8,128)(2,1)S(1)}, u32[]{:S(2)}) copy-start(bf16[2304,128]{1,0:T(8,128)(2,1)S(1)} %collective-permute-done.2.q3) | copy-start | bytes 1769476
  146.9 39.0 %collective-permute-start.4 = (bf16[2304,128]{1,0:T(8,128)(2,1)}, bf16[2304,128]{1,0:T(8,128)(2,1)}, u32[]{:S(2)}, u32[]{:S(2)}) collective-permute-start(bf16[2304,128]{1,0:T(8,128)(2,1)} %get-tuple-element.35), channel_id=1, source_target_pairs={{0,2},{1,3},{2,0},{3,1},{4,6},{5,7},{6,4},{7,5},{8,10},{9,11},{10,... | collective-permute-start | bytes 1769480 | tf_op jit(solution)/shard_map/ppermute | solution.py:330
  148.7 48.6 %collective-permute-start.3 = (bf16[2304,128]{1,0:T(8,128)(2,1)}, bf16[2304,128]{1,0:T(8,128)(2,1)}, u32[]{:S(2)}, u32[]{:S(2)}) collective-permute-start(bf16[2304,128]{1,0:T(8,128)(2,1)} %get-tuple-element.36), channel_id=1, source_target_pairs={{0,1},{1,2},{2,3},{3,0},{4,5},{5,6},{6,7},{7,4},{8,9},{9,10},{10,1... | collective-permute-start | bytes 1769480 | tf_op jit(solution)/shard_map/ppermute | solution.py:330
  153.2 44.1 %copy-start.4 = (f32[2,9,8,128]{3,2,1,0:T(8,128)}, f32[2,9,8,128]{3,2,1,0:T(8,128)S(1)}, u32[]{:S(2)}) copy-start(f32[2,9,8,128]{3,2,1,0:T(8,128)S(1)} %copy.75.ld_ref) | copy-start | bytes 221188
  160.5 58.6 %copy-start.3 = (bf16[2304,128]{1,0:T(8,128)(2,1)}, bf16[2304,128]{1,0:T(8,128)(2,1)S(1)}, u32[]{:S(2)}) copy-start(bf16[2304,128]{1,0:T(8,128)(2,1)S(1)} %collective-permute-done.1.q2) | copy-start | bytes 1769476
  219.8 0.9 copy-start.5
  238.2 0.8 copy-start.6
  239.9 11.7 %copy-start.8 = (f32[2,2,128,128]{3,2,1,0:T(8,128)S(1)}, f32[2,2,128,128]{3,2,1,0:T(8,128)}, u32[]{:S(2)}) copy-start(f32[2,2,128,128]{3,2,1,0:T(8,128)} %copy-done.7) | copy-start | bytes 786436
  239.9 176.5 %all-to-all-start.2 = ((bf16[64,2,128,128]{3,2,1,0:T(8,128)(2,1)}), bf16[64,2,128,128]{3,2,1,0:T(8,128)(2,1)}, u32[]{:S(2)}, u32[]{:S(2)}) async-start(bf16[64,2,128,128]{3,2,1,0:T(8,128)(2,1)} %get-tuple-element.14), calls=%async_computation.2 | async-start | bytes 8388608 | tf_op jit(solution)/shard_map/all_to_all | solution.py:326
  251.5 131.6 %copy-start.10 = (bf16[2304,128]{1,0:T(8,128)(2,1)S(1)}, bf16[2304,128]{1,0:T(8,128)(2,1)}, u32[]{:S(2)}) copy-start(bf16[2304,128]{1,0:T(8,128)(2,1)} %copy-done.9) | copy-start | bytes 1769476
  251.5 147.1 %copy-start = (f32[11,2,128,128]{3,2,1,0:T(8,128)S(1)}, f32[11,2,128,128]{3,2,1,0:T(8,128)}, u32[]{:S(2)}) copy-start(f32[11,2,128,128]{3,2,1,0:T(8,128)} %get-tuple-element.21.ext) | copy-start | bytes 4325380
  251.5 101.7 %collective-permute-start.22 = (f32[2,2,128,128]{3,2,1,0:T(8,128)S(1)}, f32[2,2,128,128]{3,2,1,0:T(8,128)S(1)}, u32[]{:S(2)}, u32[]{:S(2)}) collective-permute-start(f32[2,2,128,128]{3,2,1,0:T(8,128)S(1)} %copy-done.8), channel_id=1, source_target_pairs={{128,0},{132,4},{136,8},{140,12},{144,16},{148,20},{152,24},{156,2... | collective-permute-start | bytes 786440 | tf_op jit(solution)/shard_map/ppermute | solution.py:357
  353.3 19.2 %collective-permute-start.23 = (f32[2,2,128,128]{3,2,1,0:T(8,128)S(1)}, f32[2,2,128,128]{3,2,1,0:T(8,128)S(1)}, u32[]{:S(2)}, u32[]{:S(2)}) collective-permute-start(f32[2,2,128,128]{3,2,1,0:T(8,128)S(1)} %add.89), channel_id=1, source_target_pairs={{64,0},{68,4},{72,8},{76,12},{80,16},{84,20},{88,24},{92,28},{96,3... | collective-permute-start | bytes 786440 | tf_op jit(solution)/shard_map/ppermute | solution.py:357
  372.5 9.2 %collective-permute-start.24 = (f32[2,2,128,128]{3,2,1,0:T(8,128)S(1)}, f32[2,2,128,128]{3,2,1,0:T(8,128)S(1)}, u32[]{:S(2)}, u32[]{:S(2)}) collective-permute-start(f32[2,2,128,128]{3,2,1,0:T(8,128)S(1)} %add.90), channel_id=1, source_target_pairs={{32,0},{36,4},{40,8},{44,12},{48,16},{52,20},{56,24},{60,28},{33,1... | collective-permute-start | bytes 786440 | tf_op jit(solution)/shard_map/ppermute | solution.py:357
  381.7 9.8 %collective-permute-start.25 = (f32[2,2,128,128]{3,2,1,0:T(8,128)S(1)}, f32[2,2,128,128]{3,2,1,0:T(8,128)S(1)}, u32[]{:S(2)}, u32[]{:S(2)}) collective-permute-start(f32[2,2,128,128]{3,2,1,0:T(8,128)S(1)} %add.91), channel_id=1, source_target_pairs={{16,0},{20,4},{24,8},{28,12},{17,1},{21,5},{25,9},{29,13},{18,2},{... | collective-permute-start | bytes 786440 | tf_op jit(solution)/shard_map/ppermute | solution.py:357
  383.0 27.5 %collective-permute-start.17 = (bf16[2304,128]{1,0:T(8,128)(2,1)}, bf16[2304,128]{1,0:T(8,128)(2,1)S(1)}, u32[]{:S(2)}, u32[]{:S(2)}) collective-permute-start(bf16[2304,128]{1,0:T(8,128)(2,1)} %get-tuple-element.16), channel_id=1, source_target_pairs={{0,1},{1,2},{2,3},{3,0},{4,5},{5,6},{6,7},{7,4},{8,9},{9,10},{10,1... | collective-permute-start | bytes 1769480 | tf_op jit(solution)/shard_map/ppermute | solution.py:330
  383.1 27.4 %collective-permute-start.18 = (bf16[2304,128]{1,0:T(8,128)(2,1)S(1)}, bf16[2304,128]{1,0:T(8,128)(2,1)S(1)}, u32[]{:S(2)}, u32[]{:S(2)}) collective-permute-start(bf16[2304,128]{1,0:T(8,128)(2,1)S(1)} %copy-done.10), channel_id=1, source_target_pairs={{0,2},{1,3},{2,0},{3,1},{4,6},{5,7},{6,4},{7,5},{8,10},{9,11},{10,... | collective-permute-start | bytes 1769480 | tf_op jit(solution)/shard_map/ppermute | solution.py:330
  385.2 25.7 %collective-permute-start.19 = (bf16[2304,128]{1,0:T(8,128)(2,1)S(1)}, bf16[2304,128]{1,0:T(8,128)(2,1)S(1)}, u32[]{:S(2)}, u32[]{:S(2)}) collective-permute-start(bf16[2304,128]{1,0:T(8,128)(2,1)S(1)} %get-tuple-element.18), channel_id=1, source_target_pairs={{0,3},{1,0},{2,1},{3,2},{4,7},{5,4},{6,5},{7,6},{8,11},{9,8},{10,9... | collective-permute-start | bytes 1769480 | tf_op jit(solution)/shard_map/ppermute | solution.py:330
  391.5 6.3 %collective-permute-start.26 = (f32[2,2,128,128]{3,2,1,0:T(8,128)S(1)}, f32[2,2,128,128]{3,2,1,0:T(8,128)S(1)}, u32[]{:S(2)}, u32[]{:S(2)}) collective-permute-start(f32[2,2,128,128]{3,2,1,0:T(8,128)S(1)} %add.92), channel_id=1, source_target_pairs={{8,0},{12,4},{9,1},{13,5},{10,2},{14,6},{11,3},{15,7}} | collective-permute-start | bytes 786440 | tf_op jit(solution)/shard_map/ppermute | solution.py:357
  397.9 2.8 collective-permute-start.27
  398.7 17.6 %collective-permute-start.21 = (bf16[1,2,128,128]{3,2,1,0:T(8,128)(2,1)S(1)}, bf16[1,2,128,128]{3,2,1,0:T(8,128)(2,1)S(1)}, u32[]{:S(2)}, u32[]{:S(2)}) collective-permute-start(bf16[1,2,128,128]{3,2,1,0:T(8,128)(2,1)S(1)} %get-tuple-element.42), channel_id=1, source_target_pairs={{0,4},{4,8},{8,12},{12,16},{16,20},{20,24},{24,28},{28,32},{32,36}... | collective-permute-start | bytes 196616 | tf_op jit(solution)/shard_map/ppermute | solution.py:396
  400.6 15.7 %collective-permute-start.20 = (bf16[1,2,128,128]{3,2,1,0:T(8,128)(2,1)S(1)}, bf16[1,2,128,128]{3,2,1,0:T(8,128)(2,1)S(1)}, u32[]{:S(2)}, u32[]{:S(2)}) collective-permute-start(bf16[1,2,128,128]{3,2,1,0:T(8,128)(2,1)S(1)} %get-tuple-element.43), channel_id=1, source_target_pairs={{4,0},{8,4},{12,8},{16,12},{20,16},{24,20},{28,24},{32,28},{36,32}... | collective-permute-start | bytes 196616 | tf_op jit(solution)/shard_map/ppermute | solution.py:395
  410.5 1.7 copy-start.12
  410.5 0.9 copy-start.13
  (5 other events, 3.6 us)

commit v3 on v2

--- a/solution.py
+++ b/solution.py
@@ -14,7 +14,8 @@
 RND = 3
 NZ, NX, NC, NH = 8, 4, 2, 4
 SEQ = ("z", "x", "c")
-NSEQ = NZ * NX * NC
+NXC = NX * NC
+NSEQ = NZ * NXC
 QB = 9
 NB = NSEQ * QB
 HL = 8
@@ -71,8 +72,8 @@
 
 
 def near_kernel(
-    meta, q0, q1, q2, q3, d0, d1, d2, d3, ld_ref, kv_ref, gl_ref,
-    dqt_ref, dkv_ref, dg_ref, q_scr, do_scr, key_scr, p_scr, ds_scr, sems,
+    meta, q0, q1, q2, q3, d0, d1, d2, d3, ld_ref, kv_ref, gl_ref, dqt_ref,
+    dq0, dq1, dq2, dq3, dkv_ref, dg_ref, q_scr, do_scr, dq_scr, key_scr, p_scr, ds_scr, sems, dq_sems,
 ):
     b = pl.program_id(0)
 
@@ -83,8 +84,8 @@
         dg_ref[...] = jnp.zeros_like(dg_ref)
 
     block = meta[AT_SEQ] * QB + b
-    keys = [gl_ref[0, 0], gl_ref[1, 0]] + [kv_ref[b + w, 0] for w in range(3)]
-    values = [gl_ref[0, 1], gl_ref[1, 1]] + [kv_ref[b + w, 1] for w in range(3)]
+    keys = [gl_ref[0], gl_ref[1]] + [kv_ref[b + w, 0] for w in range(3)]
+    values = [gl_ref[G], gl_ref[G + 1]] + [kv_ref[b + w, 1] for w in range(3)]
     biases = [0.0, 0.0]
     for w in range(3):
         c = block + (w - 1)
@@ -94,7 +95,7 @@
     dk, dv, dqt = pair_grads(
         keys, values, biases, q_scr[rows, :], do_scr[rows, :], lse2, delta, key_scr, p_scr, ds_scr
     )
-    dqt_ref[0] = dqt
+    dq_scr[rows, :] = ((dqt + dqt_ref[0]).T * SCALE).astype(BF)
     for t in range(G):
         dg_ref[t, 0] += dk[t * BLK : (t + 1) * BLK]
         dg_ref[t, 1] += dv[t * BLK : (t + 1) * BLK]
@@ -103,11 +104,23 @@
         dkv_ref[b + w, 0] += dk[t * BLK : (t + 1) * BLK]
         dkv_ref[b + w, 1] += dv[t * BLK : (t + 1) * BLK]
 
+    @pl.when(b == QB - 1)
+    def _():
+        copies = []
+        for k, target in enumerate((dq0, dq1, dq2, dq3)):
+            row = pl.multiple_of(((meta[AT_HEAD] + k) & (NH - 1)) * PART, PART)
+            copies.append(
+                pltpu.make_async_copy(dq_scr.at[pl.ds(row, PART)], target, dq_sems.at[k])
+            )
+        for c in copies:
+            c.start()
+        for c in copies:
+            c.wait()
+
 
 def random_kernel(
-    meta, q0, q1, q2, q3, d0, d1, d2, d3, ld_ref, got_ref, dqt_ref,
-    dq0, dq1, dq2, dq3, dkv_ref,
-    q_scr, do_scr, dq_scr, kv_scr, out_scr, key_scr, p_scr, ds_scr, sems, in_sems, out_sems, dq_sems,
+    meta, q0, q1, q2, q3, d0, d1, d2, d3, ld_ref, got_ref,
+    dqt_ref, dkv_ref, q_scr, do_scr, kv_scr, out_scr, key_scr, p_scr, ds_scr, sems, in_sems, out_sems,
 ):
     b = pl.program_id(0)
 
@@ -138,7 +151,7 @@
         [kv_scr[first + j, 1] for j in range(RND)],
         biases, q_scr[rows, :], do_scr[rows, :], lse2, delta, key_scr, p_scr, ds_scr,
     )
-    dq_scr[rows, :] = ((dqt + dqt_ref[0]).T * SCALE).astype(BF)
+    dqt_ref[0] = dqt
     for j in range(RND):
         n = first + j
         out_scr[n, 0] = dk[j * BLK : (j + 1) * BLK].astype(BF)
@@ -147,16 +160,6 @@
 
     @pl.when(b == QB - 1)
     def _():
-        copies = []
-        for k, target in enumerate((dq0, dq1, dq2, dq3)):
-            row = pl.multiple_of(((meta[AT_HEAD] + k) & (NH - 1)) * PART, PART)
-            copies.append(
-                pltpu.make_async_copy(dq_scr.at[pl.ds(row, PART)], target, dq_sems.at[k])
-            )
-        for c in copies:
-            c.start()
-        for c in copies:
-            c.wait()
         for e in range(ENT):
             give(e).wait()
 
@@ -221,51 +224,52 @@
 DQT = pl.BlockSpec((1, HD, ROWS), lambda b, m: (b, 0, 0))
 
 
-def call_near(meta, q, do, ld, kvx, gl):
+def call_near(meta, q, do, ld, kvx, gl, dqt):
     return pl.pallas_call(
         near_kernel,
         grid_spec=pltpu.PrefetchScalarGridSpec(
             num_scalar_prefetch=1,
             grid=(QB,),
-            in_specs=anywhere(2 * NH) + [ROW_PAIR, full(QB + 2, *TILE), full(G, *TILE)],
-            out_specs=[DQT, full(QB + 2, *TILE), full(G, *TILE)],
-            scratch_shapes=[pltpu.VMEM((QB * ROWS, HD), BF)] * 2
+            in_specs=anywhere(2 * NH) + [ROW_PAIR, full(QB + 2, *TILE), full(2 * G, BLK, HD), DQT],
+            out_specs=anywhere(NH) + [full(QB + 2, *TILE), full(G, *TILE)],
+            scratch_shapes=[pltpu.VMEM((QB * ROWS, HD), BF)] * 3
             + work_scratch(G + 3)
-            + [pltpu.SemaphoreType.DMA((2, NH))],
+            + [pltpu.SemaphoreType.DMA((2, NH)), pltpu.SemaphoreType.DMA((NH,))],
         ),
-        out_shape=[
-            jax.ShapeDtypeStruct((QB, HD, ROWS), F32),
+        out_shape=[jax.ShapeDtypeStruct((PART, HD), BF)] * NH
+        + [
             jax.ShapeDtypeStruct((QB + 2, *TILE), F32),
             jax.ShapeDtypeStruct((G, *TILE), F32),
         ],
         compiler_params=PARAMS,
         name="near",
-    )(meta, *q, *do, ld, kvx, gl)
-
-
-def call_random(meta, q, do, ld, got, dqt):
+    )(meta, *q, *do, ld, kvx, gl, dqt)
+
+
+def call_random(meta, q, do, ld, got):
     return pl.pallas_call(
         random_kernel,
         grid_spec=pltpu.PrefetchScalarGridSpec(
             num_scalar_prefetch=1,
             grid=(QB,),
-            in_specs=anywhere(2 * NH) + [ROW_PAIR] + anywhere(1) + [DQT],
-            out_specs=anywhere(NH + 1),
-            scratch_shapes=[pltpu.VMEM((QB * ROWS, HD), BF)] * 3
+            in_specs=anywhere(2 * NH) + [ROW_PAIR] + anywhere(1),
+            out_specs=[DQT] + anywhere(1),
+            scratch_shapes=[pltpu.VMEM((QB * ROWS, HD), BF)] * 2
             + [pltpu.VMEM((ENT, *TILE), BF)] * 2
             + work_scratch(RND)
             + [
                 pltpu.SemaphoreType.DMA((2, NH)),
                 pltpu.SemaphoreType.DMA((ENT,)),
                 pltpu.SemaphoreType.DMA((ENT,)),
-                pltpu.SemaphoreType.DMA((NH,)),
             ],
         ),
-        out_shape=[jax.ShapeDtypeStruct((PART, HD), BF)] * NH
-        + [jax.ShapeDtypeStruct((NSEQ, *TILE), BF)],
+        out_shape=[
+            jax.ShapeDtypeStruct((QB, HD, ROWS), F32),
+            jax.ShapeDtypeStruct((NSEQ, *TILE), BF),
+        ],
         compiler_params=PARAMS,
         name="random",
-    )(meta, *q, *do, ld, got, dqt)
+    )(meta, *q, *do, ld, got)
 
 
 STEP_TILES = pl.BlockSpec((STEP, *TILE), lambda b, m: (b, 0, 0, 0))
@@ -344,17 +348,17 @@
 
 def spread(value, index):
     k = 1
-    while k < NSEQ:
-        got = lax.ppermute(value, SEQ, [(i, i + k) for i in range(k)])
+    while k < NXC:
+        got = lax.ppermute(value, ("x", "c"), [(i, i + k) for i in range(k)])
         value = jnp.where((index >= k) & (index < 2 * k), got, value)
         k *= 2
     return value
 
 
 def gather_sum(value):
-    k = NSEQ // 2
+    k = NXC // 2
     while k:
-        value = value + lax.ppermute(value, SEQ, [(i + k, i) for i in range(k)])
+        value = value + lax.ppermute(value, ("x", "c"), [(i + k, i) for i in range(k)])
         k //= 2
     return value
 
@@ -366,36 +370,49 @@
     want = jnp.max(jnp.where(named >> 4 == seq, named & 15, -1), axis=1)
     meta = jnp.concatenate([mine, jnp.stack([seq, head]).astype(jnp.int32), want])
 
-    kv = jnp.stack([k, v]).transpose(2, 0, 1, 3)
-    kv = plain_a2a(kv, "head")
+    z, xc = lax.axis_index("z"), lax.axis_index(("x", "c"))
+    up = [(i, i + 1) for i in range(NSEQ - 1)]
+    down = [(i + 1, i) for i in range(NSEQ - 1)]
+    kvs = jnp.stack([k, v]).transpose(2, 0, 1, 3)
+    kv, meta = tie(plain_a2a(kvs, "head"), meta)
     kv = kv.transpose(1, 0, 2, 3).reshape(2, QB, BLK, HD).transpose(1, 0, 2, 3)
     got = plain_a2a(call_select(meta, kv), SEQ)
 
-    up = [(i, i + 1) for i in range(NSEQ - 1)]
-    down = [(i + 1, i) for i in range(NSEQ - 1)]
     qp, dop = head_parts(q, head), head_parts(do, head)
     ql = [turn(p, i) for i, p in enumerate(qp)]
     dol = [turn(p, i) for i, p in enumerate(dop)]
-    before = lax.ppermute(kv[QB - 1 :], SEQ, up)
-    after = lax.ppermute(kv[:1], SEQ, down)
-    kvx = jnp.concatenate([before, kv, after])
-    gl = spread(kv[:G], seq)
     delta = jnp.sum(do.astype(F32) * o.astype(F32), axis=-1)
     ld = jnp.stack([lse * LOG2E, delta]).reshape(2, TOK, NH, HL).transpose(2, 0, 1, 3)
     ld = ld.reshape(NH, 2, PART // BLK, BLK)
-    ld = jnp.stack([turn(lax.dynamic_index_in_dim(ld, lax.rem(head + i, NH), 0, keepdims=False), i) for i in range(NH)])
+    ld = jnp.stack(
+        [turn(lax.dynamic_index_in_dim(ld, lax.rem(head + i, NH), 0, keepdims=False), i) for i in range(NH)]
+    )
     ld = jnp.roll(ld[::-1], head + 1, axis=0)
     ld = ld.transpose(1, 0, 2, 3).reshape(2, QB, HL, BLK)
 
-    dqt, dkvx, dg = call_near(meta, ql, dol, ld, kvx, gl)
-    *dq, back = call_random(meta, ql, dol, ld, got, dqt)
-
+    *parts, ld, kv = tie(*ql, *dol, ld, kv)
+    ql, dol = parts[:NH], parts[NH:]
+    gl = jnp.concatenate([kv[:G, 0], kv[:G, 1]])
+    low = [lax.ppermute(gl, "z", [(0, i)]) for i in range(1, 4)]
+    gl = jnp.where(z == 0, gl, low[0] + low[1] + low[2])
+    high = lax.ppermute(gl, "z", [(i, i + 4) for i in range(4)])
+    before = lax.ppermute(kv[QB - 1 :], SEQ, up)
+    after = lax.ppermute(kv[:1], SEQ, down)
+
+    dqt, back = call_random(meta, ql, dol, ld, got)
+    back, before, after, high = tie(back, before, after, high)
     back = plain_a2a(back, SEQ)
-    dq = call_join(head.reshape(1), [turn(p, i) for i, p in enumerate(dq)])
+    gl = spread(jnp.where(z < 4, gl, high), xc)
+    kvx = jnp.concatenate([before, kv, after])
+    *dq, dkvx, dg = call_near(meta, ql, dol, ld, kvx, gl, dqt)
+    dq, dg = tie([turn(p, i) for i, p in enumerate(dq)], gather_sum(dg))
+    dq, dg, dkvx = tie(call_join(head.reshape(1), dq), dg, dkvx)
     lower = lax.ppermute(dkvx[:1].astype(BF), SEQ, down)
     upper = lax.ppermute(dkvx[QB + 1 :].astype(BF), SEQ, up)
-    back, dq = tie(back, dq)
-    total = call_collect(meta, back, dkvx, lower, upper, gather_sum(dg))
+    part = dg.astype(BF)
+    for i in range(1, NZ):
+        dg = dg + lax.ppermute(part, "z", [(i, 0)]).astype(F32)
+    total = call_collect(meta, back, dkvx, lower, upper, dg)
     dkv = total.transpose(1, 0, 2, 3).reshape(2, NH, TOK, HD).transpose(1, 0, 2, 3)
     dkv = plain_a2a(dkv, "head")
     dk = dkv[:, 0].transpose(1, 0, 2)

time: 440 us -> 310 us (0.70)
  waiting for transfers between devices: 267 us -> 128 us
  starting transfers between devices: 72.4 us -> 82.6 us
    ppermute x12 -> x17, waiting for transfers between devices: 212 us -> 81.5 us  [the longest x3 25.9 us: per_device(): low = [lax.ppermute(gl, 'z', [(0, i)]) for i in range(1, 4)]]
    ppermute x12 -> x17, starting transfers between devices: 16.4 us -> 31.6 us  [the longest x3 9.76 us: per_device(): low = [lax.ppermute(gl, 'z', [(0, i)]) for i in range(1, 4)]]
    ppermute x12, waiting for transfers between devices: 45.8 us -> 36.7 us  [turn(): lax.ppermute(value, 'head', [(i, (i + k) % NH) for i in range(NH)])]
  transfers between devices with their start and end apart: 31 -> 36, of which waited for: 16 -> 17; matrix products, arithmetic and copies ran while one was open for 5% -> 7% of each run, Pallas kernels for 6% -> 14%
where the time goes in v3:
time: 310 us; the launch traced here: 307 us
  waiting for transfers between devices  128 us (41%)
  starting transfers between devices  82.6 us (27%)
  Pallas kernels  52.8 us (17%)
  local copies, waits for them, and re-layouts  20.1 us (6%)
  blocking collectives  13.1 us (4%)
  other arithmetic  9.55 us (3%)
    ppermute x12, waiting for transfers between devices, turn(): lax.ppermute(value, 'head', [(i, (i + k) % NH) for i in range(NH)])  36.7 us
    ppermute x3, waiting for transfers between devices, per_device(): low = [lax.ppermute(gl, 'z', [(0, i)]) for i in range(1, 4)]  25.9 us
    all_to_all x3, starting transfers between devices, plain_a2a(): return lax.all_to_all(value, axis, split_axis=0, concat_axis=0, tiled=True)  25.5 us
    pallas_call x1, Pallas kernels, call_near(): pl.pallas_call(near_kernel, grid_spec=pltpu.PrefetchScalarGridSpec(num_sc...  23.3 us
    ppermute x7, waiting for transfers between devices, per_device(): dg = dg + lax.ppermute(part, 'z', [(i, 0)]).astype(F32)  22.1 us
    ppermute x3, waiting for transfers between devices, gather_sum(): lax.ppermute(value, ('x', 'c'), [(i + k, i) for i in range(k)])  18.2 us
    pallas_call x1, Pallas kernels, call_random(): pl.pallas_call(random_kernel, grid_spec=pltpu.PrefetchScalarGridSpec(num_...  15.6 us
    ppermute x12, starting transfers between devices, turn(): lax.ppermute(value, 'head', [(i, (i + k) % NH) for i in range(NH)])  15.5 us
  transfers between devices with their start and end apart: 36, of which 17 were waited for; matrix products, arithmetic and copies ran while one was open for 7% of the time, Pallas kernels for 14%

profile of v3, /device:TPU:2, one launch (start us, length us, event | category | flops | bytes accessed | tf_op | source)
XLA Modules:
  0.0 307.1 jit_solution(395417025143731766)
XLA Ops:
  2.7 4.5 %all-to-all-start = ((bf16[4,2,288,128]{3,2,1,0:T(8,128)(2,1)}), bf16[4,2,288,128]{3,2,1,0:T(8,128)(2,1)S(1)}, u32[]{:S(2)}, u32[]{:S(2)}) async-start(bf16[4,2,288,128]{3,2,1,0:T(8,128)(2,1)} %maximum_bitcast_fusion), calls=%async_computation | async-start | bytes 1179648 | tf_op jit(solution)/shard_map/all_to_all | solution.py:330
  7.8 9.5 %all-to-all-done = bf16[4,2,288,128]{3,2,1,0:T(8,128)(2,1)S(1)} async-done(((bf16[4,2,288,128]{3,2,1,0:T(8,128)(2,1)}), bf16[4,2,288,128]{3,2,1,0:T(8,128)(2,1)S(1)}, u32[]{:S(2)}, u32[]{:S(2)}) %all-to-all-start) | async-done | bytes 589856 | tf_op jit(solution)/shard_map/all_to_all | solution.py:330
  18.2 4.1 %select.11 = bf16[64,2,128,128]{3,2,1,0:T(8,128)(2,1)} custom-call(s32[93]{0:T(128)S(1)} %pad_add_fusion.meta, bf16[9,2,128,128]{3,2,1,0:T(8,128)(2,1)S(1)} %copy.76.kv_ref), custom_call_target="tpu_custom_call" | custom-call | tf_op jit(solution)/shard_map/select/pallas_call | solution.py:279
  22.4 12.5 %all-to-all-start.1 = ((bf16[64,2,128,128]{3,2,1,0:T(8,128)(2,1)}), bf16[64,2,128,128]{3,2,1,0:T(8,128)(2,1)}, u32[]{:S(2)}, u32[]{:S(2)}) async-start(bf16[64,2,128,128]{3,2,1,0:T(8,128)(2,1)} %select.11), calls=%async_computation.1 | async-start | bytes 8388608 | tf_op jit(solution)/shard_map/all_to_all | solution.py:330
  34.9 1.4 dynamic-slice_bitcast_fusion.4
  36.9 2.1 collective-permute-start.1
  39.0 1.3 multiply_reduce_fusion
  42.6 2.9 collective-permute-start.7
  45.5 2.9 dynamic-slice_bitcast_fusion
  48.4 6.1 %collective-permute-done.8 = f32[2,18,128]{2,1,0:T(8,128)S(1)} collective-permute-done((f32[2,18,128]{2,1,0:T(8,128)S(1)}, f32[2,18,128]{2,1,0:T(8,128)S(1)}, u32[]{:S(2)}, u32[]{:S(2)}) %collective-permute-start.8) | collective-permute-done | bytes 18464 | tf_op jit(solution)/shard_map/ppermute | solution.py:334
  54.6 2.6 collective-permute-start.2
  57.2 8.9 %collective-permute-done.7 = f32[2,18,128]{2,1,0:T(8,128)S(1)} collective-permute-done((f32[2,18,128]{2,1,0:T(8,128)S(1)}, f32[2,18,128]{2,1,0:T(8,128)S(1)}, u32[]{:S(2)}, u32[]{:S(2)}) %collective-permute-start.7) | collective-permute-done | bytes 18464 | tf_op jit(solution)/shard_map/ppermute | solution.py:334
  67.6 2.6 collective-permute-start.5
  70.2 1.4 pad_maximum_fusion.2
  71.6 1.5 rev.3
  74.8 8.7 %collective-permute-done.2.q3 = bf16[2304,128]{1,0:T(8,128)(2,1)S(1)} collective-permute-done((bf16[2304,128]{1,0:T(8,128)(2,1)}, bf16[2304,128]{1,0:T(8,128)(2,1)S(1)}, u32[]{:S(2)}, u32[]{:S(2)}) %collective-permute-start.2) | collective-permute-done | bytes 589856 | tf_op jit(solution)/shard_map/ppermute | solution.py:334
  83.5 11.0 %collective-permute-done.3.d1 = bf16[2304,128]{1,0:T(8,128)(2,1)S(1)} collective-permute-done((bf16[2304,128]{1,0:T(8,128)(2,1)}, bf16[2304,128]{1,0:T(8,128)(2,1)S(1)}, u32[]{:S(2)}, u32[]{:S(2)}) %collective-permute-start.3) | collective-permute-done | bytes 589856 | tf_op jit(solution)/shard_map/ppermute | solution.py:334
  97.8 5.9 %collective-permute-start.13 = (bf16[4,128,128]{2,1,0:T(8,128)(2,1)}, bf16[4,128,128]{2,1,0:T(8,128)(2,1)}, u32[]{:S(2)}, u32[]{:S(2)}) collective-permute-start(bf16[4,128,128]{2,1,0:T(8,128)(2,1)} %pad_maximum_fusion.1), channel_id=1, source_target_pairs={{0,96},{1,97},{2,98},{3,99},{4,100},{5,101},{6,102},{7,103},{8,104... | collective-permute-start | bytes 393224 | tf_op jit(solution)/shard_map/ppermute | solution.py:396
  103.7 1.9 collective-permute-start.11
  105.6 2.0 collective-permute-start.12
  107.6 20.6 %collective-permute-done.13 = bf16[4,128,128]{2,1,0:T(8,128)(2,1)} collective-permute-done((bf16[4,128,128]{2,1,0:T(8,128)(2,1)}, bf16[4,128,128]{2,1,0:T(8,128)(2,1)}, u32[]{:S(2)}, u32[]{:S(2)}) %collective-permute-start.13) | collective-permute-done | bytes 131104 | tf_op jit(solution)/shard_map/ppermute | solution.py:396
  128.2 3.0 collective-permute-done.11
  131.2 2.3 collective-permute-done.12
  133.5 1.7 add_select_fusion
  135.2 1.9 collective-permute-start.14
  137.2 1.5 fusion.4
  138.7 1.9 collective-permute-start.9
  140.6 3.8 %collective-permute-start.10 = (bf16[1,2,128,128]{3,2,0,1:T(8,128)(2,1)}, bf16[1,2,128,128]{3,2,0,1:T(8,128)(2,1)}, u32[]{:S(2)}, u32[]{:S(2)}) collective-permute-start(bf16[1,2,128,128]{3,2,0,1:T(8,128)(2,1)} %get-tuple-element.92), channel_id=1, source_target_pairs={{4,0},{8,4},{12,8},{16,12},{20,16},{24,20},{28,24},{32,28},{36,32}... | collective-permute-start | bytes 196616 | tf_op jit(solution)/shard_map/ppermute | solution.py:400
  144.5 1.5 copy.78.ld_ref
  146.9 15.6 %random.1 = (f32[9,128,1024]{2,1,0:T(8,128)}, bf16[64,2,128,128]{3,2,1,0:T(8,128)(2,1)}) custom-call(s32[93]{0:T(128)S(1)} %pad_add_fusion.meta, bf16[2304,128]{1,0:T(8,128)(2,1)S(1)} %get-tuple-element.37.q0, bf16[2304,128]{1,0:T(8,128)(2,1)S(1)} %collective-permute-done.q1, bf16[2304,128]{1,0:T(8,128)(2,1)S(1)} %collective-permute-done.1.q2, ...), custom_call_target="tpu_custom_call" | custom-call | tf_op jit(solution)/shard_map/random/pallas_call | solution.py:250
  162.6 8.5 %all-to-all-start.2 = ((bf16[64,2,128,128]{3,2,1,0:T(8,128)(2,1)}), bf16[64,2,128,128]{3,2,1,0:T(8,128)(2,1)}, u32[]{:S(2)}, u32[]{:S(2)}) async-start(bf16[64,2,128,128]{3,2,1,0:T(8,128)(2,1)} %get-tuple-element.64), calls=%async_computation.2 | async-start | bytes 8388608 | tf_op jit(solution)/shard_map/all_to_all | solution.py:330
  172.8 1.3 collective-permute-start.16
  174.1 12.1 %collective-permute-done.16 = bf16[4,128,128]{2,1,0:T(8,128)(2,1)S(1)} collective-permute-done((bf16[4,128,128]{2,1,0:T(8,128)(2,1)S(1)}, bf16[4,128,128]{2,1,0:T(8,128)(2,1)S(1)}, u32[]{:S(2)}, u32[]{:S(2)}) %collective-permute-start.16) | collective-permute-done | bytes 131104 | tf_op jit(solution)/shard_map/ppermute | solution.py:352
  186.3 1.3 collective-permute-start.17
  189.5 3.2 %collective-permute-done.17 = bf16[4,128,128]{2,1,0:T(8,128)(2,1)S(1)} collective-permute-done((bf16[4,128,128]{2,1,0:T(8,128)(2,1)S(1)}, bf16[4,128,128]{2,1,0:T(8,128)(2,1)S(1)}, u32[]{:S(2)}, u32[]{:S(2)}) %collective-permute-start.17) | collective-permute-done | bytes 131104 | tf_op jit(solution)/shard_map/ppermute | solution.py:352
  192.7 23.3 %near.1 = (bf16[2304,128]{1,0:T(8,128)(2,1)S(1)}, bf16[2304,128]{1,0:T(8,128)(2,1)S(1)}, bf16[2304,128]{1,0:T(8,128)(2,1)S(1)}, bf16[2304,128]{1,0:T(8,128)(2,1)...) custom-call(s32[93]{0:T(128)S(1)} %pad_add_fusion.meta, bf16[2304,128]{1,0:T(8,128)(2,1)S(1)} %get-tuple-element.37.q0, ...), custom_call_target="tpu_custom_call" | custom-call | tf_op jit(solution)/shard_map/near/pallas_call | solution.py:228
  217.9 2.1 collective-permute-start.19
  220.7 9.8 %collective-permute-done.21 = f32[2,2,128,128]{3,2,1,0:T(8,128)S(1)} collective-permute-done((f32[2,2,128,128]{3,2,1,0:T(8,128)S(1)}, f32[2,2,128,128]{3,2,1,0:T(8,128)S(1)}, u32[]{:S(2)}, u32[]{:S(2)}) %collective-permute-start.21) | collective-permute-done | bytes 262176 | tf_op jit(solution)/shard_map/ppermute | solution.py:361
  230.5 5.6 %collective-permute-start.22 = (f32[2,2,128,128]{3,2,1,0:T(8,128)S(1)}, f32[2,2,128,128]{3,2,1,0:T(8,128)S(1)}, u32[]{:S(2)}, u32[]{:S(2)}) collective-permute-start(f32[2,2,128,128]{3,2,1,0:T(8,128)S(1)} %add.110), channel_id=1, source_target_pairs={{8,0},{12,4},{9,1},{13,5},{10,2},{14,6},{11,3},{15,7},{40,32},{44,... | collective-permute-start | bytes 786440 | tf_op jit(solution)/shard_map/ppermute | solution.py:361
  236.1 8.5 %collective-permute-done.22 = f32[2,2,128,128]{3,2,1,0:T(8,128)S(1)} collective-permute-done((f32[2,2,128,128]{3,2,1,0:T(8,128)S(1)}, f32[2,2,128,128]{3,2,1,0:T(8,128)S(1)}, u32[]{:S(2)}, u32[]{:S(2)}) %collective-permute-start.22) | collective-permute-done | bytes 262176 | tf_op jit(solution)/shard_map/ppermute | solution.py:361
  246.6 4.2 %join.1 = bf16[288,4,8,128]{3,2,1,0:T(8,128)(2,1)} custom-call(s32[1]{0:T(128)} %bitcast.head, bf16[288,8,128]{2,1,0:T(8,128)(2,1)} %bitcast.89, bf16[288,8,128]{2,1,0:T(8,128)(2,1)} %bitcast.99, bf16[288,8,128]{2,1,0:T(8,128)(2,1)} %bitcast.100, bf16[288,8,128]{2,1,0:T(8,128)(2,1)} %bitcast.101), custom_call_target="tpu_custom_call" | custom-call | tf_op jit(solution)/shard_map/join/pallas_call | solution.py:316
  257.4 18.4 %collective-permute-done.32 = bf16[2,2,128,128]{3,2,1,0:T(8,128)(2,1)S(1)} collective-permute-done((bf16[2,2,128,128]{3,2,1,0:T(8,128)(2,1)S(1)}, bf16[2,2,128,128]{3,2,1,0:T(8,128)(2,1)S(1)}, u32[]{:S(2)}, u32[]{:S(2)}) %collective-permute-start.32) | collective-permute-done | bytes 131104 | tf_op jit(solution)/shard_map/ppermute | solution.py:414
  277.2 1.3 collective-permute-start.26
  278.5 2.0 collective-permute-start.24
  280.5 2.3 collective-permute-start.25
  283.8 2.7 collective-permute-done.26
  286.7 5.5 %collect.1 = bf16[9,2,128,128]{3,2,1,0:T(8,128)(2,1)S(1)} custom-call(s32[93]{0:T(128)S(1)} %pad_add_fusion.meta, bf16[64,2,128,128]{3,2,1,0:T(8,128)(2,1)} %all-to-all-done.2.got, f32[11,2,128,128]{3,2,1,0:T(8,128)S(1)} %copy-done, bf16[1,2,128,128]{3,2,1,0:T(8,128)(2,1)S(1)} %collective-permute-done.24.lower, ...), custom_call_target="tpu_custom_call" | custom-call | tf_op jit(solution)/shard_map/collect/pallas_call | solution.py:294
  292.3 13.1 %all_to_all.20 = bf16[4,2,288,128]{3,2,1,0:T(8,128)(2,1)S(1)} all-to-all(bf16[4,2,288,128]{3,2,1,0:T(8,128)(2,1)S(1)} %copy.81), channel_id=1, replica_groups=mesh['z'=8,'x'=4,'c'=2,'head'=4] {'head'}, dimensions={0} | all-to-all | bytes 1179648 | tf_op jit(solution)/shard_map/all_to_all | solution.py:330
  (125 shorter events, 32.7 us)
Async XLA Ops:
  0.6 6.5 %copy-start.22 = (s32[576,3]{0,1:T(4,128)S(1)}, s32[576,3]{0,1:T(4,128)}, u32[]{:S(2)}) copy-start(s32[576,3]{0,1:T(4,128)} %param.15) | copy-start | bytes 20740
  0.6 6.5 %copy-start.23 = (s32[576,3]{0,1:T(4,128)S(1)}, s32[576,3]{0,1:T(4,128)}, u32[]{:S(2)}) copy-start(s32[576,3]{0,1:T(4,128)} %param.14) | copy-start | bytes 20740
  2.7 14.6 %all-to-all-start = ((bf16[4,2,288,128]{3,2,1,0:T(8,128)(2,1)}), bf16[4,2,288,128]{3,2,1,0:T(8,128)(2,1)S(1)}, u32[]{:S(2)}, u32[]{:S(2)}) async-start(bf16[4,2,288,128]{3,2,1,0:T(8,128)(2,1)} %maximum_bitcast_fusion), calls=%async_computation | async-start | bytes 1179648 | tf_op jit(solution)/shard_map/all_to_all | solution.py:330
  22.4 12.5 %copy-start.11 = (bf16[288,32,128]{2,1,0:T(8,128)(2,1)S(1)}, bf16[288,32,128]{2,1,0:T(8,128)(2,1)}, u32[]{:S(2)}) copy-start(bf16[288,32,128]{2,1,0:T(8,128)(2,1)} %param.8) | copy-start | bytes 7077892
  22.4 123.7 %all-to-all-start.1 = ((bf16[64,2,128,128]{3,2,1,0:T(8,128)(2,1)}), bf16[64,2,128,128]{3,2,1,0:T(8,128)(2,1)}, u32[]{:S(2)}, u32[]{:S(2)}) async-start(bf16[64,2,128,128]{3,2,1,0:T(8,128)(2,1)} %select.11), calls=%async_computation.1 | async-start | bytes 8388608 | tf_op jit(solution)/shard_map/all_to_all | solution.py:330
  36.3 31.2 %collective-permute-start = (bf16[2304,128]{1,0:T(8,128)(2,1)}, bf16[2304,128]{1,0:T(8,128)(2,1)S(1)}, u32[]{:S(2)}, u32[]{:S(2)}) collective-permute-start(bf16[2304,128]{1,0:T(8,128)(2,1)} %get-tuple-element.84), channel_id=1, source_target_pairs={{0,1},{1,2},{2,3},{3,0},{4,5},{5,6},{6,7},{7,4},{8,9},{9,10},{10,1... | collective-permute-start | bytes 1769480 | tf_op jit(solution)/shard_map/ppermute | solution.py:334
  36.9 37.8 %collective-permute-start.1 = (bf16[2304,128]{1,0:T(8,128)(2,1)}, bf16[2304,128]{1,0:T(8,128)(2,1)S(1)}, u32[]{:S(2)}, u32[]{:S(2)}) collective-permute-start(bf16[2304,128]{1,0:T(8,128)(2,1)} %get-tuple-element.83), channel_id=1, source_target_pairs={{0,2},{1,3},{2,0},{3,1},{4,6},{5,7},{6,4},{7,5},{8,10},{9,11},{10,... | collective-permute-start | bytes 1769480 | tf_op jit(solution)/shard_map/ppermute | solution.py:334
  42.0 12.6 %collective-permute-start.8 = (f32[2,18,128]{2,1,0:T(8,128)S(1)}, f32[2,18,128]{2,1,0:T(8,128)S(1)}, u32[]{:S(2)}, u32[]{:S(2)}) collective-permute-start(f32[2,18,128]{2,1,0:T(8,128)S(1)} %get-tuple-element.95), channel_id=1, source_target_pairs={{0,3},{1,0},{2,1},{3,2},{4,7},{5,4},{6,5},{7,6},{8,11},{9,8},{10,9... | collective-permute-start | bytes 55304 | tf_op jit(solution)/shard_map/ppermute | solution.py:334
  42.6 23.5 %collective-permute-start.7 = (f32[2,18,128]{2,1,0:T(8,128)S(1)}, f32[2,18,128]{2,1,0:T(8,128)S(1)}, u32[]{:S(2)}, u32[]{:S(2)}) collective-permute-start(f32[2,18,128]{2,1,0:T(8,128)S(1)} %get-tuple-element.96), channel_id=1, source_target_pairs={{0,2},{1,3},{2,0},{3,1},{4,6},{5,7},{6,4},{7,5},{8,10},{9,11},{10,... | collective-permute-start | bytes 55304 | tf_op jit(solution)/shard_map/ppermute | solution.py:334
  45.5 21.3 %collective-permute-start.6 = (f32[2,18,128]{2,1,0:T(8,128)S(1)}, f32[2,18,128]{2,1,0:T(8,128)S(1)}, u32[]{:S(2)}, u32[]{:S(2)}) collective-permute-start(f32[2,18,128]{2,1,0:T(8,128)S(1)} %get-tuple-element.97), channel_id=1, source_target_pairs={{0,1},{1,2},{2,3},{3,0},{4,5},{5,6},{6,7},{7,4},{8,9},{9,10},{10,1... | collective-permute-start | bytes 55304 | tf_op jit(solution)/shard_map/ppermute | solution.py:334
  48.4 114.1 %copy-start.1 = (bf16[2304,128]{1,0:T(8,128)(2,1)}, bf16[2304,128]{1,0:T(8,128)(2,1)S(1)}, u32[]{:S(2)}) copy-start(bf16[2304,128]{1,0:T(8,128)(2,1)S(1)} %get-tuple-element.41.d0) | copy-start | bytes 1769476
  54.6 13.0 %copy-start.19 = (f32[2,18,128]{2,1,0:T(8,128)}, f32[2,18,128]{2,1,0:T(8,128)S(1)}, u32[]{:S(2)}) copy-start(f32[2,18,128]{2,1,0:T(8,128)S(1)} %collective-permute-done.8) | copy-start | bytes 55300
  54.6 28.9 %collective-permute-start.2 = (bf16[2304,128]{1,0:T(8,128)(2,1)}, bf16[2304,128]{1,0:T(8,128)(2,1)S(1)}, u32[]{:S(2)}, u32[]{:S(2)}) collective-permute-start(bf16[2304,128]{1,0:T(8,128)(2,1)} %get-tuple-element.82), channel_id=1, source_target_pairs={{0,3},{1,0},{2,1},{3,2},{4,7},{5,4},{6,5},{7,6},{8,11},{9,8},{10,9... | collective-permute-start | bytes 1769480 | tf_op jit(solution)/shard_map/ppermute | solution.py:334
  66.1 28.4 %collective-permute-start.3 = (bf16[2304,128]{1,0:T(8,128)(2,1)}, bf16[2304,128]{1,0:T(8,128)(2,1)S(1)}, u32[]{:S(2)}, u32[]{:S(2)}) collective-permute-start(bf16[2304,128]{1,0:T(8,128)(2,1)} %get-tuple-element.80), channel_id=1, source_target_pairs={{0,1},{1,2},{2,3},{3,0},{4,5},{5,6},{6,7},{7,4},{8,9},{9,10},{10,1... | collective-permute-start | bytes 1769480 | tf_op jit(solution)/shard_map/ppermute | solution.py:334
  66.8 27.6 %collective-permute-start.4 = (bf16[2304,128]{1,0:T(8,128)(2,1)}, bf16[2304,128]{1,0:T(8,128)(2,1)}, u32[]{:S(2)}, u32[]{:S(2)}) collective-permute-start(bf16[2304,128]{1,0:T(8,128)(2,1)} %get-tuple-element.79), channel_id=1, source_target_pairs={{0,2},{1,3},{2,0},{3,1},{4,6},{5,7},{6,4},{7,5},{8,10},{9,11},{10,... | collective-permute-start | bytes 1769480 | tf_op jit(solution)/shard_map/ppermute | solution.py:334
  67.6 28.1 %collective-permute-start.5 = (bf16[2304,128]{1,0:T(8,128)(2,1)}, bf16[2304,128]{1,0:T(8,128)(2,1)}, u32[]{:S(2)}, u32[]{:S(2)}) collective-permute-start(bf16[2304,128]{1,0:T(8,128)(2,1)} %get-tuple-element.78), channel_id=1, source_target_pairs={{0,3},{1,0},{2,1},{3,2},{4,7},{5,4},{6,5},{7,6},{8,11},{9,8},{10,9... | collective-permute-start | bytes 1769480 | tf_op jit(solution)/shard_map/ppermute | solution.py:334
  74.8 87.8 %copy-start.2 = (bf16[2304,128]{1,0:T(8,128)(2,1)}, bf16[2304,128]{1,0:T(8,128)(2,1)S(1)}, u32[]{:S(2)}) copy-start(bf16[2304,128]{1,0:T(8,128)(2,1)S(1)} %collective-permute-done.1.q2) | copy-start | bytes 1769476
  83.5 79.1 %copy-start.3 = (bf16[2304,128]{1,0:T(8,128)(2,1)}, bf16[2304,128]{1,0:T(8,128)(2,1)S(1)}, u32[]{:S(2)}) copy-start(bf16[2304,128]{1,0:T(8,128)(2,1)S(1)} %collective-permute-done.2.q3) | copy-start | bytes 1769476
  94.5 68.1 %copy-start.4 = (bf16[2304,128]{1,0:T(8,128)(2,1)}, bf16[2304,128]{1,0:T(8,128)(2,1)S(1)}, u32[]{:S(2)}) copy-start(bf16[2304,128]{1,0:T(8,128)(2,1)S(1)} %collective-permute-done.3.d1) | copy-start | bytes 1769476
  97.8 30.4 %collective-permute-start.13 = (bf16[4,128,128]{2,1,0:T(8,128)(2,1)}, bf16[4,128,128]{2,1,0:T(8,128)(2,1)}, u32[]{:S(2)}, u32[]{:S(2)}) collective-permute-start(bf16[4,128,128]{2,1,0:T(8,128)(2,1)} %pad_maximum_fusion.1), channel_id=1, source_target_pairs={{0,96},{1,97},{2,98},{3,99},{4,100},{5,101},{6,102},{7,103},{8,104... | collective-permute-start | bytes 393224 | tf_op jit(solution)/shard_map/ppermute | solution.py:396
  103.7 27.5 %collective-permute-start.11 = (bf16[4,128,128]{2,1,0:T(8,128)(2,1)}, bf16[4,128,128]{2,1,0:T(8,128)(2,1)}, u32[]{:S(2)}, u32[]{:S(2)}) collective-permute-start(bf16[4,128,128]{2,1,0:T(8,128)(2,1)} %pad_maximum_fusion.1), channel_id=1, source_target_pairs={{0,32},{1,33},{2,34},{3,35},{4,36},{5,37},{6,38},{7,39},{8,40},{9,... | collective-permute-start | bytes 393224 | tf_op jit(solution)/shard_map/ppermute | solution.py:396
  105.6 27.9 %collective-permute-start.12 = (bf16[4,128,128]{2,1,0:T(8,128)(2,1)}, bf16[4,128,128]{2,1,0:T(8,128)(2,1)}, u32[]{:S(2)}, u32[]{:S(2)}) collective-permute-start(bf16[4,128,128]{2,1,0:T(8,128)(2,1)} %pad_maximum_fusion.1), channel_id=1, source_target_pairs={{0,64},{1,65},{2,66},{3,67},{4,68},{5,69},{6,70},{7,71},{8,72},{9,... | collective-permute-start | bytes 393224 | tf_op jit(solution)/shard_map/ppermute | solution.py:396
  135.2 27.3 %collective-permute-start.14 = (bf16[4,128,128]{2,1,0:T(8,128)(2,1)}, bf16[4,128,128]{2,1,0:T(8,128)(2,1)}, u32[]{:S(2)}, u32[]{:S(2)}) collective-permute-start(bf16[4,128,128]{2,1,0:T(8,128)(2,1)} %add_select_fusion), channel_id=1, source_target_pairs={{0,128},{32,160},{64,192},{96,224},{1,129},{33,161},{65,193},{97,2... | collective-permute-start | bytes 393224 | tf_op jit(solution)/shard_map/ppermute | solution.py:398
  138.7 23.8 %collective-permute-start.9 = (bf16[1,2,128,128]{3,2,0,1:T(8,128)(2,1)}, bf16[1,2,128,128]{3,2,0,1:T(8,128)(2,1)}, u32[]{:S(2)}, u32[]{:S(2)}) collective-permute-start(bf16[1,2,128,128]{3,2,0,1:T(8,128)(2,1)} %get-tuple-element.93), channel_id=1, source_target_pairs={{0,4},{4,8},{8,12},{12,16},{16,20},{20,24},{24,28},{28,32},{32,36}... | collective-permute-start | bytes 196616 | tf_op jit(solution)/shard_map/ppermute | solution.py:399
  140.6 21.9 %collective-permute-start.10 = (bf16[1,2,128,128]{3,2,0,1:T(8,128)(2,1)}, bf16[1,2,128,128]{3,2,0,1:T(8,128)(2,1)}, u32[]{:S(2)}, u32[]{:S(2)}) collective-permute-start(bf16[1,2,128,128]{3,2,0,1:T(8,128)(2,1)} %get-tuple-element.92), channel_id=1, source_target_pairs={{4,0},{8,4},{12,8},{16,12},{20,16},{24,20},{28,24},{32,28},{36,32}... | collective-permute-start | bytes 196616 | tf_op jit(solution)/shard_map/ppermute | solution.py:400
  162.6 25.0 %copy-start.10 = (bf16[2,4,288,128]{3,2,1,0:T(8,128)(2,1)S(1)}, bf16[2,4,288,128]{3,2,1,0:T(8,128)(2,1)}, u32[]{:S(2)}) copy-start(bf16[2,4,288,128]{3,2,1,0:T(8,128)(2,1)} %copy-done.9) | copy-start | bytes 1769476
  162.6 124.1 %all-to-all-start.2 = ((bf16[64,2,128,128]{3,2,1,0:T(8,128)(2,1)}), bf16[64,2,128,128]{3,2,1,0:T(8,128)(2,1)}, u32[]{:S(2)}, u32[]{:S(2)}) async-start(bf16[64,2,128,128]{3,2,1,0:T(8,128)(2,1)} %get-tuple-element.64), calls=%async_computation.2 | async-start | bytes 8388608 | tf_op jit(solution)/shard_map/all_to_all | solution.py:330
  171.1 21.5 %copy-start.6 = (f32[2,9,8,128]{3,2,1,0:T(8,128)S(1)}, f32[2,9,8,128]{3,2,1,0:T(8,128)}, u32[]{:S(2)}) copy-start(f32[2,9,8,128]{3,2,1,0:T(8,128)} %copy.78.ld_ref) | copy-start | bytes 221188
  172.1 0.7 collective-permute-start.15
  172.8 13.4 %collective-permute-start.16 = (bf16[4,128,128]{2,1,0:T(8,128)(2,1)S(1)}, bf16[4,128,128]{2,1,0:T(8,128)(2,1)S(1)}, u32[]{:S(2)}, u32[]{:S(2)}) collective-permute-start(bf16[4,128,128]{2,1,0:T(8,128)(2,1)S(1)} %broadcast_select_fusion.1), channel_id=1, source_target_pairs={{0,8},{4,12},{1,9},{5,13},{2,10},{6,14},{3,11},{7,15},{32,40},{36,... | collective-permute-start | bytes 393224 | tf_op jit(solution)/shard_map/ppermute | solution.py:352
  186.3 6.4 %collective-permute-start.17 = (bf16[4,128,128]{2,1,0:T(8,128)(2,1)S(1)}, bf16[4,128,128]{2,1,0:T(8,128)(2,1)S(1)}, u32[]{:S(2)}, u32[]{:S(2)}) collective-permute-start(bf16[4,128,128]{2,1,0:T(8,128)(2,1)S(1)} %broadcast_select_fusion.2), channel_id=1, source_target_pairs={{0,16},{4,20},{8,24},{12,28},{1,17},{5,21},{9,25},{13,29},{2,18},{... | collective-permute-start | bytes 393224 | tf_op jit(solution)/shard_map/ppermute | solution.py:352
  216.0 29.4 %copy-start.7 = (bf16[2304,128]{1,0:T(8,128)(2,1)}, bf16[2304,128]{1,0:T(8,128)(2,1)S(1)}, u32[]{:S(2)}) copy-start(bf16[2304,128]{1,0:T(8,128)(2,1)S(1)} %get-tuple-element.57) | copy-start | bytes 1769476
  216.0 14.5 %collective-permute-start.21 = (f32[2,2,128,128]{3,2,1,0:T(8,128)S(1)}, f32[2,2,128,128]{3,2,1,0:T(8,128)S(1)}, u32[]{:S(2)}, u32[]{:S(2)}) collective-permute-start(f32[2,2,128,128]{3,2,1,0:T(8,128)S(1)} %get-tuple-element.56), channel_id=1, source_target_pairs={{16,0},{20,4},{24,8},{28,12},{17,1},{21,5},{25,9},{29,13},{18,2},{... | collective-permute-start | bytes 786440 | tf_op jit(solution)/shard_map/ppermute | solution.py:361
  217.3 28.0 %collective-permute-start.18 = (bf16[2304,128]{1,0:T(8,128)(2,1)S(1)}, bf16[2304,128]{1,0:T(8,128)(2,1)S(1)}, u32[]{:S(2)}, u32[]{:S(2)}) collective-permute-start(bf16[2304,128]{1,0:T(8,128)(2,1)S(1)} %get-tuple-element.53), channel_id=1, source_target_pairs={{0,1},{1,2},{2,3},{3,0},{4,5},{5,6},{6,7},{7,4},{8,9},{9,10},{10,1... | collective-permute-start | bytes 1769480 | tf_op jit(solution)/shard_map/ppermute | solution.py:334
  217.9 27.4 %collective-permute-start.19 = (bf16[2304,128]{1,0:T(8,128)(2,1)S(1)}, bf16[2304,128]{1,0:T(8,128)(2,1)S(1)}, u32[]{:S(2)}, u32[]{:S(2)}) collective-permute-start(bf16[2304,128]{1,0:T(8,128)(2,1)S(1)} %get-tuple-element.54), channel_id=1, source_target_pairs={{0,2},{1,3},{2,0},{3,1},{4,6},{5,7},{6,4},{7,5},{8,10},{9,11},{10,... | collective-permute-start | bytes 1769480 | tf_op jit(solution)/shard_map/ppermute | solution.py:334
  220.0 25.4 %collective-permute-start.20 = (bf16[2304,128]{1,0:T(8,128)(2,1)S(1)}, bf16[2304,128]{1,0:T(8,128)(2,1)S(1)}, u32[]{:S(2)}, u32[]{:S(2)}) collective-permute-start(bf16[2304,128]{1,0:T(8,128)(2,1)S(1)} %get-tuple-element.55), channel_id=1, source_target_pairs={{0,3},{1,0},{2,1},{3,2},{4,7},{5,4},{6,5},{7,6},{8,11},{9,8},{10,9... | collective-permute-start | bytes 1769480 | tf_op jit(solution)/shard_map/ppermute | solution.py:334
  230.5 14.1 %collective-permute-start.22 = (f32[2,2,128,128]{3,2,1,0:T(8,128)S(1)}, f32[2,2,128,128]{3,2,1,0:T(8,128)S(1)}, u32[]{:S(2)}, u32[]{:S(2)}) collective-permute-start(f32[2,2,128,128]{3,2,1,0:T(8,128)S(1)} %add.110), channel_id=1, source_target_pairs={{8,0},{12,4},{9,1},{13,5},{10,2},{14,6},{11,3},{15,7},{40,32},{44,... | collective-permute-start | bytes 786440 | tf_op jit(solution)/shard_map/ppermute | solution.py:361
  244.6 0.7 collective-permute-start.23
  246.6 10.7 %copy-start = (f32[11,2,128,128]{3,2,1,0:T(8,128)S(1)}, f32[11,2,128,128]{3,2,1,0:T(8,128)}, u32[]{:S(2)}) copy-start(f32[11,2,128,128]{3,2,1,0:T(8,128)} %get-tuple-element.65.ext) | copy-start | bytes 4325380
  250.8 25.1 %collective-permute-start.32 = (bf16[2,2,128,128]{3,2,1,0:T(8,128)(2,1)S(1)}, bf16[2,2,128,128]{3,2,1,0:T(8,128)(2,1)S(1)}, u32[]{:S(2)}, u32[]{:S(2)}) collective-permute-start(bf16[2,2,128,128]{3,2,1,0:T(8,128)(2,1)S(1)} %convert_element_type.34), channel_id=1, source_target_pairs={{224,0},{225,1},{226,2},{227,3},{228,4},{229,5},{230,6},{231,7},{2... | collective-permute-start | bytes 393224 | tf_op jit(solution)/shard_map/ppermute | solution.py:414
  252.1 25.1 %collective-permute-start.31 = (bf16[2,2,128,128]{3,2,1,0:T(8,128)(2,1)S(1)}, bf16[2,2,128,128]{3,2,1,0:T(8,128)(2,1)S(1)}, u32[]{:S(2)}, u32[]{:S(2)}) collective-permute-start(bf16[2,2,128,128]{3,2,1,0:T(8,128)(2,1)S(1)} %convert_element_type.34), channel_id=1, source_target_pairs={{192,0},{193,1},{194,2},{195,3},{196,4},{197,5},{198,6},{199,7},{2... | collective-permute-start | bytes 393224 | tf_op jit(solution)/shard_map/ppermute | solution.py:414
  253.4 25.1 %collective-permute-start.30 = (bf16[2,2,128,128]{3,2,1,0:T(8,128)(2,1)S(1)}, bf16[2,2,128,128]{3,2,1,0:T(8,128)(2,1)S(1)}, u32[]{:S(2)}, u32[]{:S(2)}) collective-permute-start(bf16[2,2,128,128]{3,2,1,0:T(8,128)(2,1)S(1)} %convert_element_type.34), channel_id=1, source_target_pairs={{160,0},{161,1},{162,2},{163,3},{164,4},{165,5},{166,6},{167,7},{1... | collective-permute-start | bytes 393224 | tf_op jit(solution)/shard_map/ppermute | solution.py:414
  254.7 25.8 %collective-permute-start.29 = (bf16[2,2,128,128]{3,2,1,0:T(8,128)(2,1)S(1)}, bf16[2,2,128,128]{3,2,1,0:T(8,128)(2,1)S(1)}, u32[]{:S(2)}, u32[]{:S(2)}) collective-permute-start(bf16[2,2,128,128]{3,2,1,0:T(8,128)(2,1)S(1)} %convert_element_type.34), channel_id=1, source_target_pairs={{128,0},{129,1},{130,2},{131,3},{132,4},{133,5},{134,6},{135,7},{1... | collective-permute-start | bytes 393224 | tf_op jit(solution)/shard_map/ppermute | solution.py:414
  256.0 26.9 %collective-permute-start.28 = (bf16[2,2,128,128]{3,2,1,0:T(8,128)(2,1)S(1)}, bf16[2,2,128,128]{3,2,1,0:T(8,128)(2,1)S(1)}, u32[]{:S(2)}, u32[]{:S(2)}) collective-permute-start(bf16[2,2,128,128]{3,2,1,0:T(8,128)(2,1)S(1)} %convert_element_type.34), channel_id=1, source_target_pairs={{96,0},{97,1},{98,2},{99,3},{100,4},{101,5},{102,6},{103,7},{104,8... | collective-permute-start | bytes 393224 | tf_op jit(solution)/shard_map/ppermute | solution.py:414
  275.9 7.9 %collective-permute-start.27 = (bf16[2,2,128,128]{3,2,1,0:T(8,128)(2,1)S(1)}, bf16[2,2,128,128]{3,2,1,0:T(8,128)(2,1)S(1)}, u32[]{:S(2)}, u32[]{:S(2)}) collective-permute-start(bf16[2,2,128,128]{3,2,1,0:T(8,128)(2,1)S(1)} %convert_element_type.34), channel_id=1, source_target_pairs={{64,0},{65,1},{66,2},{67,3},{68,4},{69,5},{70,6},{71,7},{72,8},{73... | collective-permute-start | bytes 393224 | tf_op jit(solution)/shard_map/ppermute | solution.py:414
  277.2 9.3 %collective-permute-start.26 = (bf16[2,2,128,128]{3,2,1,0:T(8,128)(2,1)S(1)}, bf16[2,2,128,128]{3,2,1,0:T(8,128)(2,1)S(1)}, u32[]{:S(2)}, u32[]{:S(2)}) collective-permute-start(bf16[2,2,128,128]{3,2,1,0:T(8,128)(2,1)S(1)} %convert_element_type.34), channel_id=1, source_target_pairs={{32,0},{33,1},{34,2},{35,3},{36,4},{37,5},{38,6},{39,7},{40,8},{41... | collective-permute-start | bytes 393224 | tf_op jit(solution)/shard_map/ppermute | solution.py:414
  278.5 8.1 %collective-permute-start.24 = (bf16[1,2,128,128]{3,2,1,0:T(8,128)(2,1)S(1)}, bf16[1,2,128,128]{3,2,1,0:T(8,128)(2,1)S(1)}, u32[]{:S(2)}, u32[]{:S(2)}) collective-permute-start(bf16[1,2,128,128]{3,2,1,0:T(8,128)(2,1)S(1)} %get-tuple-element.87), channel_id=1, source_target_pairs={{4,0},{8,4},{12,8},{16,12},{20,16},{24,20},{28,24},{32,28},{36,32}... | collective-permute-start | bytes 196616 | tf_op jit(solution)/shard_map/ppermute | solution.py:410
  280.5 6.1 %collective-permute-start.25 = (bf16[1,2,128,128]{3,2,1,0:T(8,128)(2,1)S(1)}, bf16[1,2,128,128]{3,2,1,0:T(8,128)(2,1)S(1)}, u32[]{:S(2)}, u32[]{:S(2)}) collective-permute-start(bf16[1,2,128,128]{3,2,1,0:T(8,128)(2,1)S(1)} %get-tuple-element.86), channel_id=1, source_target_pairs={{0,4},{4,8},{8,12},{12,16},{16,20},{20,24},{24,28},{28,32},{32,36}... | collective-permute-start | bytes 196616 | tf_op jit(solution)/shard_map/ppermute | solution.py:411
  (12 other events, 20.6 us)

commit v4 on v3

--- a/solution.py
+++ b/solution.py
@@ -25,7 +25,10 @@
 LOG2E = 1.4426950408889634
 MASKED = 1e30
 ENT = QB * RND
-AT_SEQ, AT_HEAD, AT_WANT = ENT, ENT + 1, ENT + 2
+AT_SEQ, AT_HEAD, AT_Z, AT_WANT = ENT, ENT + 1, ENT + 2, ENT + 3
+AT_PLANE = AT_WANT + NSEQ
+NEAR, FAR = (0, 1, 2, 6, 7), (3, 4, 5)
+CUT = 5
 STEP = 8
 PART = TOK * HL
 BF = jnp.bfloat16
@@ -118,14 +121,21 @@
             c.wait()
 
 
+def place_of(meta, owner):
+    r = ((owner >> 3) - meta[AT_Z]) & (NZ - 1)
+    far = (r >= FAR[0]) & (r <= FAR[-1])
+    pos = jnp.where(r >= FAR[0], r - FAR[0], r)
+    return far, (owner & (NXC - 1)) * jnp.where(far, len(FAR), len(NEAR)) + pos
+
+
 def random_kernel(
-    meta, q0, q1, q2, q3, d0, d1, d2, d3, ld_ref, got_ref,
+    meta, q0, q1, q2, q3, d0, d1, d2, d3, ld_ref, near_ref, far_ref,
     dqt_ref, dkv_ref, q_scr, do_scr, kv_scr, out_scr, key_scr, p_scr, ds_scr, sems, in_sems, out_sems,
 ):
     b = pl.program_id(0)
 
-    def fetch(e):
-        return pltpu.make_async_copy(got_ref.at[meta[e] >> 4], kv_scr.at[e], in_sems.at[e])
+    def fetch(src, at, e):
+        return pltpu.make_async_copy(src.at[at], kv_scr.at[e], in_sems.at[e])
 
     def give(e):
         return pltpu.make_async_copy(out_scr.at[e], dkv_ref.at[meta[e] >> 4], out_sems.at[e])
@@ -133,7 +143,16 @@
     @pl.when(b == 0)
     def _():
         for e in range(ENT):
-            fetch(e).start()
+            far, at = place_of(meta, meta[e] >> 4)
+
+            @pl.when(far)
+            def _():
+                fetch(far_ref, at, e).start()
+
+            @pl.when(jnp.logical_not(far))
+            def _():
+                fetch(near_ref, at, e).start()
+
         load_parts(meta, ((q0, q1, q2, q3), (d0, d1, d2, d3)), (q_scr, do_scr), sems)
 
     first = b * RND
@@ -143,7 +162,7 @@
         named = meta[first + j]
         r = (named >> 4) * QB + (named & 15)
         biases.append(jnp.where((r >= G) & (jnp.abs(r - block) >= 2), 0.0, MASKED))
-        fetch(first + j).wait()
+        fetch(near_ref, 0, first + j).wait()
     lse2, delta = row_vector(ld_ref[0, 0]), row_vector(ld_ref[1, 0])
     rows = pl.ds(pl.multiple_of(b * ROWS, ROWS), ROWS)
     dk, dv, dqt = pair_grads(
@@ -164,14 +183,23 @@
             give(e).wait()
 
 
-def select_kernel(meta, kv_ref, out_ref):
-    base = pl.program_id(0) * STEP
-    for i in range(STEP):
-        slot = meta[AT_WANT + base + i]
-
-        @pl.when(slot >= 0)
+def select_kernel(steps, meta, *refs):
+    sources, dst = refs[:-1], refs[-1]
+
+    def lay(wanted, src, slot, at):
+        @pl.when(wanted)
         def _():
-            out_ref[i] = kv_ref[slot]
+            dst[at] = src[slot]
+
+    for d in range(NXC):
+        for i, r in enumerate(steps):
+            slot = meta[AT_PLANE + d * NZ + r]
+            at = d * len(steps) + i
+            if r == 4:
+                lay((slot >= 0) & (slot < CUT), sources[i], slot, at)
+                lay(slot >= CUT, sources[-1], slot - CUT, at)
+            else:
+                lay(slot >= 0, sources[i], slot, at)
 
 
 def collect_kernel(meta, got, ext, lower, upper, dg, out, acc):
@@ -246,13 +274,13 @@
     )(meta, *q, *do, ld, kvx, gl, dqt)
 
 
-def call_random(meta, q, do, ld, got):
+def call_random(meta, q, do, ld, near, far):
     return pl.pallas_call(
         random_kernel,
         grid_spec=pltpu.PrefetchScalarGridSpec(
             num_scalar_prefetch=1,
             grid=(QB,),
-            in_specs=anywhere(2 * NH) + [ROW_PAIR] + anywhere(1),
+            in_specs=anywhere(2 * NH) + [ROW_PAIR] + anywhere(2),
             out_specs=[DQT] + anywhere(1),
             scratch_shapes=[pltpu.VMEM((QB * ROWS, HD), BF)] * 2
             + [pltpu.VMEM((ENT, *TILE), BF)] * 2
@@ -269,25 +297,26 @@
         ],
         compiler_params=PARAMS,
         name="random",
-    )(meta, *q, *do, ld, got)
+    )(meta, *q, *do, ld, near, far)
 
 
 STEP_TILES = pl.BlockSpec((STEP, *TILE), lambda b, m: (b, 0, 0, 0))
 
 
-def call_select(meta, kv):
+def call_select(meta, steps, sources):
+    n = NXC * len(steps)
     return pl.pallas_call(
-        select_kernel,
+        functools.partial(select_kernel, steps),
         grid_spec=pltpu.PrefetchScalarGridSpec(
             num_scalar_prefetch=1,
-            grid=(NSEQ // STEP,),
-            in_specs=[full(QB, *TILE)],
-            out_specs=STEP_TILES,
+            grid=(1,),
+            in_specs=[full(*x.shape) for x in sources],
+            out_specs=full(n, *TILE),
         ),
-        out_shape=jax.ShapeDtypeStruct((NSEQ, *TILE), BF),
+        out_shape=jax.ShapeDtypeStruct((n, *TILE), BF),
         compiler_params=PARAMS,
         name="select",
-    )(meta, kv)
+    )(meta, *sources)
 
 
 def call_collect(meta, got, ext, lower, upper, dg):
@@ -346,6 +375,10 @@
     return lax.optimization_barrier(values)
 
 
+def along_z(value, step):
+    return lax.ppermute(value, "z", [(i, (i + step) % NZ) for i in range(NZ)])
+
+
 def spread(value, index):
     k = 1
     while k < NXC:
@@ -368,41 +401,47 @@
     named = (owner * 16 + slot).reshape(NSEQ, ENT)
     mine = lax.dynamic_index_in_dim(named, seq, 0, keepdims=False)
     want = jnp.max(jnp.where(named >> 4 == seq, named & 15, -1), axis=1)
-    meta = jnp.concatenate([mine, jnp.stack([seq, head]).astype(jnp.int32), want])
-
     z, xc = lax.axis_index("z"), lax.axis_index(("x", "c"))
+    plane = lax.dynamic_slice_in_dim(named, z * NXC, NXC, 0)[:, None, :]
+    column = ((z + jnp.arange(NZ, dtype=jnp.int32)) % NZ * NXC + xc)[None, :, None]
+    ask = jnp.max(jnp.where(plane >> 4 == column, plane & 15, -1), axis=2)
+    spot = jnp.stack([seq, head, z]).astype(jnp.int32)
+    meta = jnp.concatenate([mine, spot, want, ask.reshape(-1)])
     up = [(i, i + 1) for i in range(NSEQ - 1)]
     down = [(i + 1, i) for i in range(NSEQ - 1)]
-    kvs = jnp.stack([k, v]).transpose(2, 0, 1, 3)
-    kv, meta = tie(plain_a2a(kvs, "head"), meta)
-    kv = kv.transpose(1, 0, 2, 3).reshape(2, QB, BLK, HD).transpose(1, 0, 2, 3)
-    got = plain_a2a(call_select(meta, kv), SEQ)
-
-    qp, dop = head_parts(q, head), head_parts(do, head)
-    ql = [turn(p, i) for i, p in enumerate(qp)]
-    dol = [turn(p, i) for i, p in enumerate(dop)]
     delta = jnp.sum(do.astype(F32) * o.astype(F32), axis=-1)
     ld = jnp.stack([lse * LOG2E, delta]).reshape(2, TOK, NH, HL).transpose(2, 0, 1, 3)
     ld = ld.reshape(NH, 2, PART // BLK, BLK)
-    ld = jnp.stack(
-        [turn(lax.dynamic_index_in_dim(ld, lax.rem(head + i, NH), 0, keepdims=False), i) for i in range(NH)]
+    lp = [lax.dynamic_index_in_dim(ld, lax.rem(head + i, NH), 0, keepdims=False) for i in range(NH)]
+    qp, dop = head_parts(q, head), head_parts(do, head)
+
+    kvs = jnp.stack([k, v]).transpose(2, 0, 1, 3)
+    kv, meta, lp = tie(plain_a2a(kvs, "head"), meta, lp)
+    kv = kv.transpose(1, 0, 2, 3).reshape(2, QB, BLK, HD).transpose(1, 0, 2, 3)
+    u1, d1, q1, q3 = tie(along_z(kv, 1), along_z(kv, -1), turn(qp[1], 1), turn(qp[3], 3))
+    u2, d2, q2 = tie(along_z(u1, 1), along_z(d1, -1), turn(qp[2], 2))
+    near = plain_a2a(call_select(meta, NEAR, [kv, d1, d2, u2, u1]), ("x", "c"))
+    u3, d3, do1, do3 = tie(
+        along_z(u2, 1), along_z(d2, -1), turn(dop[1], 1), turn(dop[3], 3)
     )
+    u4, d4, do2 = tie(along_z(u3[:CUT], 1), along_z(d3[CUT:], -1), turn(dop[2], 2))
+    near, u4 = tie(near, u4)
+    far, edges = tie(call_select(meta, FAR, [d3, u4, u3, d4]), kv)
+    far = plain_a2a(far, ("x", "c"))
+    before = lax.ppermute(edges[QB - 1 :], SEQ, up)
+    after = lax.ppermute(edges[:1], SEQ, down)
+    ql, dol = (qp[0], q1, q2, q3), (dop[0], do1, do2, do3)
+    ld = jnp.stack([turn(p, i) for i, p in enumerate(lp)])
     ld = jnp.roll(ld[::-1], head + 1, axis=0)
     ld = ld.transpose(1, 0, 2, 3).reshape(2, QB, HL, BLK)
 
-    *parts, ld, kv = tie(*ql, *dol, ld, kv)
-    ql, dol = parts[:NH], parts[NH:]
-    gl = jnp.concatenate([kv[:G, 0], kv[:G, 1]])
-    low = [lax.ppermute(gl, "z", [(0, i)]) for i in range(1, 4)]
-    gl = jnp.where(z == 0, gl, low[0] + low[1] + low[2])
-    high = lax.ppermute(gl, "z", [(i, i + 4) for i in range(4)])
-    before = lax.ppermute(kv[QB - 1 :], SEQ, up)
-    after = lax.ppermute(kv[:1], SEQ, down)
-
-    dqt, back = call_random(meta, ql, dol, ld, got)
-    back, before, after, high = tie(back, before, after, high)
+    dqt, back = call_random(meta, ql, dol, ld, near, far)
+    gl, back, before, after = tie(kv[:G], back, before, after)
+    for i, shard in enumerate((u1, u2, u3, u4, d3, d2, d1)):
+        gl = jnp.where(z == i + 1, shard[:G], gl)
+    gl = gl.transpose(1, 0, 2, 3).reshape(2 * G, BLK, HD)
     back = plain_a2a(back, SEQ)
-    gl = spread(jnp.where(z < 4, gl, high), xc)
+    gl = spread(gl, xc)
     kvx = jnp.concatenate([before, kv, after])
     *dq, dkvx, dg = call_near(meta, ql, dol, ld, kvx, gl, dqt)
     dq, dg = tie([turn(p, i) for i, p in enumerate(dq)], gather_sum(dg))

time: 310 us -> 301 us (0.971)
  waiting for transfers between devices: 128 us -> 91.3 us
  starting transfers between devices: 82.6 us -> 100 us
  local copies, waits for them, and re-layouts: 20.1 us -> 27.6 us
    ppermute x12, waiting for transfers between devices: 36.7 us -> 13 us  [turn(): lax.ppermute(value, 'head', [(i, (i + k) % NH) for i in range(NH)])]
    ppermute x6 -> x10, starting transfers between devices: 17.4 us -> 32.3 us  [the longest x8 26.8 us: along_z(): return lax.ppermute(value, 'z', [(i, (i + step) % NZ) for i in range(NZ)])]
    unnamed x50 -> x68, local copies, waits for them, and re-layouts: 5.24 us -> 15.3 us
    ppermute x12, starting transfers between devices: 15.5 us -> 22.2 us  [turn(): lax.ppermute(value, 'head', [(i, (i + k) % NH) for i in range(NH)])]
    all_to_all x3 -> x4, waiting for transfers between devices: 9.5 us -> 3.26 us  [plain_a2a(): return lax.all_to_all(value, axis, split_axis=0, concat_axis=0, tiled=True)]
    all_to_all x3 -> x4, starting transfers between devices: 25.5 us -> 21.7 us  [plain_a2a(): return lax.all_to_all(value, axis, split_axis=0, concat_axis=0, tiled=True)]
    ppermute x6 -> x10, waiting for transfers between devices: 25.9 us -> 25.8 us  [the longest x8 25.7 us: along_z(): return lax.ppermute(value, 'z', [(i, (i + step) % NZ) for i in range(NZ)])]
  transfers between devices with their start and end apart: 36 -> 41, of which waited for: 17 -> 18; matrix products, arithmetic and copies ran while one was open for 7% -> 7% of each run, Pallas kernels for 14% -> 14%
where the time goes in v4:
time: 301 us; the launch traced here: 300 us
  starting transfers between devices  100 us (33%)
  waiting for transfers between devices  91.3 us (30%)
  Pallas kernels  53.2 us (18%)
  local copies, waits for them, and re-layouts  27.6 us (9%)
  blocking collectives  15.2 us (5%)
  other arithmetic  10.9 us (4%)
    ppermute x8, starting transfers between devices, along_z(): return lax.ppermute(value, 'z', [(i, (i + step) % NZ) for i in range(NZ)])  26.8 us
    ppermute x8, waiting for transfers between devices, along_z(): return lax.ppermute(value, 'z', [(i, (i + step) % NZ) for i in range(NZ)])  25.7 us
    pallas_call x1, Pallas kernels, call_near(): pl.pallas_call(near_kernel, grid_spec=pltpu.PrefetchScalarGridSpec(num_sc...  23.3 us
    ppermute x12, starting transfers between devices, turn(): lax.ppermute(value, 'head', [(i, (i + k) % NH) for i in range(NH)])  22.2 us
    all_to_all x4, starting transfers between devices, plain_a2a(): return lax.all_to_all(value, axis, split_axis=0, concat_axis=0, tiled=True)  21.7 us
    ppermute x7, waiting for transfers between devices, per_device(): dg = dg + lax.ppermute(part, 'z', [(i, 0)]).astype(F32)  19.2 us
    pallas_call x1, Pallas kernels, call_random(): pl.pallas_call(random_kernel, grid_spec=pltpu.PrefetchScalarGridSpec(num_...  15.7 us
    unnamed x68, local copies, waits for them, and re-layouts  15.3 us
  transfers between devices with their start and end apart: 41, of which 18 were waited for; matrix products, arithmetic and copies ran while one was open for 7% of the time, Pallas kernels for 14%

profile of v4, /device:TPU:2, one launch (start us, length us, event | category | flops | bytes accessed | tf_op | source)
XLA Modules:
  0.0 299.7 jit_solution(10843704810279250458)
XLA Ops:
  2.8 4.5 %all-to-all-start = ((bf16[4,2,288,128]{3,2,1,0:T(8,128)(2,1)}), bf16[4,2,288,128]{3,2,1,0:T(8,128)(2,1)}, u32[]{:S(2)}, u32[]{:S(2)}) async-start(bf16[4,2,288,128]{3,2,1,0:T(8,128)(2,1)} %maximum_bitcast_fusion), calls=%async_computation | async-start | bytes 1179648 | tf_op jit(solution)/shard_map/all_to_all | solution.py:359
  7.3 1.4 dynamic-slice_bitcast_fusion.4
  8.7 2.0 collective-permute-start.2
  11.9 3.7 %multiply_reduce_fusion = f32[288,32]{1,0:T(8,128)S(1)} fusion(bf16[288,32,128]{2,1,0:T(8,128)(2,1)} %param.11, bf16[288,32,128]{2,1,0:T(8,128)(2,1)} %param.12), kind=kLoop, calls=%fused_computation | loop fusion | flops 4709376 | bytes 4755456 | tf_op jit(solution)/shard_map/reduce_sum | solution.py:412
  20.2 2.0 collective-permute-start
  22.2 4.0 %collective-permute-start.1 = (bf16[9,2,128,128]{3,2,1,0:T(8,128)(2,1)S(1)}, bf16[9,2,128,128]{3,2,1,0:T(8,128)(2,1)S(1)}, u32[]{:S(2)}, u32[]{:S(2)}) collective-permute-start(bf16[9,2,128,128]{3,2,1,0:T(8,128)(2,1)S(1)} %bitcast.95), channel_id=1, source_target_pairs={{0,224},{32,0},{64,32},{96,64},{128,96},{160,128},{192,160},{224,1... | collective-permute-start | bytes 1769480 | tf_op jit(solution)/shard_map/ppermute | solution.py:379
  26.2 2.3 collective-permute-start.6
  28.6 1.6 collective-permute-done.2.q1
  30.2 8.5 %collective-permute-done.refs_4_ = bf16[9,2,128,128]{3,2,1,0:T(8,128)(2,1)S(1)} collective-permute-done((bf16[9,2,128,128]{3,2,1,0:T(8,128)(2,1)S(1)}, bf16[9,2,128,128]{3,2,1,0:T(8,128)(2,1)S(1)}, u32[]{:S(2)}, u32[]{:S(2)}) %collective-permute-start) | collective-permute-done | bytes 589856 | tf_op jit(solution)/shard_map/ppermute | solution.py:379
  38.7 3.2 %collective-permute-start.5 = (bf16[9,2,128,128]{3,2,1,0:T(8,128)(2,1)S(1)}, bf16[9,2,128,128]{3,2,1,0:T(8,128)(2,1)S(1)}, u32[]{:S(2)}, u32[]{:S(2)}) collective-permute-start(bf16[9,2,128,128]{3,2,1,0:T(8,128)(2,1)S(1)} %collective-permute-done.1.refs_1_), channel_id=1, source_target_pairs={{0,224},{32,0},{64,32},{96,64},{128,96},{160,128},{192,160},{224,1... | collective-permute-start | bytes 1769480 | tf_op jit(solution)/shard_map/ppermute | solution.py:379
  42.7 10.9 %collective-permute-done.4.refs_3_ = bf16[9,2,128,128]{3,2,1,0:T(8,128)(2,1)S(1)} collective-permute-done((bf16[9,2,128,128]{3,2,1,0:T(8,128)(2,1)S(1)}, bf16[9,2,128,128]{3,2,1,0:T(8,128)(2,1)S(1)}, u32[]{:S(2)}, u32[]{:S(2)}) %collective-permute-start.4) | collective-permute-done | bytes 589856 | tf_op jit(solution)/shard_map/ppermute | solution.py:379
  53.6 2.5 select.20
  58.6 4.8 %all-to-all-start.1 = ((bf16[40,2,128,128]{3,2,1,0:T(8,128)(2,1)}), bf16[40,2,128,128]{3,2,1,0:T(8,128)(2,1)}, u32[]{:S(2)}, u32[]{:S(2)}) async-start(bf16[40,2,128,128]{3,2,1,0:T(8,128)(2,1)} %select.20), calls=%async_computation.1 | async-start | bytes 5242880 | tf_op jit(solution)/shard_map/all_to_all | solution.py:359
  63.4 1.9 dynamic-slice_bitcast_fusion
  65.3 1.5 collective-permute-start.10
  67.4 1.9 collective-permute-start.7
  70.7 3.9 %collective-permute-start.13 = (bf16[2304,128]{1,0:T(8,128)(2,1)S(1)}, bf16[2304,128]{1,0:T(8,128)(2,1)S(1)}, u32[]{:S(2)}, u32[]{:S(2)}) collective-permute-start(bf16[2304,128]{1,0:T(8,128)(2,1)S(1)} %get-tuple-element.105), channel_id=1, source_target_pairs={{0,2},{1,3},{2,0},{3,1},{4,6},{5,7},{6,4},{7,5},{8,10},{9,11},{10,... | collective-permute-start | bytes 1769480 | tf_op jit(solution)/shard_map/ppermute | solution.py:363
  74.5 7.0 %collective-permute-done.10.d3 = bf16[2304,128]{1,0:T(8,128)(2,1)S(1)} collective-permute-done((bf16[2304,128]{1,0:T(8,128)(2,1)S(1)}, bf16[2304,128]{1,0:T(8,128)(2,1)S(1)}, u32[]{:S(2)}, u32[]{:S(2)}) %collective-permute-start.10) | collective-permute-done | bytes 589856 | tf_op jit(solution)/shard_map/ppermute | solution.py:363
  81.6 1.8 collective-permute-done.9.d1
  85.1 14.3 %collective-permute-start.11 = (bf16[5,2,128,128]{3,2,1,0:T(8,128)(2,1)S(1)}, bf16[5,2,128,128]{3,2,1,0:T(8,128)(2,1)S(1)}, u32[]{:S(2)}, u32[]{:S(2)}) collective-permute-start(bf16[5,2,128,128]{3,2,1,0:T(8,128)(2,1)S(1)} %slice.50), channel_id=1, source_target_pairs={{0,32},{32,64},{64,96},{96,128},{128,160},{160,192},{192,224},{224... | collective-permute-start | bytes 983048 | tf_op jit(solution)/shard_map/ppermute | solution.py:379
  100.2 6.4 %collective-permute-done.12.refs_3_ = bf16[4,2,128,128]{3,2,1,0:T(8,128)(2,1)S(1)} collective-permute-done((bf16[4,2,128,128]{3,2,1,0:T(8,128)(2,1)S(1)}, bf16[4,2,128,128]{3,2,1,0:T(8,128)(2,1)S(1)}, u32[]{:S(2)}, u32[]{:S(2)}) %collective-permute-start.12) | collective-permute-done | bytes 262176 | tf_op jit(solution)/shard_map/ppermute | solution.py:379
  112.1 1.9 select.21
  114.0 5.4 %all-to-all-start.2 = ((bf16[24,2,128,128]{3,2,1,0:T(8,128)(2,1)}), bf16[24,2,128,128]{3,2,1,0:T(8,128)(2,1)}, u32[]{:S(2)}, u32[]{:S(2)}) async-start(bf16[24,2,128,128]{3,2,1,0:T(8,128)(2,1)} %select.21), calls=%async_computation.2 | async-start | bytes 3145728 | tf_op jit(solution)/shard_map/all_to_all | solution.py:359
  120.8 2.6 collective-permute-start.16
  125.8 1.4 pad_maximum_fusion.1
  127.3 1.5 rev.3
  129.5 1.9 collective-permute-start.17
  131.4 3.6 %collective-permute-start.18 = (bf16[1,2,128,128]{3,2,1,0:T(8,128)(2,1)}, bf16[1,2,128,128]{3,2,1,0:T(8,128)(2,1)}, u32[]{:S(2)}, u32[]{:S(2)}) collective-permute-start(bf16[1,2,128,128]{3,2,1,0:T(8,128)(2,1)} %get-tuple-element.117), channel_id=1, source_target_pairs={{4,0},{8,4},{12,8},{16,12},{20,16},{24,20},{28,24},{32,28},{36,32}... | collective-permute-start | bytes 196616 | tf_op jit(solution)/shard_map/ppermute | solution.py:432
  136.6 3.3 %all-to-all-done.2.far_ref = bf16[24,2,128,128]{3,2,1,0:T(8,128)(2,1)} async-done(((bf16[24,2,128,128]{3,2,1,0:T(8,128)(2,1)}), bf16[24,2,128,128]{3,2,1,0:T(8,128)(2,1)}, u32[]{:S(2)}, u32[]{:S(2)}) %all-to-all-start.2) | async-done | bytes 1572896 | tf_op jit(solution)/shard_map/all_to_all | solution.py:359
  141.8 15.7 %random.1 = (f32[9,128,1024]{2,1,0:T(8,128)}, bf16[64,2,128,128]{3,2,1,0:T(8,128)(2,1)}) custom-call(s32[158]{0:T(256)S(1)} %concatenate.11.meta, bf16[2304,128]{1,0:T(8,128)(2,1)S(1)} %get-tuple-element.112.q0, bf16[2304,128]{1,0:T(8,128)(2,1)S(1)} %collective-permute-done.2.q1, bf16[2304,128]{1,0:T(8,128)(2,1)S(1)} %collective-permute-done.6.q2, ...), custom_call_target="tpu_custom_call" | custom-call | tf_op jit(solution)/shard_map/random/pallas_call | solution.py:278
  157.6 7.0 %all-to-all-start.3 = ((bf16[64,2,128,128]{3,2,1,0:T(8,128)(2,1)}), bf16[64,2,128,128]{3,2,1,0:T(8,128)(2,1)}, u32[]{:S(2)}, u32[]{:S(2)}) async-start(bf16[64,2,128,128]{3,2,1,0:T(8,128)(2,1)} %get-tuple-element.88), calls=%async_computation.3 | async-start | bytes 8388608 | tf_op jit(solution)/shard_map/all_to_all | solution.py:359
  168.0 11.6 %collective-permute-done.20 = bf16[4,128,128]{2,1,0:T(8,128)(2,1)S(1)} collective-permute-done((bf16[4,128,128]{2,1,0:T(8,128)(2,1)S(1)}, bf16[4,128,128]{2,1,0:T(8,128)(2,1)S(1)}, u32[]{:S(2)}, u32[]{:S(2)}) %collective-permute-start.20) | collective-permute-done | bytes 131104 | tf_op jit(solution)/shard_map/ppermute | solution.py:385
  180.9 1.8 pad_maximum_fusion.kv_ref
  182.7 3.3 %collective-permute-done.21 = bf16[4,128,128]{2,1,0:T(8,128)(2,1)S(1)} collective-permute-done((bf16[4,128,128]{2,1,0:T(8,128)(2,1)S(1)}, bf16[4,128,128]{2,1,0:T(8,128)(2,1)S(1)}, u32[]{:S(2)}, u32[]{:S(2)}) %collective-permute-start.21) | collective-permute-done | bytes 131104 | tf_op jit(solution)/shard_map/ppermute | solution.py:385
  186.0 23.3 %near.1 = (bf16[2304,128]{1,0:T(8,128)(2,1)S(1)}, bf16[2304,128]{1,0:T(8,128)(2,1)S(1)}, bf16[2304,128]{1,0:T(8,128)(2,1)S(1)}, bf16[2304,128]{1,0:T(8,128)(2,1)...) custom-call(s32[158]{0:T(256)S(1)} %concatenate.11.meta, bf16[2304,128]{1,0:T(8,128)(2,1)S(1)} %get-tuple-element.112.q0, ...), custom_call_target="tpu_custom_call" | custom-call | tf_op jit(solution)/shard_map/near/pallas_call | solution.py:256
  211.3 3.9 %collective-permute-start.23 = (bf16[2304,128]{1,0:T(8,128)(2,1)S(1)}, bf16[2304,128]{1,0:T(8,128)(2,1)S(1)}, u32[]{:S(2)}, u32[]{:S(2)}) collective-permute-start(bf16[2304,128]{1,0:T(8,128)(2,1)S(1)} %get-tuple-element.78), channel_id=1, source_target_pairs={{0,2},{1,3},{2,0},{3,1},{4,6},{5,7},{6,4},{7,5},{8,10},{9,11},{10,... | collective-permute-start | bytes 1769480 | tf_op jit(solution)/shard_map/ppermute | solution.py:363
  215.2 2.2 collective-permute-start.24
  217.4 6.6 %collective-permute-done.25 = f32[2,2,128,128]{3,2,1,0:T(8,128)S(1)} collective-permute-done((f32[2,2,128,128]{3,2,1,0:T(8,128)S(1)}, f32[2,2,128,128]{3,2,1,0:T(8,128)S(1)}, u32[]{:S(2)}, u32[]{:S(2)}) %collective-permute-start.25) | collective-permute-done | bytes 262176 | tf_op jit(solution)/shard_map/ppermute | solution.py:394
  224.0 5.2 %collective-permute-start.26 = (f32[2,2,128,128]{3,2,1,0:T(8,128)S(1)}, f32[2,2,128,128]{3,2,1,0:T(8,128)S(1)}, u32[]{:S(2)}, u32[]{:S(2)}) collective-permute-start(f32[2,2,128,128]{3,2,1,0:T(8,128)S(1)} %add.141), channel_id=1, source_target_pairs={{8,0},{12,4},{9,1},{13,5},{10,2},{14,6},{11,3},{15,7},{40,32},{44,... | collective-permute-start | bytes 786440 | tf_op jit(solution)/shard_map/ppermute | solution.py:394
  229.3 8.6 %collective-permute-done.26 = f32[2,2,128,128]{3,2,1,0:T(8,128)S(1)} collective-permute-done((f32[2,2,128,128]{3,2,1,0:T(8,128)S(1)}, f32[2,2,128,128]{3,2,1,0:T(8,128)S(1)}, u32[]{:S(2)}, u32[]{:S(2)}) %collective-permute-start.26) | collective-permute-done | bytes 262176 | tf_op jit(solution)/shard_map/ppermute | solution.py:394
  239.9 4.2 %join.1 = bf16[288,4,8,128]{3,2,1,0:T(8,128)(2,1)} custom-call(s32[1]{0:T(128)} %bitcast.head, bf16[288,8,128]{2,1,0:T(8,128)(2,1)} %bitcast.101, bf16[288,8,128]{2,1,0:T(8,128)(2,1)} %bitcast.107, bf16[288,8,128]{2,1,0:T(8,128)(2,1)} %bitcast.108, bf16[288,8,128]{2,1,0:T(8,128)(2,1)} %bitcast.109), custom_call_target="tpu_custom_call" | custom-call | tf_op jit(solution)/shard_map/join/pallas_call | solution.py:345
  250.7 14.3 %collective-permute-done.30 = bf16[2,2,128,128]{3,2,1,0:T(8,128)(2,1)S(1)} collective-permute-done((bf16[2,2,128,128]{3,2,1,0:T(8,128)(2,1)S(1)}, bf16[2,2,128,128]{3,2,1,0:T(8,128)(2,1)S(1)}, u32[]{:S(2)}, u32[]{:S(2)}) %collective-permute-start.30) | collective-permute-done | bytes 131104 | tf_op jit(solution)/shard_map/ppermute | solution.py:453
  267.7 2.0 collective-permute-start.28
  269.7 2.3 collective-permute-start.29
  272.1 2.1 collective-permute-done.35
  274.2 2.7 collective-permute-done.36
  277.1 5.6 %collect.1 = bf16[9,2,128,128]{3,2,1,0:T(8,128)(2,1)S(1)} custom-call(s32[158]{0:T(256)S(1)} %concatenate.11.meta, bf16[64,2,128,128]{3,2,1,0:T(8,128)(2,1)} %all-to-all-done.3.got, f32[11,2,128,128]{3,2,1,0:T(8,128)S(1)} %copy-done, bf16[1,2,128,128]{3,2,1,0:T(8,128)(2,1)S(1)} %collective-permute-done.28.lower, ...), custom_call_target="tpu_custom_call" | custom-call | tf_op jit(solution)/shard_map/collect/pallas_call | solution.py:323
  282.7 15.2 %all_to_all.25 = bf16[4,2,288,128]{3,2,1,0:T(8,128)(2,1)S(1)} all-to-all(bf16[4,2,288,128]{3,2,1,0:T(8,128)(2,1)S(1)} %copy.111), channel_id=1, replica_groups=mesh['z'=8,'x'=4,'c'=2,'head'=4] {'head'}, dimensions={0} | all-to-all | bytes 1179648 | tf_op jit(solution)/shard_map/all_to_all | solution.py:359
  (159 shorter events, 48.6 us)
Async XLA Ops:
  2.8 16.3 %all-to-all-start = ((bf16[4,2,288,128]{3,2,1,0:T(8,128)(2,1)}), bf16[4,2,288,128]{3,2,1,0:T(8,128)(2,1)}, u32[]{:S(2)}, u32[]{:S(2)}) async-start(bf16[4,2,288,128]{3,2,1,0:T(8,128)(2,1)} %maximum_bitcast_fusion), calls=%async_computation | async-start | bytes 1179648 | tf_op jit(solution)/shard_map/all_to_all | solution.py:359
  8.7 21.5 %collective-permute-start.2 = (bf16[2304,128]{1,0:T(8,128)(2,1)}, bf16[2304,128]{1,0:T(8,128)(2,1)S(1)}, u32[]{:S(2)}, u32[]{:S(2)}) collective-permute-start(bf16[2304,128]{1,0:T(8,128)(2,1)} %get-tuple-element.111), channel_id=1, source_target_pairs={{0,1},{1,2},{2,3},{3,0},{4,5},{5,6},{6,7},{7,4},{8,9},{9,10},{10,1... | collective-permute-start | bytes 1769480 | tf_op jit(solution)/shard_map/ppermute | solution.py:363
  10.7 19.5 %collective-permute-start.3 = (bf16[2304,128]{1,0:T(8,128)(2,1)}, bf16[2304,128]{1,0:T(8,128)(2,1)S(1)}, u32[]{:S(2)}, u32[]{:S(2)}) collective-permute-start(bf16[2304,128]{1,0:T(8,128)(2,1)} %get-tuple-element.110), channel_id=1, source_target_pairs={{0,3},{1,0},{2,1},{3,2},{4,7},{5,4},{6,5},{7,6},{8,11},{9,8},{10,9... | collective-permute-start | bytes 1769480 | tf_op jit(solution)/shard_map/ppermute | solution.py:363
  20.2 18.5 %collective-permute-start = (bf16[9,2,128,128]{3,2,1,0:T(8,128)(2,1)S(1)}, bf16[9,2,128,128]{3,2,1,0:T(8,128)(2,1)S(1)}, u32[]{:S(2)}, u32[]{:S(2)}) collective-permute-start(bf16[9,2,128,128]{3,2,1,0:T(8,128)(2,1)S(1)} %bitcast.94), channel_id=1, source_target_pairs={{0,32},{32,64},{64,96},{96,128},{128,160},{160,192},{192,224},{224... | collective-permute-start | bytes 1769480 | tf_op jit(solution)/shard_map/ppermute | solution.py:379
  22.2 16.5 %collective-permute-start.1 = (bf16[9,2,128,128]{3,2,1,0:T(8,128)(2,1)S(1)}, bf16[9,2,128,128]{3,2,1,0:T(8,128)(2,1)S(1)}, u32[]{:S(2)}, u32[]{:S(2)}) collective-permute-start(bf16[9,2,128,128]{3,2,1,0:T(8,128)(2,1)S(1)} %bitcast.95), channel_id=1, source_target_pairs={{0,224},{32,0},{64,32},{96,64},{128,96},{160,128},{192,160},{224,1... | collective-permute-start | bytes 1769480 | tf_op jit(solution)/shard_map/ppermute | solution.py:379
  26.2 16.5 %collective-permute-start.6 = (bf16[2304,128]{1,0:T(8,128)(2,1)}, bf16[2304,128]{1,0:T(8,128)(2,1)S(1)}, u32[]{:S(2)}, u32[]{:S(2)}) collective-permute-start(bf16[2304,128]{1,0:T(8,128)(2,1)} %get-tuple-element.109), channel_id=1, source_target_pairs={{0,2},{1,3},{2,0},{3,1},{4,6},{5,7},{6,4},{7,5},{8,10},{9,11},{10,... | collective-permute-start | bytes 1769480 | tf_op jit(solution)/shard_map/ppermute | solution.py:363
  30.2 109.7 %copy-start.2 = (bf16[2304,128]{1,0:T(8,128)(2,1)}, bf16[2304,128]{1,0:T(8,128)(2,1)S(1)}, u32[]{:S(2)}) copy-start(bf16[2304,128]{1,0:T(8,128)(2,1)S(1)} %collective-permute-done.3.q3) | copy-start | bytes 1769476
  38.7 17.3 %copy-start.11 = (bf16[9,2,128,128]{3,2,1,0:T(8,128)(2,1)}, bf16[9,2,128,128]{3,2,1,0:T(8,128)(2,1)S(1)}, u32[]{:S(2)}) copy-start(bf16[9,2,128,128]{3,2,1,0:T(8,128)(2,1)S(1)} %collective-permute-done.1.refs_1_) | copy-start | bytes 1769476
  38.7 14.9 %collective-permute-start.4 = (bf16[9,2,128,128]{3,2,1,0:T(8,128)(2,1)S(1)}, bf16[9,2,128,128]{3,2,1,0:T(8,128)(2,1)S(1)}, u32[]{:S(2)}, u32[]{:S(2)}) collective-permute-start(bf16[9,2,128,128]{3,2,1,0:T(8,128)(2,1)S(1)} %collective-permute-done.refs_4_), channel_id=1, source_target_pairs={{0,32},{32,64},{64,96},{96,128},{128,160},{160,192},{192,224},{224... | collective-permute-start | bytes 1769480 | tf_op jit(solution)/shard_map/ppermute | solution.py:379
  38.7 14.9 %collective-permute-start.5 = (bf16[9,2,128,128]{3,2,1,0:T(8,128)(2,1)S(1)}, bf16[9,2,128,128]{3,2,1,0:T(8,128)(2,1)S(1)}, u32[]{:S(2)}, u32[]{:S(2)}) collective-permute-start(bf16[9,2,128,128]{3,2,1,0:T(8,128)(2,1)S(1)} %collective-permute-done.1.refs_1_), channel_id=1, source_target_pairs={{0,224},{32,0},{64,32},{96,64},{128,96},{160,128},{192,160},{224,1... | collective-permute-start | bytes 1769480 | tf_op jit(solution)/shard_map/ppermute | solution.py:379
  42.7 97.1 %copy-start.3 = (bf16[2304,128]{1,0:T(8,128)(2,1)}, bf16[2304,128]{1,0:T(8,128)(2,1)S(1)}, u32[]{:S(2)}) copy-start(bf16[2304,128]{1,0:T(8,128)(2,1)S(1)} %collective-permute-done.6.q2) | copy-start | bytes 1769476
  58.6 49.5 %all-to-all-start.1 = ((bf16[40,2,128,128]{3,2,1,0:T(8,128)(2,1)}), bf16[40,2,128,128]{3,2,1,0:T(8,128)(2,1)}, u32[]{:S(2)}, u32[]{:S(2)}) async-start(bf16[40,2,128,128]{3,2,1,0:T(8,128)(2,1)} %select.20), calls=%async_computation.1 | async-start | bytes 5242880 | tf_op jit(solution)/shard_map/all_to_all | solution.py:359
  65.3 74.5 %copy-start.1 = (bf16[2304,128]{1,0:T(8,128)(2,1)}, bf16[2304,128]{1,0:T(8,128)(2,1)S(1)}, u32[]{:S(2)}) copy-start(bf16[2304,128]{1,0:T(8,128)(2,1)S(1)} %get-tuple-element.108.d0) | copy-start | bytes 1769476
  65.3 16.2 %collective-permute-start.10 = (bf16[2304,128]{1,0:T(8,128)(2,1)S(1)}, bf16[2304,128]{1,0:T(8,128)(2,1)S(1)}, u32[]{:S(2)}, u32[]{:S(2)}) collective-permute-start(bf16[2304,128]{1,0:T(8,128)(2,1)S(1)} %get-tuple-element.106), channel_id=1, source_target_pairs={{0,3},{1,0},{2,1},{3,2},{4,7},{5,4},{6,5},{7,6},{8,11},{9,8},{10,9... | collective-permute-start | bytes 1769480 | tf_op jit(solution)/shard_map/ppermute | solution.py:363
  66.9 16.6 %collective-permute-start.9 = (bf16[2304,128]{1,0:T(8,128)(2,1)S(1)}, bf16[2304,128]{1,0:T(8,128)(2,1)S(1)}, u32[]{:S(2)}, u32[]{:S(2)}) collective-permute-start(bf16[2304,128]{1,0:T(8,128)(2,1)S(1)} %get-tuple-element.107), channel_id=1, source_target_pairs={{0,1},{1,2},{2,3},{3,0},{4,5},{5,6},{6,7},{7,4},{8,9},{9,10},{10,1... | collective-permute-start | bytes 1769480 | tf_op jit(solution)/shard_map/ppermute | solution.py:363
  67.4 16.8 %collective-permute-start.7 = (bf16[9,2,128,128]{3,2,1,0:T(8,128)(2,1)S(1)}, bf16[9,2,128,128]{3,2,1,0:T(8,128)(2,1)S(1)}, u32[]{:S(2)}, u32[]{:S(2)}) collective-permute-start(bf16[9,2,128,128]{3,2,1,0:T(8,128)(2,1)S(1)} %copy-done.13), channel_id=1, source_target_pairs={{0,32},{32,64},{64,96},{96,128},{128,160},{160,192},{192,224},{224... | collective-permute-start | bytes 1769480 | tf_op jit(solution)/shard_map/ppermute | solution.py:379
  69.3 14.9 %collective-permute-start.8 = (bf16[9,2,128,128]{3,2,1,0:T(8,128)(2,1)S(1)}, bf16[9,2,128,128]{3,2,1,0:T(8,128)(2,1)S(1)}, u32[]{:S(2)}, u32[]{:S(2)}) collective-permute-start(bf16[9,2,128,128]{3,2,1,0:T(8,128)(2,1)S(1)} %copy-done.15), channel_id=1, source_target_pairs={{0,224},{32,0},{64,32},{96,64},{128,96},{160,128},{192,160},{224,1... | collective-permute-start | bytes 1769480 | tf_op jit(solution)/shard_map/ppermute | solution.py:379
  70.7 29.5 %collective-permute-start.13 = (bf16[2304,128]{1,0:T(8,128)(2,1)S(1)}, bf16[2304,128]{1,0:T(8,128)(2,1)S(1)}, u32[]{:S(2)}, u32[]{:S(2)}) collective-permute-start(bf16[2304,128]{1,0:T(8,128)(2,1)S(1)} %get-tuple-element.105), channel_id=1, source_target_pairs={{0,2},{1,3},{2,0},{3,1},{4,6},{5,7},{6,4},{7,5},{8,10},{9,11},{10,... | collective-permute-start | bytes 1769480 | tf_op jit(solution)/shard_map/ppermute | solution.py:363
  81.6 25.0 %copy-start.24 = (bf16[2304,128]{1,0:T(8,128)(2,1)}, bf16[2304,128]{1,0:T(8,128)(2,1)S(1)}, u32[]{:S(2)}) copy-start(bf16[2304,128]{1,0:T(8,128)(2,1)S(1)} %collective-permute-done.10.d3) | copy-start | bytes 1769476
  85.1 22.2 %collective-permute-start.11 = (bf16[5,2,128,128]{3,2,1,0:T(8,128)(2,1)S(1)}, bf16[5,2,128,128]{3,2,1,0:T(8,128)(2,1)S(1)}, u32[]{:S(2)}, u32[]{:S(2)}) collective-permute-start(bf16[5,2,128,128]{3,2,1,0:T(8,128)(2,1)S(1)} %slice.50), channel_id=1, source_target_pairs={{0,32},{32,64},{64,96},{96,128},{128,160},{160,192},{192,224},{224... | collective-permute-start | bytes 983048 | tf_op jit(solution)/shard_map/ppermute | solution.py:379
  100.2 6.4 %collective-permute-start.12 = (bf16[4,2,128,128]{3,2,1,0:T(8,128)(2,1)S(1)}, bf16[4,2,128,128]{3,2,1,0:T(8,128)(2,1)S(1)}, u32[]{:S(2)}, u32[]{:S(2)}) collective-permute-start(bf16[4,2,128,128]{3,2,1,0:T(8,128)(2,1)S(1)} %slice.51), channel_id=1, source_target_pairs={{0,224},{32,0},{64,32},{96,64},{128,96},{160,128},{192,160},{224,1... | collective-permute-start | bytes 786440 | tf_op jit(solution)/shard_map/ppermute | solution.py:379
  114.0 25.8 %all-to-all-start.2 = ((bf16[24,2,128,128]{3,2,1,0:T(8,128)(2,1)}), bf16[24,2,128,128]{3,2,1,0:T(8,128)(2,1)}, u32[]{:S(2)}, u32[]{:S(2)}) async-start(bf16[24,2,128,128]{3,2,1,0:T(8,128)(2,1)} %select.21), calls=%async_computation.2 | async-start | bytes 3145728 | tf_op jit(solution)/shard_map/all_to_all | solution.py:359
  119.5 5.3 %collective-permute-start.14 = (f32[2,18,128]{2,0,1:T(2,128)}, f32[2,18,128]{2,0,1:T(2,128)}, u32[]{:S(2)}, u32[]{:S(2)}) collective-permute-start(f32[2,18,128]{2,0,1:T(2,128)} %get-tuple-element.62), channel_id=1, source_target_pairs={{0,1},{1,2},{2,3},{3,0},{4,5},{5,6},{6,7},{7,4},{8,9},{9,10},{10,1... | collective-permute-start | bytes 55304 | tf_op jit(solution)/shard_map/ppermute | solution.py:363
  119.5 5.6 %collective-permute-start.15 = (f32[2,18,128]{2,0,1:T(2,128)}, f32[2,18,128]{2,0,1:T(2,128)}, u32[]{:S(2)}, u32[]{:S(2)}) collective-permute-start(f32[2,18,128]{2,0,1:T(2,128)} %get-tuple-element.63), channel_id=1, source_target_pairs={{0,2},{1,3},{2,0},{3,1},{4,6},{5,7},{6,4},{7,5},{8,10},{9,11},{10,... | collective-permute-start | bytes 55304 | tf_op jit(solution)/shard_map/ppermute | solution.py:363
  120.8 5.0 %collective-permute-start.16 = (f32[2,18,128]{2,0,1:T(2,128)}, f32[2,18,128]{2,0,1:T(2,128)}, u32[]{:S(2)}, u32[]{:S(2)}) collective-permute-start(f32[2,18,128]{2,0,1:T(2,128)} %get-tuple-element.64), channel_id=1, source_target_pairs={{0,3},{1,0},{2,1},{3,2},{4,7},{5,4},{6,5},{7,6},{8,11},{9,8},{10,9... | collective-permute-start | bytes 55304 | tf_op jit(solution)/shard_map/ppermute | solution.py:363
  129.5 28.1 %collective-permute-start.17 = (bf16[1,2,128,128]{3,2,1,0:T(8,128)(2,1)}, bf16[1,2,128,128]{3,2,1,0:T(8,128)(2,1)}, u32[]{:S(2)}, u32[]{:S(2)}) collective-permute-start(bf16[1,2,128,128]{3,2,1,0:T(8,128)(2,1)} %get-tuple-element.118), channel_id=1, source_target_pairs={{0,4},{4,8},{8,12},{12,16},{16,20},{20,24},{24,28},{28,32},{32,36}... | collective-permute-start | bytes 196616 | tf_op jit(solution)/shard_map/ppermute | solution.py:431
  131.4 26.2 %collective-permute-start.18 = (bf16[1,2,128,128]{3,2,1,0:T(8,128)(2,1)}, bf16[1,2,128,128]{3,2,1,0:T(8,128)(2,1)}, u32[]{:S(2)}, u32[]{:S(2)}) collective-permute-start(bf16[1,2,128,128]{3,2,1,0:T(8,128)(2,1)} %get-tuple-element.117), channel_id=1, source_target_pairs={{4,0},{8,4},{12,8},{16,12},{20,16},{24,20},{28,24},{32,28},{36,32}... | collective-permute-start | bytes 196616 | tf_op jit(solution)/shard_map/ppermute | solution.py:432
  157.6 119.5 %all-to-all-start.3 = ((bf16[64,2,128,128]{3,2,1,0:T(8,128)(2,1)}), bf16[64,2,128,128]{3,2,1,0:T(8,128)(2,1)}, u32[]{:S(2)}, u32[]{:S(2)}) async-start(bf16[64,2,128,128]{3,2,1,0:T(8,128)(2,1)} %get-tuple-element.88), calls=%async_computation.3 | async-start | bytes 8388608 | tf_op jit(solution)/shard_map/all_to_all | solution.py:359
  164.6 21.4 %copy-start.17 = (f32[2,9,8,128]{3,2,1,0:T(8,128)S(1)}, f32[2,9,8,128]{3,2,1,0:T(8,128)}, u32[]{:S(2)}) copy-start(f32[2,9,8,128]{3,2,1,0:T(8,128)} %copy.109.ld_ref) | copy-start | bytes 221188
  165.9 0.7 collective-permute-start.19
  166.7 12.9 %collective-permute-start.20 = (bf16[4,128,128]{2,1,0:T(8,128)(2,1)S(1)}, bf16[4,128,128]{2,1,0:T(8,128)(2,1)S(1)}, u32[]{:S(2)}, u32[]{:S(2)}) collective-permute-start(bf16[4,128,128]{2,1,0:T(8,128)(2,1)S(1)} %broadcast_select_fusion), channel_id=1, source_target_pairs={{0,8},{4,12},{1,9},{5,13},{2,10},{6,14},{3,11},{7,15},{32,40},{36,... | collective-permute-start | bytes 393224 | tf_op jit(solution)/shard_map/ppermute | solution.py:385
  179.6 6.4 %collective-permute-start.21 = (bf16[4,128,128]{2,1,0:T(8,128)(2,1)S(1)}, bf16[4,128,128]{2,1,0:T(8,128)(2,1)S(1)}, u32[]{:S(2)}, u32[]{:S(2)}) collective-permute-start(bf16[4,128,128]{2,1,0:T(8,128)(2,1)S(1)} %broadcast_select_fusion.1), channel_id=1, source_target_pairs={{0,16},{4,20},{8,24},{12,28},{1,17},{5,21},{9,25},{13,29},{2,18},{... | collective-permute-start | bytes 393224 | tf_op jit(solution)/shard_map/ppermute | solution.py:385
  209.4 29.4 %copy-start.20 = (bf16[2304,128]{1,0:T(8,128)(2,1)}, bf16[2304,128]{1,0:T(8,128)(2,1)S(1)}, u32[]{:S(2)}) copy-start(bf16[2304,128]{1,0:T(8,128)(2,1)S(1)} %get-tuple-element.81) | copy-start | bytes 1769476
  209.4 14.6 %collective-permute-start.25 = (f32[2,2,128,128]{3,2,1,0:T(8,128)S(1)}, f32[2,2,128,128]{3,2,1,0:T(8,128)S(1)}, u32[]{:S(2)}, u32[]{:S(2)}) collective-permute-start(f32[2,2,128,128]{3,2,1,0:T(8,128)S(1)} %get-tuple-element.80), channel_id=1, source_target_pairs={{16,0},{20,4},{24,8},{28,12},{17,1},{21,5},{25,9},{29,13},{18,2},{... | collective-permute-start | bytes 786440 | tf_op jit(solution)/shard_map/ppermute | solution.py:394
  210.7 28.0 %collective-permute-start.22 = (bf16[2304,128]{1,0:T(8,128)(2,1)S(1)}, bf16[2304,128]{1,0:T(8,128)(2,1)S(1)}, u32[]{:S(2)}, u32[]{:S(2)}) collective-permute-start(bf16[2304,128]{1,0:T(8,128)(2,1)S(1)} %get-tuple-element.77), channel_id=1, source_target_pairs={{0,1},{1,2},{2,3},{3,0},{4,5},{5,6},{6,7},{7,4},{8,9},{9,10},{10,1... | collective-permute-start | bytes 1769480 | tf_op jit(solution)/shard_map/ppermute | solution.py:363
  211.3 27.4 %collective-permute-start.23 = (bf16[2304,128]{1,0:T(8,128)(2,1)S(1)}, bf16[2304,128]{1,0:T(8,128)(2,1)S(1)}, u32[]{:S(2)}, u32[]{:S(2)}) collective-permute-start(bf16[2304,128]{1,0:T(8,128)(2,1)S(1)} %get-tuple-element.78), channel_id=1, source_target_pairs={{0,2},{1,3},{2,0},{3,1},{4,6},{5,7},{6,4},{7,5},{8,10},{9,11},{10,... | collective-permute-start | bytes 1769480 | tf_op jit(solution)/shard_map/ppermute | solution.py:363
  215.2 23.5 %collective-permute-start.24 = (bf16[2304,128]{1,0:T(8,128)(2,1)S(1)}, bf16[2304,128]{1,0:T(8,128)(2,1)S(1)}, u32[]{:S(2)}, u32[]{:S(2)}) collective-permute-start(bf16[2304,128]{1,0:T(8,128)(2,1)S(1)} %get-tuple-element.79), channel_id=1, source_target_pairs={{0,3},{1,0},{2,1},{3,2},{4,7},{5,4},{6,5},{7,6},{8,11},{9,8},{10,9... | collective-permute-start | bytes 1769480 | tf_op jit(solution)/shard_map/ppermute | solution.py:363
  224.0 13.9 %collective-permute-start.26 = (f32[2,2,128,128]{3,2,1,0:T(8,128)S(1)}, f32[2,2,128,128]{3,2,1,0:T(8,128)S(1)}, u32[]{:S(2)}, u32[]{:S(2)}) collective-permute-start(f32[2,2,128,128]{3,2,1,0:T(8,128)S(1)} %add.141), channel_id=1, source_target_pairs={{8,0},{12,4},{9,1},{13,5},{10,2},{14,6},{11,3},{15,7},{40,32},{44,... | collective-permute-start | bytes 786440 | tf_op jit(solution)/shard_map/ppermute | solution.py:394
  237.9 0.7 collective-permute-start.27
  244.1 20.9 %collective-permute-start.30 = (bf16[2,2,128,128]{3,2,1,0:T(8,128)(2,1)S(1)}, bf16[2,2,128,128]{3,2,1,0:T(8,128)(2,1)S(1)}, u32[]{:S(2)}, u32[]{:S(2)}) collective-permute-start(bf16[2,2,128,128]{3,2,1,0:T(8,128)(2,1)S(1)} %convert_element_type.34), channel_id=1, source_target_pairs={{32,0},{33,1},{34,2},{35,3},{36,4},{37,5},{38,6},{39,7},{40,8},{41... | collective-permute-start | bytes 393224 | tf_op jit(solution)/shard_map/ppermute | solution.py:453
  245.4 20.9 %collective-permute-start.31 = (bf16[2,2,128,128]{3,2,1,0:T(8,128)(2,1)S(1)}, bf16[2,2,128,128]{3,2,1,0:T(8,128)(2,1)S(1)}, u32[]{:S(2)}, u32[]{:S(2)}) collective-permute-start(bf16[2,2,128,128]{3,2,1,0:T(8,128)(2,1)S(1)} %convert_element_type.34), channel_id=1, source_target_pairs={{64,0},{65,1},{66,2},{67,3},{68,4},{69,5},{70,6},{71,7},{72,8},{73... | collective-permute-start | bytes 393224 | tf_op jit(solution)/shard_map/ppermute | solution.py:453
  246.7 21.0 %collective-permute-start.32 = (bf16[2,2,128,128]{3,2,1,0:T(8,128)(2,1)S(1)}, bf16[2,2,128,128]{3,2,1,0:T(8,128)(2,1)S(1)}, u32[]{:S(2)}, u32[]{:S(2)}) collective-permute-start(bf16[2,2,128,128]{3,2,1,0:T(8,128)(2,1)S(1)} %convert_element_type.34), channel_id=1, source_target_pairs={{96,0},{97,1},{98,2},{99,3},{100,4},{101,5},{102,6},{103,7},{104,8... | collective-permute-start | bytes 393224 | tf_op jit(solution)/shard_map/ppermute | solution.py:453
  248.0 21.7 %collective-permute-start.33 = (bf16[2,2,128,128]{3,2,1,0:T(8,128)(2,1)S(1)}, bf16[2,2,128,128]{3,2,1,0:T(8,128)(2,1)S(1)}, u32[]{:S(2)}, u32[]{:S(2)}) collective-permute-start(bf16[2,2,128,128]{3,2,1,0:T(8,128)(2,1)S(1)} %convert_element_type.34), channel_id=1, source_target_pairs={{128,0},{129,1},{130,2},{131,3},{132,4},{133,5},{134,6},{135,7},{1... | collective-permute-start | bytes 393224 | tf_op jit(solution)/shard_map/ppermute | solution.py:453
  249.3 22.7 %collective-permute-start.34 = (bf16[2,2,128,128]{3,2,1,0:T(8,128)(2,1)S(1)}, bf16[2,2,128,128]{3,2,1,0:T(8,128)(2,1)S(1)}, u32[]{:S(2)}, u32[]{:S(2)}) collective-permute-start(bf16[2,2,128,128]{3,2,1,0:T(8,128)(2,1)S(1)} %convert_element_type.34), channel_id=1, source_target_pairs={{160,0},{161,1},{162,2},{163,3},{164,4},{165,5},{166,6},{167,7},{1... | collective-permute-start | bytes 393224 | tf_op jit(solution)/shard_map/ppermute | solution.py:453
  265.1 9.1 %collective-permute-start.35 = (bf16[2,2,128,128]{3,2,1,0:T(8,128)(2,1)S(1)}, bf16[2,2,128,128]{3,2,1,0:T(8,128)(2,1)S(1)}, u32[]{:S(2)}, u32[]{:S(2)}) collective-permute-start(bf16[2,2,128,128]{3,2,1,0:T(8,128)(2,1)S(1)} %convert_element_type.34), channel_id=1, source_target_pairs={{192,0},{193,1},{194,2},{195,3},{196,4},{197,5},{198,6},{199,7},{2... | collective-permute-start | bytes 393224 | tf_op jit(solution)/shard_map/ppermute | solution.py:453
  266.4 10.5 %collective-permute-start.36 = (bf16[2,2,128,128]{3,2,1,0:T(8,128)(2,1)S(1)}, bf16[2,2,128,128]{3,2,1,0:T(8,128)(2,1)S(1)}, u32[]{:S(2)}, u32[]{:S(2)}) collective-permute-start(bf16[2,2,128,128]{3,2,1,0:T(8,128)(2,1)S(1)} %convert_element_type.34), channel_id=1, source_target_pairs={{224,0},{225,1},{226,2},{227,3},{228,4},{229,5},{230,6},{231,7},{2... | collective-permute-start | bytes 393224 | tf_op jit(solution)/shard_map/ppermute | solution.py:453
  267.7 9.4 %collective-permute-start.28 = (bf16[1,2,128,128]{3,2,1,0:T(8,128)(2,1)S(1)}, bf16[1,2,128,128]{3,2,1,0:T(8,128)(2,1)S(1)}, u32[]{:S(2)}, u32[]{:S(2)}) collective-permute-start(bf16[1,2,128,128]{3,2,1,0:T(8,128)(2,1)S(1)} %get-tuple-element.114), channel_id=1, source_target_pairs={{4,0},{8,4},{12,8},{16,12},{20,16},{24,20},{28,24},{32,28},{36,32}... | collective-permute-start | bytes 196616 | tf_op jit(solution)/shard_map/ppermute | solution.py:449
  269.7 7.3 %collective-permute-start.29 = (bf16[1,2,128,128]{3,2,1,0:T(8,128)(2,1)S(1)}, bf16[1,2,128,128]{3,2,1,0:T(8,128)(2,1)S(1)}, u32[]{:S(2)}, u32[]{:S(2)}) collective-permute-start(bf16[1,2,128,128]{3,2,1,0:T(8,128)(2,1)S(1)} %get-tuple-element.113), channel_id=1, source_target_pairs={{0,4},{4,8},{8,12},{12,16},{16,20},{20,24},{24,28},{28,32},{32,36}... | collective-permute-start | bytes 196616 | tf_op jit(solution)/shard_map/ppermute | solution.py:450
  (26 other events, 62.3 us)

commit v5 on v4

--- a/solution.py
+++ b/solution.py
@@ -61,17 +61,21 @@
 
 
 def load_parts(meta, parts, whole, sems):
-    copies = []
-    for i, (four, target) in enumerate(zip(parts, whole)):
-        for k in range(NH):
-            row = pl.multiple_of(((meta[AT_HEAD] - k) & (NH - 1)) * PART, PART)
-            copies.append(
-                pltpu.make_async_copy(four[k], target.at[pl.ds(row, PART)], sems.at[i, k])
-            )
-    for c in copies:
-        c.start()
-    for c in copies:
-        c.wait()
+    for k in range(NH):
+        chunk = (meta[AT_HEAD] - k) & (NH - 1)
+        rows = pl.ds(pl.multiple_of(chunk * PART, PART), PART)
+        for i, (four, target) in enumerate(zip(parts, whole)):
+            pltpu.make_async_copy(four[k], target.at[rows], sems.at[i, chunk]).start()
+
+
+def await_parts(block, parts, whole, sems):
+    for chunk in range(NH):
+
+        @pl.when(block == 2 * chunk)
+        def _():
+            rows = pl.ds(chunk * PART, PART)
+            for i, (four, target) in enumerate(zip(parts, whole)):
+                pltpu.make_async_copy(four[0], target.at[rows], sems.at[i, chunk]).wait()
 
 
 def near_kernel(
@@ -85,6 +89,8 @@
         load_parts(meta, ((q0, q1, q2, q3), (d0, d1, d2, d3)), (q_scr, do_scr), sems)
         dkv_ref[...] = jnp.zeros_like(dkv_ref)
         dg_ref[...] = jnp.zeros_like(dg_ref)
+
+    await_parts(b, ((q0,), (d0,)), (q_scr, do_scr), sems)
 
     block = meta[AT_SEQ] * QB + b
     keys = [gl_ref[0], gl_ref[1]] + [kv_ref[b + w, 0] for w in range(3)]
@@ -155,6 +161,7 @@
 
         load_parts(meta, ((q0, q1, q2, q3), (d0, d1, d2, d3)), (q_scr, do_scr), sems)
 
+    await_parts(b, ((q0,), (d0,)), (q_scr, do_scr), sems)
     first = b * RND
     block = meta[AT_SEQ] * QB + b
     biases = []
@@ -448,9 +455,12 @@
     dq, dg, dkvx = tie(call_join(head.reshape(1), dq), dg, dkvx)
     lower = lax.ppermute(dkvx[:1].astype(BF), SEQ, down)
     upper = lax.ppermute(dkvx[QB + 1 :].astype(BF), SEQ, up)
+    half = lax.ppermute(dg.astype(BF), "z", [(i + 4, i) for i in range(4)])
+    half, lower, upper = tie(half, lower, upper)
+    dg = dg + half.astype(F32)
     part = dg.astype(BF)
-    for i in range(1, NZ):
-        dg = dg + lax.ppermute(part, "z", [(i, 0)]).astype(F32)
+    for some in [lax.ppermute(part, "z", [(i, 0)]) for i in range(1, 4)]:
+        dg = dg + some.astype(F32)
     total = call_collect(meta, back, dkvx, lower, upper, dg)
     dkv = total.transpose(1, 0, 2, 3).reshape(2, NH, TOK, HD).transpose(1, 0, 2, 3)
     dkv = plain_a2a(dkv, "head")

time: 301 us -> 301 us (level)
    ppermute x7 -> x4, starting transfers between devices: 9.03 us -> 5.17 us  [the longest x3 3.88 us: per_device(): lax.ppermute(part, 'z', [(i, 0)])]
    ppermute x3, waiting for transfers between devices: 15.2 us -> 11.7 us  [gather_sum(): lax.ppermute(value, ('x', 'c'), [(i + k, i) for i in range(k)])]
    ppermute x1, starting transfers between devices: 2.02 us -> 5.19 us  [per_device(): lower = lax.ppermute(dkvx[:1].astype(BF), SEQ, down)]
    ppermute x7 -> x4, waiting for transfers between devices: 19.2 us -> 17.7 us  [the longest x3 9.88 us: per_device(): lax.ppermute(part, 'z', [(i, 0)])]
  transfers between devices with their start and end apart: 41 -> 38, of which waited for: 18 -> 20; matrix products, arithmetic and copies ran while one was open for 7% -> 7% of each run, Pallas kernels for 14% -> 14%
where the time goes in v5:
time: 301 us; the launch traced here: 299 us
  starting transfers between devices  101 us (34%)
  waiting for transfers between devices  92.4 us (31%)
  Pallas kernels  50.9 us (17%)
  local copies, waits for them, and re-layouts  27.5 us (9%)
  blocking collectives  15.6 us (5%)
  other arithmetic  10.9 us (4%)
    ppermute x8, starting transfers between devices, along_z(): return lax.ppermute(value, 'z', [(i, (i + step) % NZ) for i in range(NZ)])  26.8 us
    ppermute x8, waiting for transfers between devices, along_z(): return lax.ppermute(value, 'z', [(i, (i + step) % NZ) for i in range(NZ)])  25.8 us
    ppermute x12, starting transfers between devices, turn(): lax.ppermute(value, 'head', [(i, (i + k) % NH) for i in range(NH)])  23.7 us
    pallas_call x1, Pallas kernels, call_near(): pl.pallas_call(near_kernel, grid_spec=pltpu.PrefetchScalarGridSpec(num_sc...  22.2 us
    all_to_all x4, starting transfers between devices, plain_a2a(): return lax.all_to_all(value, axis, split_axis=0, concat_axis=0, tiled=True)  21.7 us
    all_to_all x1, blocking collectives, plain_a2a(): return lax.all_to_all(value, axis, split_axis=0, concat_axis=0, tiled=True)  15.6 us
    unnamed x68, local copies, waits for them, and re-layouts  15.2 us
    ppermute x12, waiting for transfers between devices, turn(): lax.ppermute(value, 'head', [(i, (i + k) % NH) for i in range(NH)])  15 us
  transfers between devices with their start and end apart: 38, of which 20 were waited for; matrix products, arithmetic and copies ran while one was open for 7% of the time, Pallas kernels for 14%

profile of v5, /device:TPU:2, one launch (start us, length us, event | category | flops | bytes accessed | tf_op | source)
XLA Modules:
  0.0 299.4 jit_solution(10673455193373349660)
XLA Ops:
  2.8 4.5 %all-to-all-start = ((bf16[4,2,288,128]{3,2,1,0:T(8,128)(2,1)}), bf16[4,2,288,128]{3,2,1,0:T(8,128)(2,1)}, u32[]{:S(2)}, u32[]{:S(2)}) async-start(bf16[4,2,288,128]{3,2,1,0:T(8,128)(2,1)} %maximum_bitcast_fusion), calls=%async_computation | async-start | bytes 1179648 | tf_op jit(solution)/shard_map/all_to_all | solution.py:366
  8.7 2.0 collective-permute-start.2
  12.0 3.7 %multiply_reduce_fusion = f32[288,32]{1,0:T(8,128)S(1)} fusion(bf16[288,32,128]{2,1,0:T(8,128)(2,1)} %param.11, bf16[288,32,128]{2,1,0:T(8,128)(2,1)} %param.12), kind=kLoop, calls=%fused_computation | loop fusion | flops 4709376 | bytes 4755456 | tf_op jit(solution)/shard_map/reduce_sum | solution.py:419
  20.2 2.0 collective-permute-start
  22.2 4.0 %collective-permute-start.1 = (bf16[9,2,128,128]{3,2,1,0:T(8,128)(2,1)S(1)}, bf16[9,2,128,128]{3,2,1,0:T(8,128)(2,1)S(1)}, u32[]{:S(2)}, u32[]{:S(2)}) collective-permute-start(bf16[9,2,128,128]{3,2,1,0:T(8,128)(2,1)S(1)} %bitcast.95), channel_id=1, source_target_pairs={{0,224},{32,0},{64,32},{96,64},{128,96},{160,128},{192,160},{224,1... | collective-permute-start | bytes 1769480 | tf_op jit(solution)/shard_map/ppermute | solution.py:386
  26.3 2.3 collective-permute-start.6
  28.6 1.6 collective-permute-done.2.q1
  30.2 8.6 %collective-permute-done.refs_4_ = bf16[9,2,128,128]{3,2,1,0:T(8,128)(2,1)S(1)} collective-permute-done((bf16[9,2,128,128]{3,2,1,0:T(8,128)(2,1)S(1)}, bf16[9,2,128,128]{3,2,1,0:T(8,128)(2,1)S(1)}, u32[]{:S(2)}, u32[]{:S(2)}) %collective-permute-start) | collective-permute-done | bytes 589856 | tf_op jit(solution)/shard_map/ppermute | solution.py:386
  38.8 3.2 %collective-permute-start.5 = (bf16[9,2,128,128]{3,2,1,0:T(8,128)(2,1)S(1)}, bf16[9,2,128,128]{3,2,1,0:T(8,128)(2,1)S(1)}, u32[]{:S(2)}, u32[]{:S(2)}) collective-permute-start(bf16[9,2,128,128]{3,2,1,0:T(8,128)(2,1)S(1)} %collective-permute-done.1.refs_1_), channel_id=1, source_target_pairs={{0,224},{32,0},{64,32},{96,64},{128,96},{160,128},{192,160},{224,1... | collective-permute-start | bytes 1769480 | tf_op jit(solution)/shard_map/ppermute | solution.py:386
  42.7 10.9 %collective-permute-done.4.refs_3_ = bf16[9,2,128,128]{3,2,1,0:T(8,128)(2,1)S(1)} collective-permute-done((bf16[9,2,128,128]{3,2,1,0:T(8,128)(2,1)S(1)}, bf16[9,2,128,128]{3,2,1,0:T(8,128)(2,1)S(1)}, u32[]{:S(2)}, u32[]{:S(2)}) %collective-permute-start.4) | collective-permute-done | bytes 589856 | tf_op jit(solution)/shard_map/ppermute | solution.py:386
  53.6 2.5 select.20
  58.6 4.9 %all-to-all-start.1 = ((bf16[40,2,128,128]{3,2,1,0:T(8,128)(2,1)}), bf16[40,2,128,128]{3,2,1,0:T(8,128)(2,1)}, u32[]{:S(2)}, u32[]{:S(2)}) async-start(bf16[40,2,128,128]{3,2,1,0:T(8,128)(2,1)} %select.20), calls=%async_computation.1 | async-start | bytes 5242880 | tf_op jit(solution)/shard_map/all_to_all | solution.py:366
  63.5 1.9 dynamic-slice_bitcast_fusion
  65.4 1.5 collective-permute-start.10
  67.5 1.9 collective-permute-start.7
  70.7 3.8 %collective-permute-start.13 = (bf16[2304,128]{1,0:T(8,128)(2,1)S(1)}, bf16[2304,128]{1,0:T(8,128)(2,1)S(1)}, u32[]{:S(2)}, u32[]{:S(2)}) collective-permute-start(bf16[2304,128]{1,0:T(8,128)(2,1)S(1)} %get-tuple-element.111), channel_id=1, source_target_pairs={{0,2},{1,3},{2,0},{3,1},{4,6},{5,7},{6,4},{7,5},{8,10},{9,11},{10,... | collective-permute-start | bytes 1769480 | tf_op jit(solution)/shard_map/ppermute | solution.py:370
  74.6 7.1 %collective-permute-done.10.d3 = bf16[2304,128]{1,0:T(8,128)(2,1)S(1)} collective-permute-done((bf16[2304,128]{1,0:T(8,128)(2,1)S(1)}, bf16[2304,128]{1,0:T(8,128)(2,1)S(1)}, u32[]{:S(2)}, u32[]{:S(2)}) %collective-permute-start.10) | collective-permute-done | bytes 589856 | tf_op jit(solution)/shard_map/ppermute | solution.py:370
  81.6 1.9 collective-permute-done.9.d1
  85.2 14.3 %collective-permute-start.11 = (bf16[5,2,128,128]{3,2,1,0:T(8,128)(2,1)S(1)}, bf16[5,2,128,128]{3,2,1,0:T(8,128)(2,1)S(1)}, u32[]{:S(2)}, u32[]{:S(2)}) collective-permute-start(bf16[5,2,128,128]{3,2,1,0:T(8,128)(2,1)S(1)} %slice.50), channel_id=1, source_target_pairs={{0,32},{32,64},{64,96},{96,128},{128,160},{160,192},{192,224},{224... | collective-permute-start | bytes 983048 | tf_op jit(solution)/shard_map/ppermute | solution.py:386
  100.3 6.4 %collective-permute-done.12.refs_3_ = bf16[4,2,128,128]{3,2,1,0:T(8,128)(2,1)S(1)} collective-permute-done((bf16[4,2,128,128]{3,2,1,0:T(8,128)(2,1)S(1)}, bf16[4,2,128,128]{3,2,1,0:T(8,128)(2,1)S(1)}, u32[]{:S(2)}, u32[]{:S(2)}) %collective-permute-start.12) | collective-permute-done | bytes 262176 | tf_op jit(solution)/shard_map/ppermute | solution.py:386
  112.2 1.9 select.21
  114.1 5.4 %all-to-all-start.2 = ((bf16[24,2,128,128]{3,2,1,0:T(8,128)(2,1)}), bf16[24,2,128,128]{3,2,1,0:T(8,128)(2,1)}, u32[]{:S(2)}, u32[]{:S(2)}) async-start(bf16[24,2,128,128]{3,2,1,0:T(8,128)(2,1)} %select.21), calls=%async_computation.2 | async-start | bytes 3145728 | tf_op jit(solution)/shard_map/all_to_all | solution.py:366
  120.9 2.6 collective-permute-start.16
  125.9 1.4 pad_maximum_fusion.1
  127.3 1.5 rev.3
  129.5 1.9 collective-permute-start.17
  131.4 3.6 %collective-permute-start.18 = (bf16[1,2,128,128]{3,2,1,0:T(8,128)(2,1)}, bf16[1,2,128,128]{3,2,1,0:T(8,128)(2,1)}, u32[]{:S(2)}, u32[]{:S(2)}) collective-permute-start(bf16[1,2,128,128]{3,2,1,0:T(8,128)(2,1)} %get-tuple-element.123), channel_id=1, source_target_pairs={{4,0},{8,4},{12,8},{16,12},{20,16},{24,20},{28,24},{32,28},{36,32}... | collective-permute-start | bytes 196616 | tf_op jit(solution)/shard_map/ppermute | solution.py:439
  136.6 3.3 %all-to-all-done.2.far_ref = bf16[24,2,128,128]{3,2,1,0:T(8,128)(2,1)} async-done(((bf16[24,2,128,128]{3,2,1,0:T(8,128)(2,1)}), bf16[24,2,128,128]{3,2,1,0:T(8,128)(2,1)}, u32[]{:S(2)}, u32[]{:S(2)}) %all-to-all-start.2) | async-done | bytes 1572896 | tf_op jit(solution)/shard_map/all_to_all | solution.py:366
  141.9 14.5 %random.1 = (f32[9,128,1024]{2,1,0:T(8,128)}, bf16[64,2,128,128]{3,2,1,0:T(8,128)(2,1)}) custom-call(s32[158]{0:T(256)S(1)} %concatenate.11.meta, bf16[2304,128]{1,0:T(8,128)(2,1)S(1)} %get-tuple-element.118.q0, bf16[2304,128]{1,0:T(8,128)(2,1)S(1)} %collective-permute-done.2.q1, bf16[2304,128]{1,0:T(8,128)(2,1)S(1)} %collective-permute-done.6.q2, ...), custom_call_target="tpu_custom_call" | custom-call | tf_op jit(solution)/shard_map/random/pallas_call | solution.py:285
  156.4 7.0 %all-to-all-start.3 = ((bf16[64,2,128,128]{3,2,1,0:T(8,128)(2,1)}), bf16[64,2,128,128]{3,2,1,0:T(8,128)(2,1)}, u32[]{:S(2)}, u32[]{:S(2)}) async-start(bf16[64,2,128,128]{3,2,1,0:T(8,128)(2,1)} %get-tuple-element.91), calls=%async_computation.3 | async-start | bytes 8388608 | tf_op jit(solution)/shard_map/all_to_all | solution.py:366
  166.8 11.6 %collective-permute-done.20 = bf16[4,128,128]{2,1,0:T(8,128)(2,1)S(1)} collective-permute-done((bf16[4,128,128]{2,1,0:T(8,128)(2,1)S(1)}, bf16[4,128,128]{2,1,0:T(8,128)(2,1)S(1)}, u32[]{:S(2)}, u32[]{:S(2)}) %collective-permute-start.20) | collective-permute-done | bytes 131104 | tf_op jit(solution)/shard_map/ppermute | solution.py:392
  179.7 1.8 pad_maximum_fusion.kv_ref
  181.6 3.3 %collective-permute-done.21 = bf16[4,128,128]{2,1,0:T(8,128)(2,1)S(1)} collective-permute-done((bf16[4,128,128]{2,1,0:T(8,128)(2,1)S(1)}, bf16[4,128,128]{2,1,0:T(8,128)(2,1)S(1)}, u32[]{:S(2)}, u32[]{:S(2)}) %collective-permute-start.21) | collective-permute-done | bytes 131104 | tf_op jit(solution)/shard_map/ppermute | solution.py:392
  184.8 22.2 %near.1 = (bf16[2304,128]{1,0:T(8,128)(2,1)S(1)}, bf16[2304,128]{1,0:T(8,128)(2,1)S(1)}, bf16[2304,128]{1,0:T(8,128)(2,1)S(1)}, bf16[2304,128]{1,0:T(8,128)(2,1)...) custom-call(s32[158]{0:T(256)S(1)} %concatenate.11.meta, bf16[2304,128]{1,0:T(8,128)(2,1)S(1)} %get-tuple-element.118.q0, ...), custom_call_target="tpu_custom_call" | custom-call | tf_op jit(solution)/shard_map/near/pallas_call | solution.py:263
  209.1 5.8 %collective-permute-start.23 = (bf16[2304,128]{1,0:T(8,128)(2,1)S(1)}, bf16[2304,128]{1,0:T(8,128)(2,1)S(1)}, u32[]{:S(2)}, u32[]{:S(2)}) collective-permute-start(bf16[2304,128]{1,0:T(8,128)(2,1)S(1)} %get-tuple-element.81), channel_id=1, source_target_pairs={{0,2},{1,3},{2,0},{3,1},{4,6},{5,7},{6,4},{7,5},{8,10},{9,11},{10,... | collective-permute-start | bytes 1769480 | tf_op jit(solution)/shard_map/ppermute | solution.py:370
  215.0 1.7 collective-permute-start.24
  216.7 5.1 %collective-permute-done.25 = f32[2,2,128,128]{3,2,1,0:T(8,128)S(1)} collective-permute-done((f32[2,2,128,128]{3,2,1,0:T(8,128)S(1)}, f32[2,2,128,128]{3,2,1,0:T(8,128)S(1)}, u32[]{:S(2)}, u32[]{:S(2)}) %collective-permute-start.25) | collective-permute-done | bytes 262176 | tf_op jit(solution)/shard_map/ppermute | solution.py:401
  221.8 5.5 %collective-permute-start.26 = (f32[2,2,128,128]{3,2,1,0:T(8,128)S(1)}, f32[2,2,128,128]{3,2,1,0:T(8,128)S(1)}, u32[]{:S(2)}, u32[]{:S(2)}) collective-permute-start(f32[2,2,128,128]{3,2,1,0:T(8,128)S(1)} %add.132), channel_id=1, source_target_pairs={{8,0},{12,4},{9,1},{13,5},{10,2},{14,6},{11,3},{15,7},{40,32},{44,... | collective-permute-start | bytes 786440 | tf_op jit(solution)/shard_map/ppermute | solution.py:401
  227.3 6.6 %collective-permute-done.26 = f32[2,2,128,128]{3,2,1,0:T(8,128)S(1)} collective-permute-done((f32[2,2,128,128]{3,2,1,0:T(8,128)S(1)}, f32[2,2,128,128]{3,2,1,0:T(8,128)S(1)}, u32[]{:S(2)}, u32[]{:S(2)}) %collective-permute-start.26) | collective-permute-done | bytes 262176 | tf_op jit(solution)/shard_map/ppermute | solution.py:401
  234.7 2.0 collective-permute-done.23
  237.6 4.2 %join.1 = bf16[288,4,8,128]{3,2,1,0:T(8,128)(2,1)} custom-call(s32[1]{0:T(128)} %bitcast.head, bf16[288,8,128]{2,1,0:T(8,128)(2,1)} %bitcast.101, bf16[288,8,128]{2,1,0:T(8,128)(2,1)} %bitcast.107, bf16[288,8,128]{2,1,0:T(8,128)(2,1)} %bitcast.108, bf16[288,8,128]{2,1,0:T(8,128)(2,1)} %bitcast.109), custom_call_target="tpu_custom_call" | custom-call | tf_op jit(solution)/shard_map/join/pallas_call | solution.py:352
  243.3 5.2 %collective-permute-start.29 = (bf16[1,2,128,128]{3,2,1,0:T(8,128)(2,1)S(1)}, bf16[1,2,128,128]{3,2,1,0:T(8,128)(2,1)S(1)}, u32[]{:S(2)}, u32[]{:S(2)}) collective-permute-start(bf16[1,2,128,128]{3,2,1,0:T(8,128)(2,1)S(1)} %get-tuple-element.120), channel_id=1, source_target_pairs={{4,0},{8,4},{12,8},{16,12},{20,16},{24,20},{28,24},{32,28},{36,32}... | collective-permute-start | bytes 196616 | tf_op jit(solution)/shard_map/ppermute | solution.py:456
  248.5 1.9 collective-permute-start.30
  251.6 2.9 collective-permute-done.30.upper
  254.6 7.9 %collective-permute-done.28 = bf16[2,2,128,128]{3,2,1,0:T(8,128)(2,1)S(1)} collective-permute-done((bf16[2,2,128,128]{3,2,1,0:T(8,128)(2,1)S(1)}, bf16[2,2,128,128]{3,2,1,0:T(8,128)(2,1)S(1)}, u32[]{:S(2)}, u32[]{:S(2)}) %collective-permute-start.28) | collective-permute-done | bytes 131104 | tf_op jit(solution)/shard_map/ppermute | solution.py:458
  266.4 9.9 %collective-permute-done.31 = bf16[2,2,128,128]{3,2,1,0:T(8,128)(2,1)S(1)} collective-permute-done((bf16[2,2,128,128]{3,2,1,0:T(8,128)(2,1)S(1)}, bf16[2,2,128,128]{3,2,1,0:T(8,128)(2,1)S(1)}, u32[]{:S(2)}, u32[]{:S(2)}) %collective-permute-start.31) | collective-permute-done | bytes 131104 | tf_op jit(solution)/shard_map/ppermute | solution.py:462
  276.3 5.6 %collect.1 = bf16[9,2,128,128]{3,2,1,0:T(8,128)(2,1)S(1)} custom-call(s32[158]{0:T(256)S(1)} %concatenate.11.meta, bf16[64,2,128,128]{3,2,1,0:T(8,128)(2,1)} %all-to-all-done.3.got, f32[11,2,128,128]{3,2,1,0:T(8,128)S(1)} %copy-done, bf16[1,2,128,128]{3,2,1,0:T(8,128)(2,1)S(1)} %collective-permute-done.29.lower, ...), custom_call_target="tpu_custom_call" | custom-call | tf_op jit(solution)/shard_map/collect/pallas_call | solution.py:330
  282.0 15.6 %all_to_all.25 = bf16[4,2,288,128]{3,2,1,0:T(8,128)(2,1)S(1)} all-to-all(bf16[4,2,288,128]{3,2,1,0:T(8,128)(2,1)S(1)} %copy.111), channel_id=1, replica_groups=mesh['z'=8,'x'=4,'c'=2,'head'=4] {'head'}, dimensions={0} | all-to-all | bytes 1179648 | tf_op jit(solution)/shard_map/all_to_all | solution.py:366
  (154 shorter events, 47.4 us)
Async XLA Ops:
  0.6 6.7 %copy-start.23 = (bf16[288,32,128]{2,1,0:T(8,128)(2,1)S(1)}, bf16[288,32,128]{2,1,0:T(8,128)(2,1)}, u32[]{:S(2)}) copy-start(bf16[288,32,128]{2,1,0:T(8,128)(2,1)} %param.8) | copy-start | bytes 7077892
  2.8 16.3 %all-to-all-start = ((bf16[4,2,288,128]{3,2,1,0:T(8,128)(2,1)}), bf16[4,2,288,128]{3,2,1,0:T(8,128)(2,1)}, u32[]{:S(2)}, u32[]{:S(2)}) async-start(bf16[4,2,288,128]{3,2,1,0:T(8,128)(2,1)} %maximum_bitcast_fusion), calls=%async_computation | async-start | bytes 1179648 | tf_op jit(solution)/shard_map/all_to_all | solution.py:366
  8.7 21.5 %collective-permute-start.2 = (bf16[2304,128]{1,0:T(8,128)(2,1)}, bf16[2304,128]{1,0:T(8,128)(2,1)S(1)}, u32[]{:S(2)}, u32[]{:S(2)}) collective-permute-start(bf16[2304,128]{1,0:T(8,128)(2,1)} %get-tuple-element.117), channel_id=1, source_target_pairs={{0,1},{1,2},{2,3},{3,0},{4,5},{5,6},{6,7},{7,4},{8,9},{9,10},{10,1... | collective-permute-start | bytes 1769480 | tf_op jit(solution)/shard_map/ppermute | solution.py:370
  10.7 19.5 %collective-permute-start.3 = (bf16[2304,128]{1,0:T(8,128)(2,1)}, bf16[2304,128]{1,0:T(8,128)(2,1)S(1)}, u32[]{:S(2)}, u32[]{:S(2)}) collective-permute-start(bf16[2304,128]{1,0:T(8,128)(2,1)} %get-tuple-element.116), channel_id=1, source_target_pairs={{0,3},{1,0},{2,1},{3,2},{4,7},{5,4},{6,5},{7,6},{8,11},{9,8},{10,9... | collective-permute-start | bytes 1769480 | tf_op jit(solution)/shard_map/ppermute | solution.py:370
  20.2 18.5 %collective-permute-start = (bf16[9,2,128,128]{3,2,1,0:T(8,128)(2,1)S(1)}, bf16[9,2,128,128]{3,2,1,0:T(8,128)(2,1)S(1)}, u32[]{:S(2)}, u32[]{:S(2)}) collective-permute-start(bf16[9,2,128,128]{3,2,1,0:T(8,128)(2,1)S(1)} %bitcast.94), channel_id=1, source_target_pairs={{0,32},{32,64},{64,96},{96,128},{128,160},{160,192},{192,224},{224... | collective-permute-start | bytes 1769480 | tf_op jit(solution)/shard_map/ppermute | solution.py:386
  22.2 16.5 %collective-permute-start.1 = (bf16[9,2,128,128]{3,2,1,0:T(8,128)(2,1)S(1)}, bf16[9,2,128,128]{3,2,1,0:T(8,128)(2,1)S(1)}, u32[]{:S(2)}, u32[]{:S(2)}) collective-permute-start(bf16[9,2,128,128]{3,2,1,0:T(8,128)(2,1)S(1)} %bitcast.95), channel_id=1, source_target_pairs={{0,224},{32,0},{64,32},{96,64},{128,96},{160,128},{192,160},{224,1... | collective-permute-start | bytes 1769480 | tf_op jit(solution)/shard_map/ppermute | solution.py:386
  26.3 16.5 %collective-permute-start.6 = (bf16[2304,128]{1,0:T(8,128)(2,1)}, bf16[2304,128]{1,0:T(8,128)(2,1)S(1)}, u32[]{:S(2)}, u32[]{:S(2)}) collective-permute-start(bf16[2304,128]{1,0:T(8,128)(2,1)} %get-tuple-element.115), channel_id=1, source_target_pairs={{0,2},{1,3},{2,0},{3,1},{4,6},{5,7},{6,4},{7,5},{8,10},{9,11},{10,... | collective-permute-start | bytes 1769480 | tf_op jit(solution)/shard_map/ppermute | solution.py:370
  30.2 109.7 %copy-start.2 = (bf16[2304,128]{1,0:T(8,128)(2,1)}, bf16[2304,128]{1,0:T(8,128)(2,1)S(1)}, u32[]{:S(2)}) copy-start(bf16[2304,128]{1,0:T(8,128)(2,1)S(1)} %collective-permute-done.3.q3) | copy-start | bytes 1769476
  38.7 17.3 %copy-start.11 = (bf16[9,2,128,128]{3,2,1,0:T(8,128)(2,1)}, bf16[9,2,128,128]{3,2,1,0:T(8,128)(2,1)S(1)}, u32[]{:S(2)}) copy-start(bf16[9,2,128,128]{3,2,1,0:T(8,128)(2,1)S(1)} %collective-permute-done.1.refs_1_) | copy-start | bytes 1769476
  38.7 14.9 %collective-permute-start.4 = (bf16[9,2,128,128]{3,2,1,0:T(8,128)(2,1)S(1)}, bf16[9,2,128,128]{3,2,1,0:T(8,128)(2,1)S(1)}, u32[]{:S(2)}, u32[]{:S(2)}) collective-permute-start(bf16[9,2,128,128]{3,2,1,0:T(8,128)(2,1)S(1)} %collective-permute-done.refs_4_), channel_id=1, source_target_pairs={{0,32},{32,64},{64,96},{96,128},{128,160},{160,192},{192,224},{224... | collective-permute-start | bytes 1769480 | tf_op jit(solution)/shard_map/ppermute | solution.py:386
  38.8 14.9 %collective-permute-start.5 = (bf16[9,2,128,128]{3,2,1,0:T(8,128)(2,1)S(1)}, bf16[9,2,128,128]{3,2,1,0:T(8,128)(2,1)S(1)}, u32[]{:S(2)}, u32[]{:S(2)}) collective-permute-start(bf16[9,2,128,128]{3,2,1,0:T(8,128)(2,1)S(1)} %collective-permute-done.1.refs_1_), channel_id=1, source_target_pairs={{0,224},{32,0},{64,32},{96,64},{128,96},{160,128},{192,160},{224,1... | collective-permute-start | bytes 1769480 | tf_op jit(solution)/shard_map/ppermute | solution.py:386
  42.7 97.2 %copy-start.3 = (bf16[2304,128]{1,0:T(8,128)(2,1)}, bf16[2304,128]{1,0:T(8,128)(2,1)S(1)}, u32[]{:S(2)}) copy-start(bf16[2304,128]{1,0:T(8,128)(2,1)S(1)} %collective-permute-done.6.q2) | copy-start | bytes 1769476
  58.6 49.5 %all-to-all-start.1 = ((bf16[40,2,128,128]{3,2,1,0:T(8,128)(2,1)}), bf16[40,2,128,128]{3,2,1,0:T(8,128)(2,1)}, u32[]{:S(2)}, u32[]{:S(2)}) async-start(bf16[40,2,128,128]{3,2,1,0:T(8,128)(2,1)} %select.20), calls=%async_computation.1 | async-start | bytes 5242880 | tf_op jit(solution)/shard_map/all_to_all | solution.py:366
  65.4 74.5 %copy-start.1 = (bf16[2304,128]{1,0:T(8,128)(2,1)}, bf16[2304,128]{1,0:T(8,128)(2,1)S(1)}, u32[]{:S(2)}) copy-start(bf16[2304,128]{1,0:T(8,128)(2,1)S(1)} %get-tuple-element.114.d0) | copy-start | bytes 1769476
  65.4 16.2 %collective-permute-start.10 = (bf16[2304,128]{1,0:T(8,128)(2,1)S(1)}, bf16[2304,128]{1,0:T(8,128)(2,1)S(1)}, u32[]{:S(2)}, u32[]{:S(2)}) collective-permute-start(bf16[2304,128]{1,0:T(8,128)(2,1)S(1)} %get-tuple-element.112), channel_id=1, source_target_pairs={{0,3},{1,0},{2,1},{3,2},{4,7},{5,4},{6,5},{7,6},{8,11},{9,8},{10,9... | collective-permute-start | bytes 1769480 | tf_op jit(solution)/shard_map/ppermute | solution.py:370
  66.9 16.6 %collective-permute-start.9 = (bf16[2304,128]{1,0:T(8,128)(2,1)S(1)}, bf16[2304,128]{1,0:T(8,128)(2,1)S(1)}, u32[]{:S(2)}, u32[]{:S(2)}) collective-permute-start(bf16[2304,128]{1,0:T(8,128)(2,1)S(1)} %get-tuple-element.113), channel_id=1, source_target_pairs={{0,1},{1,2},{2,3},{3,0},{4,5},{5,6},{6,7},{7,4},{8,9},{9,10},{10,1... | collective-permute-start | bytes 1769480 | tf_op jit(solution)/shard_map/ppermute | solution.py:370
  67.5 16.8 %collective-permute-start.7 = (bf16[9,2,128,128]{3,2,1,0:T(8,128)(2,1)S(1)}, bf16[9,2,128,128]{3,2,1,0:T(8,128)(2,1)S(1)}, u32[]{:S(2)}, u32[]{:S(2)}) collective-permute-start(bf16[9,2,128,128]{3,2,1,0:T(8,128)(2,1)S(1)} %copy-done.13), channel_id=1, source_target_pairs={{0,32},{32,64},{64,96},{96,128},{128,160},{160,192},{192,224},{224... | collective-permute-start | bytes 1769480 | tf_op jit(solution)/shard_map/ppermute | solution.py:386
  69.4 14.9 %collective-permute-start.8 = (bf16[9,2,128,128]{3,2,1,0:T(8,128)(2,1)S(1)}, bf16[9,2,128,128]{3,2,1,0:T(8,128)(2,1)S(1)}, u32[]{:S(2)}, u32[]{:S(2)}) collective-permute-start(bf16[9,2,128,128]{3,2,1,0:T(8,128)(2,1)S(1)} %copy-done.15), channel_id=1, source_target_pairs={{0,224},{32,0},{64,32},{96,64},{128,96},{160,128},{192,160},{224,1... | collective-permute-start | bytes 1769480 | tf_op jit(solution)/shard_map/ppermute | solution.py:386
  70.7 29.6 %collective-permute-start.13 = (bf16[2304,128]{1,0:T(8,128)(2,1)S(1)}, bf16[2304,128]{1,0:T(8,128)(2,1)S(1)}, u32[]{:S(2)}, u32[]{:S(2)}) collective-permute-start(bf16[2304,128]{1,0:T(8,128)(2,1)S(1)} %get-tuple-element.111), channel_id=1, source_target_pairs={{0,2},{1,3},{2,0},{3,1},{4,6},{5,7},{6,4},{7,5},{8,10},{9,11},{10,... | collective-permute-start | bytes 1769480 | tf_op jit(solution)/shard_map/ppermute | solution.py:370
  81.6 25.0 %copy-start.24 = (bf16[2304,128]{1,0:T(8,128)(2,1)}, bf16[2304,128]{1,0:T(8,128)(2,1)S(1)}, u32[]{:S(2)}) copy-start(bf16[2304,128]{1,0:T(8,128)(2,1)S(1)} %collective-permute-done.10.d3) | copy-start | bytes 1769476
  85.2 22.2 %collective-permute-start.11 = (bf16[5,2,128,128]{3,2,1,0:T(8,128)(2,1)S(1)}, bf16[5,2,128,128]{3,2,1,0:T(8,128)(2,1)S(1)}, u32[]{:S(2)}, u32[]{:S(2)}) collective-permute-start(bf16[5,2,128,128]{3,2,1,0:T(8,128)(2,1)S(1)} %slice.50), channel_id=1, source_target_pairs={{0,32},{32,64},{64,96},{96,128},{128,160},{160,192},{192,224},{224... | collective-permute-start | bytes 983048 | tf_op jit(solution)/shard_map/ppermute | solution.py:386
  100.3 6.4 %collective-permute-start.12 = (bf16[4,2,128,128]{3,2,1,0:T(8,128)(2,1)S(1)}, bf16[4,2,128,128]{3,2,1,0:T(8,128)(2,1)S(1)}, u32[]{:S(2)}, u32[]{:S(2)}) collective-permute-start(bf16[4,2,128,128]{3,2,1,0:T(8,128)(2,1)S(1)} %slice.51), channel_id=1, source_target_pairs={{0,224},{32,0},{64,32},{96,64},{128,96},{160,128},{192,160},{224,1... | collective-permute-start | bytes 786440 | tf_op jit(solution)/shard_map/ppermute | solution.py:386
  100.3 6.4 %copy-start.25 = (bf16[2304,128]{1,0:T(8,128)(2,1)}, bf16[2304,128]{1,0:T(8,128)(2,1)S(1)}, u32[]{:S(2)}) copy-start(bf16[2304,128]{1,0:T(8,128)(2,1)S(1)} %collective-permute-done.13.d2) | copy-start | bytes 1769476
  114.1 25.8 %all-to-all-start.2 = ((bf16[24,2,128,128]{3,2,1,0:T(8,128)(2,1)}), bf16[24,2,128,128]{3,2,1,0:T(8,128)(2,1)}, u32[]{:S(2)}, u32[]{:S(2)}) async-start(bf16[24,2,128,128]{3,2,1,0:T(8,128)(2,1)} %select.21), calls=%async_computation.2 | async-start | bytes 3145728 | tf_op jit(solution)/shard_map/all_to_all | solution.py:366
  119.5 5.3 %collective-permute-start.14 = (f32[2,18,128]{2,0,1:T(2,128)}, f32[2,18,128]{2,0,1:T(2,128)}, u32[]{:S(2)}, u32[]{:S(2)}) collective-permute-start(f32[2,18,128]{2,0,1:T(2,128)} %get-tuple-element.65), channel_id=1, source_target_pairs={{0,1},{1,2},{2,3},{3,0},{4,5},{5,6},{6,7},{7,4},{8,9},{9,10},{10,1... | collective-permute-start | bytes 55304 | tf_op jit(solution)/shard_map/ppermute | solution.py:370
  119.5 5.6 %collective-permute-start.15 = (f32[2,18,128]{2,0,1:T(2,128)}, f32[2,18,128]{2,0,1:T(2,128)}, u32[]{:S(2)}, u32[]{:S(2)}) collective-permute-start(f32[2,18,128]{2,0,1:T(2,128)} %get-tuple-element.66), channel_id=1, source_target_pairs={{0,2},{1,3},{2,0},{3,1},{4,6},{5,7},{6,4},{7,5},{8,10},{9,11},{10,... | collective-permute-start | bytes 55304 | tf_op jit(solution)/shard_map/ppermute | solution.py:370
  120.9 5.0 %collective-permute-start.16 = (f32[2,18,128]{2,0,1:T(2,128)}, f32[2,18,128]{2,0,1:T(2,128)}, u32[]{:S(2)}, u32[]{:S(2)}) collective-permute-start(f32[2,18,128]{2,0,1:T(2,128)} %get-tuple-element.67), channel_id=1, source_target_pairs={{0,3},{1,0},{2,1},{3,2},{4,7},{5,4},{6,5},{7,6},{8,11},{9,8},{10,9... | collective-permute-start | bytes 55304 | tf_op jit(solution)/shard_map/ppermute | solution.py:370
  129.5 26.9 %collective-permute-start.17 = (bf16[1,2,128,128]{3,2,1,0:T(8,128)(2,1)}, bf16[1,2,128,128]{3,2,1,0:T(8,128)(2,1)}, u32[]{:S(2)}, u32[]{:S(2)}) collective-permute-start(bf16[1,2,128,128]{3,2,1,0:T(8,128)(2,1)} %get-tuple-element.124), channel_id=1, source_target_pairs={{0,4},{4,8},{8,12},{12,16},{16,20},{20,24},{24,28},{28,32},{32,36}... | collective-permute-start | bytes 196616 | tf_op jit(solution)/shard_map/ppermute | solution.py:438
  131.4 25.0 %collective-permute-start.18 = (bf16[1,2,128,128]{3,2,1,0:T(8,128)(2,1)}, bf16[1,2,128,128]{3,2,1,0:T(8,128)(2,1)}, u32[]{:S(2)}, u32[]{:S(2)}) collective-permute-start(bf16[1,2,128,128]{3,2,1,0:T(8,128)(2,1)} %get-tuple-element.123), channel_id=1, source_target_pairs={{4,0},{8,4},{12,8},{16,12},{20,16},{24,20},{28,24},{32,28},{36,32}... | collective-permute-start | bytes 196616 | tf_op jit(solution)/shard_map/ppermute | solution.py:439
  156.4 7.1 %copy-start.29 = (bf16[2,2,128,128]{3,2,1,0:T(8,128)(2,1)S(1)}, bf16[2,2,128,128]{3,2,1,0:T(8,128)(2,1)}, u32[]{:S(2)}) copy-start(bf16[2,2,128,128]{3,2,1,0:T(8,128)(2,1)} %slice.66) | copy-start | bytes 393220
  156.4 119.9 %all-to-all-start.3 = ((bf16[64,2,128,128]{3,2,1,0:T(8,128)(2,1)}), bf16[64,2,128,128]{3,2,1,0:T(8,128)(2,1)}, u32[]{:S(2)}, u32[]{:S(2)}) async-start(bf16[64,2,128,128]{3,2,1,0:T(8,128)(2,1)} %get-tuple-element.91), calls=%async_computation.3 | async-start | bytes 8388608 | tf_op jit(solution)/shard_map/all_to_all | solution.py:366
  163.4 21.4 %copy-start.17 = (f32[2,9,8,128]{3,2,1,0:T(8,128)S(1)}, f32[2,9,8,128]{3,2,1,0:T(8,128)}, u32[]{:S(2)}) copy-start(f32[2,9,8,128]{3,2,1,0:T(8,128)} %copy.109.ld_ref) | copy-start | bytes 221188
  164.8 0.7 collective-permute-start.19
  165.5 12.9 %collective-permute-start.20 = (bf16[4,128,128]{2,1,0:T(8,128)(2,1)S(1)}, bf16[4,128,128]{2,1,0:T(8,128)(2,1)S(1)}, u32[]{:S(2)}, u32[]{:S(2)}) collective-permute-start(bf16[4,128,128]{2,1,0:T(8,128)(2,1)S(1)} %broadcast_select_fusion), channel_id=1, source_target_pairs={{0,8},{4,12},{1,9},{5,13},{2,10},{6,14},{3,11},{7,15},{32,40},{36,... | collective-permute-start | bytes 393224 | tf_op jit(solution)/shard_map/ppermute | solution.py:392
  178.4 6.4 %collective-permute-start.21 = (bf16[4,128,128]{2,1,0:T(8,128)(2,1)S(1)}, bf16[4,128,128]{2,1,0:T(8,128)(2,1)S(1)}, u32[]{:S(2)}, u32[]{:S(2)}) collective-permute-start(bf16[4,128,128]{2,1,0:T(8,128)(2,1)S(1)} %broadcast_select_fusion.1), channel_id=1, source_target_pairs={{0,16},{4,20},{8,24},{12,28},{1,17},{5,21},{9,25},{13,29},{2,18},{... | collective-permute-start | bytes 393224 | tf_op jit(solution)/shard_map/ppermute | solution.py:392
  207.1 29.6 %copy-start.20 = (bf16[2304,128]{1,0:T(8,128)(2,1)}, bf16[2304,128]{1,0:T(8,128)(2,1)S(1)}, u32[]{:S(2)}) copy-start(bf16[2304,128]{1,0:T(8,128)(2,1)S(1)} %get-tuple-element.84) | copy-start | bytes 1769476
  207.1 14.7 %collective-permute-start.25 = (f32[2,2,128,128]{3,2,1,0:T(8,128)S(1)}, f32[2,2,128,128]{3,2,1,0:T(8,128)S(1)}, u32[]{:S(2)}, u32[]{:S(2)}) collective-permute-start(f32[2,2,128,128]{3,2,1,0:T(8,128)S(1)} %get-tuple-element.83), channel_id=1, source_target_pairs={{16,0},{20,4},{24,8},{28,12},{17,1},{21,5},{25,9},{29,13},{18,2},{... | collective-permute-start | bytes 786440 | tf_op jit(solution)/shard_map/ppermute | solution.py:401
  208.4 26.3 %collective-permute-start.22 = (bf16[2304,128]{1,0:T(8,128)(2,1)S(1)}, bf16[2304,128]{1,0:T(8,128)(2,1)S(1)}, u32[]{:S(2)}, u32[]{:S(2)}) collective-permute-start(bf16[2304,128]{1,0:T(8,128)(2,1)S(1)} %get-tuple-element.80), channel_id=1, source_target_pairs={{0,1},{1,2},{2,3},{3,0},{4,5},{5,6},{6,7},{7,4},{8,9},{9,10},{10,1... | collective-permute-start | bytes 1769480 | tf_op jit(solution)/shard_map/ppermute | solution.py:370
  209.1 27.5 %collective-permute-start.23 = (bf16[2304,128]{1,0:T(8,128)(2,1)S(1)}, bf16[2304,128]{1,0:T(8,128)(2,1)S(1)}, u32[]{:S(2)}, u32[]{:S(2)}) collective-permute-start(bf16[2304,128]{1,0:T(8,128)(2,1)S(1)} %get-tuple-element.81), channel_id=1, source_target_pairs={{0,2},{1,3},{2,0},{3,1},{4,6},{5,7},{6,4},{7,5},{8,10},{9,11},{10,... | collective-permute-start | bytes 1769480 | tf_op jit(solution)/shard_map/ppermute | solution.py:370
  215.0 21.7 %collective-permute-start.24 = (bf16[2304,128]{1,0:T(8,128)(2,1)S(1)}, bf16[2304,128]{1,0:T(8,128)(2,1)S(1)}, u32[]{:S(2)}, u32[]{:S(2)}) collective-permute-start(bf16[2304,128]{1,0:T(8,128)(2,1)S(1)} %get-tuple-element.82), channel_id=1, source_target_pairs={{0,3},{1,0},{2,1},{3,2},{4,7},{5,4},{6,5},{7,6},{8,11},{9,8},{10,9... | collective-permute-start | bytes 1769480 | tf_op jit(solution)/shard_map/ppermute | solution.py:370
  221.8 12.1 %collective-permute-start.26 = (f32[2,2,128,128]{3,2,1,0:T(8,128)S(1)}, f32[2,2,128,128]{3,2,1,0:T(8,128)S(1)}, u32[]{:S(2)}, u32[]{:S(2)}) collective-permute-start(f32[2,2,128,128]{3,2,1,0:T(8,128)S(1)} %add.132), channel_id=1, source_target_pairs={{8,0},{12,4},{9,1},{13,5},{10,2},{14,6},{11,3},{15,7},{40,32},{44,... | collective-permute-start | bytes 786440 | tf_op jit(solution)/shard_map/ppermute | solution.py:401
  233.9 0.7 collective-permute-start.27
  242.0 20.4 %collective-permute-start.28 = (bf16[2,2,128,128]{3,2,1,0:T(8,128)(2,1)S(1)}, bf16[2,2,128,128]{3,2,1,0:T(8,128)(2,1)S(1)}, u32[]{:S(2)}, u32[]{:S(2)}) collective-permute-start(bf16[2,2,128,128]{3,2,1,0:T(8,128)(2,1)S(1)} %convert_element_type.28), channel_id=1, source_target_pairs={{128,0},{160,32},{192,64},{224,96},{129,1},{161,33},{193,65},{225,... | collective-permute-start | bytes 393224 | tf_op jit(solution)/shard_map/ppermute | solution.py:458
  243.3 8.3 %collective-permute-start.29 = (bf16[1,2,128,128]{3,2,1,0:T(8,128)(2,1)S(1)}, bf16[1,2,128,128]{3,2,1,0:T(8,128)(2,1)S(1)}, u32[]{:S(2)}, u32[]{:S(2)}) collective-permute-start(bf16[1,2,128,128]{3,2,1,0:T(8,128)(2,1)S(1)} %get-tuple-element.120), channel_id=1, source_target_pairs={{4,0},{8,4},{12,8},{16,12},{20,16},{24,20},{28,24},{32,28},{36,32}... | collective-permute-start | bytes 196616 | tf_op jit(solution)/shard_map/ppermute | solution.py:456
  248.5 6.0 %collective-permute-start.30 = (bf16[1,2,128,128]{3,2,1,0:T(8,128)(2,1)S(1)}, bf16[1,2,128,128]{3,2,1,0:T(8,128)(2,1)S(1)}, u32[]{:S(2)}, u32[]{:S(2)}) collective-permute-start(bf16[1,2,128,128]{3,2,1,0:T(8,128)(2,1)S(1)} %get-tuple-element.119), channel_id=1, source_target_pairs={{0,4},{4,8},{8,12},{12,16},{16,20},{20,24},{24,28},{28,32},{32,36}... | collective-permute-start | bytes 196616 | tf_op jit(solution)/shard_map/ppermute | solution.py:457
  262.5 13.8 %collective-permute-start.31 = (bf16[2,2,128,128]{3,2,1,0:T(8,128)(2,1)S(1)}, bf16[2,2,128,128]{3,2,1,0:T(8,128)(2,1)S(1)}, u32[]{:S(2)}, u32[]{:S(2)}) collective-permute-start(bf16[2,2,128,128]{3,2,1,0:T(8,128)(2,1)S(1)} %fusion), channel_id=1, source_target_pairs={{32,0},{33,1},{34,2},{35,3},{36,4},{37,5},{38,6},{39,7},{40,8},{41... | collective-permute-start | bytes 393224 | tf_op jit(solution)/shard_map/ppermute | solution.py:462
  263.8 12.5 %collective-permute-start.32 = (bf16[2,2,128,128]{3,2,1,0:T(8,128)(2,1)S(1)}, bf16[2,2,128,128]{3,2,1,0:T(8,128)(2,1)S(1)}, u32[]{:S(2)}, u32[]{:S(2)}) collective-permute-start(bf16[2,2,128,128]{3,2,1,0:T(8,128)(2,1)S(1)} %fusion), channel_id=1, source_target_pairs={{64,0},{65,1},{66,2},{67,3},{68,4},{69,5},{70,6},{71,7},{72,8},{73... | collective-permute-start | bytes 393224 | tf_op jit(solution)/shard_map/ppermute | solution.py:462
  265.1 11.2 %collective-permute-start.33 = (bf16[2,2,128,128]{3,2,1,0:T(8,128)(2,1)S(1)}, bf16[2,2,128,128]{3,2,1,0:T(8,128)(2,1)S(1)}, u32[]{:S(2)}, u32[]{:S(2)}) collective-permute-start(bf16[2,2,128,128]{3,2,1,0:T(8,128)(2,1)S(1)} %fusion), channel_id=1, source_target_pairs={{96,0},{97,1},{98,2},{99,3},{100,4},{101,5},{102,6},{103,7},{104,8... | collective-permute-start | bytes 393224 | tf_op jit(solution)/shard_map/ppermute | solution.py:462
  (23 other events, 37.3 us)

commit v6 on v5

--- a/solution.py
+++ b/solution.py
@@ -425,22 +425,25 @@
     kvs = jnp.stack([k, v]).transpose(2, 0, 1, 3)
     kv, meta, lp = tie(plain_a2a(kvs, "head"), meta, lp)
     kv = kv.transpose(1, 0, 2, 3).reshape(2, QB, BLK, HD).transpose(1, 0, 2, 3)
-    u1, d1, q1, q3 = tie(along_z(kv, 1), along_z(kv, -1), turn(qp[1], 1), turn(qp[3], 3))
-    u2, d2, q2 = tie(along_z(u1, 1), along_z(d1, -1), turn(qp[2], 2))
+    u1, d1, q1, q3, lp[1] = tie(
+        along_z(kv, 1), along_z(kv, -1), turn(qp[1], 1), turn(qp[3], 3), turn(lp[1], 1)
+    )
+    u2, d2, q2, lp[2], lp[3] = tie(
+        along_z(u1, 1), along_z(d1, -1), turn(qp[2], 2), turn(lp[2], 2), turn(lp[3], 3)
+    )
     near = plain_a2a(call_select(meta, NEAR, [kv, d1, d2, u2, u1]), ("x", "c"))
     u3, d3, do1, do3 = tie(
         along_z(u2, 1), along_z(d2, -1), turn(dop[1], 1), turn(dop[3], 3)
     )
-    u4, d4, do2 = tie(along_z(u3[:CUT], 1), along_z(d3[CUT:], -1), turn(dop[2], 2))
+    ld = jnp.roll(jnp.stack(lp[::-1]), head + 1, axis=0)
+    ld = ld.transpose(1, 0, 2, 3).reshape(2, QB, HL, BLK)
+    u4, d4, do2, ld = tie(along_z(u3[:CUT], 1), along_z(d3[CUT:], -1), turn(dop[2], 2), ld)
     near, u4 = tie(near, u4)
     far, edges = tie(call_select(meta, FAR, [d3, u4, u3, d4]), kv)
     far = plain_a2a(far, ("x", "c"))
     before = lax.ppermute(edges[QB - 1 :], SEQ, up)
     after = lax.ppermute(edges[:1], SEQ, down)
     ql, dol = (qp[0], q1, q2, q3), (dop[0], do1, do2, do3)
-    ld = jnp.stack([turn(p, i) for i, p in enumerate(lp)])
-    ld = jnp.roll(ld[::-1], head + 1, axis=0)
-    ld = ld.transpose(1, 0, 2, 3).reshape(2, QB, HL, BLK)
 
     dqt, back = call_random(meta, ql, dol, ld, near, far)
     gl, back, before, after = tie(kv[:G], back, before, after)

time: 301 us -> 300 us (level)
  starting transfers between devices: 101 us -> 87.5 us
  waiting for transfers between devices: 92.4 us -> 101 us
  local copies, waits for them, and re-layouts: 27.5 us -> 33.1 us
    ppermute x8, starting transfers between devices: 26.8 us -> 15.7 us  [along_z(): return lax.ppermute(value, 'z', [(i, (i + step) % NZ) for i in range(NZ)])]
    ppermute x8, waiting for transfers between devices: 25.8 us -> 15.4 us  [along_z(): return lax.ppermute(value, 'z', [(i, (i + step) % NZ) for i in range(NZ)])]
    ppermute x12, waiting for transfers between devices: 15 us -> 24.5 us  [turn(): lax.ppermute(value, 'head', [(i, (i + k) % NH) for i in range(NH)])]
    all_to_all x4, waiting for transfers between devices: 3.27 us -> 11.9 us  [plain_a2a(): return lax.all_to_all(value, axis, split_axis=0, concat_axis=0, tiled=True)]
    ppermute x12, starting transfers between devices: 23.7 us -> 19.2 us  [turn(): lax.ppermute(value, 'head', [(i, (i + k) % NH) for i in range(NH)])]
    unnamed x68 -> x73, local copies, waits for them, and re-layouts: 15.2 us -> 19 us
    ppermute x3, waiting for transfers between devices: 11.7 us -> 15 us  [gather_sum(): lax.ppermute(value, ('x', 'c'), [(i + k, i) for i in range(k)])]
  transfers between devices with their start and end apart: 38 -> 38, of which waited for: 20 -> 16; matrix products, arithmetic and copies ran while one was open for 7% -> 9% of each run, Pallas kernels for 14% -> 14%
where the time goes in v6:
time: 300 us; the launch traced here: 298 us
  waiting for transfers between devices  101 us (34%)
  starting transfers between devices  87.5 us (29%)
  Pallas kernels  50.7 us (17%)
  local copies, waits for them, and re-layouts  33.1 us (11%)
  blocking collectives  15.8 us (5%)
  other arithmetic  8.58 us (3%)
    ppermute x12, waiting for transfers between devices, turn(): lax.ppermute(value, 'head', [(i, (i + k) % NH) for i in range(NH)])  24.5 us
    pallas_call x1, Pallas kernels, call_near(): pl.pallas_call(near_kernel, grid_spec=pltpu.PrefetchScalarGridSpec(num_sc...  22.2 us
    all_to_all x4, starting transfers between devices, plain_a2a(): return lax.all_to_all(value, axis, split_axis=0, concat_axis=0, tiled=True)  22.1 us
    ppermute x12, starting transfers between devices, turn(): lax.ppermute(value, 'head', [(i, (i + k) % NH) for i in range(NH)])  19.2 us
    unnamed x73, local copies, waits for them, and re-layouts  19 us
    all_to_all x1, blocking collectives, plain_a2a(): return lax.all_to_all(value, axis, split_axis=0, concat_axis=0, tiled=True)  15.8 us
    ppermute x8, starting transfers between devices, along_z(): return lax.ppermute(value, 'z', [(i, (i + step) % NZ) for i in range(NZ)])  15.7 us
    ppermute x8, waiting for transfers between devices, along_z(): return lax.ppermute(value, 'z', [(i, (i + step) % NZ) for i in range(NZ)])  15.4 us
  transfers between devices with their start and end apart: 38, of which 16 were waited for; matrix products, arithmetic and copies ran while one was open for 9% of the time, Pallas kernels for 14%

profile of v6, /device:TPU:2, one launch (start us, length us, event | category | flops | bytes accessed | tf_op | source)
XLA Modules:
  0.0 297.8 jit_solution(14943910491883727811)
XLA Ops:
  2.8 4.5 %all-to-all-start = ((bf16[4,2,288,128]{3,2,1,0:T(8,128)(2,1)}), bf16[4,2,288,128]{3,2,1,0:T(8,128)(2,1)}, u32[]{:S(2)}, u32[]{:S(2)}) async-start(bf16[4,2,288,128]{3,2,1,0:T(8,128)(2,1)} %maximum_bitcast_fusion), calls=%async_computation | async-start | bytes 1179648 | tf_op jit(solution)/shard_map/all_to_all | solution.py:366
  7.3 1.4 dynamic-slice_bitcast_fusion.4
  8.7 2.0 collective-permute-start.2
  11.9 3.7 %multiply_reduce_fusion = f32[288,32]{1,0:T(8,128)S(1)} fusion(bf16[288,32,128]{2,1,0:T(8,128)(2,1)} %param.11, bf16[288,32,128]{2,1,0:T(8,128)(2,1)} %param.12), kind=kLoop, calls=%fused_computation | loop fusion | flops 4709376 | bytes 4755456 | tf_op jit(solution)/shard_map/reduce_sum | solution.py:419
  20.2 2.0 collective-permute-start
  22.2 4.0 %collective-permute-start.1 = (bf16[9,2,128,128]{3,2,1,0:T(8,128)(2,1)S(1)}, bf16[9,2,128,128]{3,2,1,0:T(8,128)(2,1)S(1)}, u32[]{:S(2)}, u32[]{:S(2)}) collective-permute-start(bf16[9,2,128,128]{3,2,1,0:T(8,128)(2,1)S(1)} %bitcast.103), channel_id=1, source_target_pairs={{0,224},{32,0},{64,32},{96,64},{128,96},{160,128},{192,160},{224,1... | collective-permute-start | bytes 1769480 | tf_op jit(solution)/shard_map/ppermute | solution.py:386
  27.1 4.2 %collective-permute-done.4 = f32[2,18,128]{2,0,1:T(2,128)S(1)} collective-permute-done((f32[2,18,128]{2,0,1:T(2,128)S(1)}, f32[2,18,128]{2,0,1:T(2,128)S(1)}, u32[]{:S(2)}, u32[]{:S(2)}) %collective-permute-start.4) | collective-permute-done | bytes 18464 | tf_op jit(solution)/shard_map/ppermute | solution.py:370
  32.9 5.8 %collective-permute-done.refs_4_ = bf16[9,2,128,128]{3,2,1,0:T(8,128)(2,1)S(1)} collective-permute-done((bf16[9,2,128,128]{3,2,1,0:T(8,128)(2,1)S(1)}, bf16[9,2,128,128]{3,2,1,0:T(8,128)(2,1)S(1)}, u32[]{:S(2)}, u32[]{:S(2)}) %collective-permute-start) | collective-permute-done | bytes 589856 | tf_op jit(solution)/shard_map/ppermute | solution.py:386
  38.7 3.2 %collective-permute-start.6 = (bf16[9,2,128,128]{3,2,1,0:T(8,128)(2,1)S(1)}, bf16[9,2,128,128]{3,2,1,0:T(8,128)(2,1)S(1)}, u32[]{:S(2)}, u32[]{:S(2)}) collective-permute-start(bf16[9,2,128,128]{3,2,1,0:T(8,128)(2,1)S(1)} %collective-permute-done.1.refs_1_), channel_id=1, source_target_pairs={{0,224},{32,0},{64,32},{96,64},{128,96},{160,128},{192,160},{224,1... | collective-permute-start | bytes 1769480 | tf_op jit(solution)/shard_map/ppermute | solution.py:386
  42.0 2.0 collective-permute-start.8
  45.1 2.3 collective-permute-done.8
  47.7 5.9 %collective-permute-done.5.refs_3_ = bf16[9,2,128,128]{3,2,1,0:T(8,128)(2,1)S(1)} collective-permute-done((bf16[9,2,128,128]{3,2,1,0:T(8,128)(2,1)S(1)}, bf16[9,2,128,128]{3,2,1,0:T(8,128)(2,1)S(1)}, u32[]{:S(2)}, u32[]{:S(2)}) %collective-permute-start.5) | collective-permute-done | bytes 589856 | tf_op jit(solution)/shard_map/ppermute | solution.py:386
  53.6 2.4 select.20
  58.6 4.8 %all-to-all-start.1 = ((bf16[40,2,128,128]{3,2,1,0:T(8,128)(2,1)}), bf16[40,2,128,128]{3,2,1,0:T(8,128)(2,1)}, u32[]{:S(2)}, u32[]{:S(2)}) async-start(bf16[40,2,128,128]{3,2,1,0:T(8,128)(2,1)} %select.20), calls=%async_computation.1 | async-start | bytes 5242880 | tf_op jit(solution)/shard_map/all_to_all | solution.py:366
  63.4 2.9 dynamic-slice_bitcast_fusion
  66.4 3.2 %collective-permute-start.13 = (bf16[2304,128]{1,0:T(8,128)(2,1)}, bf16[2304,128]{1,0:T(8,128)(2,1)}, u32[]{:S(2)}, u32[]{:S(2)}) collective-permute-start(bf16[2304,128]{1,0:T(8,128)(2,1)} %get-tuple-element.120), channel_id=1, source_target_pairs={{0,3},{1,0},{2,1},{3,2},{4,7},{5,4},{6,5},{7,6},{8,11},{9,8},{10,9... | collective-permute-start | bytes 1769480 | tf_op jit(solution)/shard_map/ppermute | solution.py:370
  69.9 1.9 collective-permute-start.10
  71.8 1.3 collective-permute-start.11
  78.3 17.6 %collective-permute-done.12.d1 = bf16[2304,128]{1,0:T(8,128)(2,1)} collective-permute-done((bf16[2304,128]{1,0:T(8,128)(2,1)}, bf16[2304,128]{1,0:T(8,128)(2,1)}, u32[]{:S(2)}, u32[]{:S(2)}) %collective-permute-start.12) | collective-permute-done | bytes 589856 | tf_op jit(solution)/shard_map/ppermute | solution.py:370
  96.7 1.9 collective-permute-start.14
  99.5 1.3 collective-permute-start.15
  102.2 3.7 %collective-permute-done.15.refs_3_ = bf16[4,2,128,128]{3,2,1,0:T(8,128)(2,1)S(1)} collective-permute-done((bf16[4,2,128,128]{3,2,1,0:T(8,128)(2,1)S(1)}, bf16[4,2,128,128]{3,2,1,0:T(8,128)(2,1)S(1)}, u32[]{:S(2)}, u32[]{:S(2)}) %collective-permute-start.15) | collective-permute-done | bytes 262176 | tf_op jit(solution)/shard_map/ppermute | solution.py:386
  111.3 1.9 select.21
  113.3 4.8 %all-to-all-start.2 = ((bf16[24,2,128,128]{3,2,1,0:T(8,128)(2,1)}), bf16[24,2,128,128]{3,2,1,0:T(8,128)(2,1)}, u32[]{:S(2)}, u32[]{:S(2)}) async-start(bf16[24,2,128,128]{3,2,1,0:T(8,128)(2,1)} %select.21), calls=%async_computation.2 | async-start | bytes 3145728 | tf_op jit(solution)/shard_map/all_to_all | solution.py:366
  118.8 2.0 collective-permute-start.17
  120.8 3.5 %collective-permute-start.18 = (bf16[1,2,128,128]{3,2,1,0:T(8,128)(2,1)}, bf16[1,2,128,128]{3,2,1,0:T(8,128)(2,1)}, u32[]{:S(2)}, u32[]{:S(2)}) collective-permute-start(bf16[1,2,128,128]{3,2,1,0:T(8,128)(2,1)} %get-tuple-element.131), channel_id=1, source_target_pairs={{4,0},{8,4},{12,8},{16,12},{20,16},{24,20},{28,24},{32,28},{36,32}... | collective-permute-start | bytes 196616 | tf_op jit(solution)/shard_map/ppermute | solution.py:445
  125.0 1.5 copy.109.ld_ref
  126.5 11.9 %all-to-all-done.2.far_ref = bf16[24,2,128,128]{3,2,1,0:T(8,128)(2,1)} async-done(((bf16[24,2,128,128]{3,2,1,0:T(8,128)(2,1)}), bf16[24,2,128,128]{3,2,1,0:T(8,128)(2,1)}, u32[]{:S(2)}, u32[]{:S(2)}) %all-to-all-start.2) | async-done | bytes 1572896 | tf_op jit(solution)/shard_map/all_to_all | solution.py:366
  139.3 14.4 %random.1 = (f32[9,128,1024]{2,1,0:T(8,128)}, bf16[64,2,128,128]{3,2,1,0:T(8,128)(2,1)}) custom-call(s32[158]{0:T(256)S(1)} %concatenate.12.meta, bf16[2304,128]{1,0:T(8,128)(2,1)S(1)} %get-tuple-element.126.q0, bf16[2304,128]{1,0:T(8,128)(2,1)S(1)} %collective-permute-done.2.q1, bf16[2304,128]{1,0:T(8,128)(2,1)S(1)} %collective-permute-done.7.q2, ...), custom_call_target="tpu_custom_call" | custom-call | tf_op jit(solution)/shard_map/random/pallas_call | solution.py:285
  153.7 8.0 %all-to-all-start.3 = ((bf16[64,2,128,128]{3,2,1,0:T(8,128)(2,1)}), bf16[64,2,128,128]{3,2,1,0:T(8,128)(2,1)}, u32[]{:S(2)}, u32[]{:S(2)}) async-start(bf16[64,2,128,128]{3,2,1,0:T(8,128)(2,1)} %get-tuple-element.99), calls=%async_computation.3 | async-start | bytes 8388608 | tf_op jit(solution)/shard_map/all_to_all | solution.py:366
  161.8 1.3 select_bitcast_fusion
  165.2 11.7 %collective-permute-done.20 = bf16[4,128,128]{2,1,0:T(8,128)(2,1)S(1)} collective-permute-done((bf16[4,128,128]{2,1,0:T(8,128)(2,1)S(1)}, bf16[4,128,128]{2,1,0:T(8,128)(2,1)S(1)}, u32[]{:S(2)}, u32[]{:S(2)}) %collective-permute-start.20) | collective-permute-done | bytes 131104 | tf_op jit(solution)/shard_map/ppermute | solution.py:392
  176.9 1.3 collective-permute-start.21
  178.2 1.8 pad_maximum_fusion.kv_ref
  180.0 3.3 %collective-permute-done.21 = bf16[4,128,128]{2,1,0:T(8,128)(2,1)S(1)} collective-permute-done((bf16[4,128,128]{2,1,0:T(8,128)(2,1)S(1)}, bf16[4,128,128]{2,1,0:T(8,128)(2,1)S(1)}, u32[]{:S(2)}, u32[]{:S(2)}) %collective-permute-start.21) | collective-permute-done | bytes 131104 | tf_op jit(solution)/shard_map/ppermute | solution.py:392
  183.3 22.2 %near.1 = (bf16[2304,128]{1,0:T(8,128)(2,1)S(1)}, bf16[2304,128]{1,0:T(8,128)(2,1)S(1)}, bf16[2304,128]{1,0:T(8,128)(2,1)S(1)}, bf16[2304,128]{1,0:T(8,128)(2,1)...) custom-call(s32[158]{0:T(256)S(1)} %concatenate.12.meta, bf16[2304,128]{1,0:T(8,128)(2,1)S(1)} %get-tuple-element.126.q0, ...), custom_call_target="tpu_custom_call" | custom-call | tf_op jit(solution)/shard_map/near/pallas_call | solution.py:263
  206.9 7.2 %collective-permute-start.23 = (bf16[2304,128]{1,0:T(8,128)(2,1)S(1)}, bf16[2304,128]{1,0:T(8,128)(2,1)S(1)}, u32[]{:S(2)}, u32[]{:S(2)}) collective-permute-start(bf16[2304,128]{1,0:T(8,128)(2,1)S(1)} %get-tuple-element.89), channel_id=1, source_target_pairs={{0,2},{1,3},{2,0},{3,1},{4,6},{5,7},{6,4},{7,5},{8,10},{9,11},{10,... | collective-permute-start | bytes 1769480 | tf_op jit(solution)/shard_map/ppermute | solution.py:370
  214.2 5.9 %collective-permute-done.25 = f32[2,2,128,128]{3,2,1,0:T(8,128)S(1)} collective-permute-done((f32[2,2,128,128]{3,2,1,0:T(8,128)S(1)}, f32[2,2,128,128]{3,2,1,0:T(8,128)S(1)}, u32[]{:S(2)}, u32[]{:S(2)}) %collective-permute-start.25) | collective-permute-done | bytes 262176 | tf_op jit(solution)/shard_map/ppermute | solution.py:401
  220.2 5.7 %collective-permute-start.26 = (f32[2,2,128,128]{3,2,1,0:T(8,128)S(1)}, f32[2,2,128,128]{3,2,1,0:T(8,128)S(1)}, u32[]{:S(2)}, u32[]{:S(2)}) collective-permute-start(f32[2,2,128,128]{3,2,1,0:T(8,128)S(1)} %add.132), channel_id=1, source_target_pairs={{8,0},{12,4},{9,1},{13,5},{10,2},{14,6},{11,3},{15,7},{40,32},{44,... | collective-permute-start | bytes 786440 | tf_op jit(solution)/shard_map/ppermute | solution.py:401
  225.8 9.0 %collective-permute-done.26 = f32[2,2,128,128]{3,2,1,0:T(8,128)S(1)} collective-permute-done((f32[2,2,128,128]{3,2,1,0:T(8,128)S(1)}, f32[2,2,128,128]{3,2,1,0:T(8,128)S(1)}, u32[]{:S(2)}, u32[]{:S(2)}) %collective-permute-start.26) | collective-permute-done | bytes 262176 | tf_op jit(solution)/shard_map/ppermute | solution.py:401
  236.9 4.2 %join.1 = bf16[288,4,8,128]{3,2,1,0:T(8,128)(2,1)} custom-call(s32[1]{0:T(128)} %bitcast.head, bf16[288,8,128]{2,1,0:T(8,128)(2,1)} %bitcast.109, bf16[288,8,128]{2,1,0:T(8,128)(2,1)} %bitcast.115, bf16[288,8,128]{2,1,0:T(8,128)(2,1)} %bitcast.116, bf16[288,8,128]{2,1,0:T(8,128)(2,1)} %bitcast.117), custom_call_target="tpu_custom_call" | custom-call | tf_op jit(solution)/shard_map/join/pallas_call | solution.py:352
  242.6 6.9 %collective-permute-start.29 = (bf16[1,2,128,128]{3,2,1,0:T(8,128)(2,1)S(1)}, bf16[1,2,128,128]{3,2,1,0:T(8,128)(2,1)S(1)}, u32[]{:S(2)}, u32[]{:S(2)}) collective-permute-start(bf16[1,2,128,128]{3,2,1,0:T(8,128)(2,1)S(1)} %get-tuple-element.128), channel_id=1, source_target_pairs={{4,0},{8,4},{12,8},{16,12},{20,16},{24,20},{28,24},{32,28},{36,32}... | collective-permute-start | bytes 196616 | tf_op jit(solution)/shard_map/ppermute | solution.py:459
  249.5 1.9 collective-permute-start.30
  251.4 3.6 %collective-permute-done.30.upper = bf16[1,2,128,128]{3,2,1,0:T(8,128)(2,1)S(1)} collective-permute-done((bf16[1,2,128,128]{3,2,1,0:T(8,128)(2,1)S(1)}, bf16[1,2,128,128]{3,2,1,0:T(8,128)(2,1)S(1)}, u32[]{:S(2)}, u32[]{:S(2)}) %collective-permute-start.30) | collective-permute-done | bytes 65568 | tf_op jit(solution)/shard_map/ppermute | solution.py:460
  255.1 5.6 %collective-permute-done.28 = bf16[2,2,128,128]{3,2,1,0:T(8,128)(2,1)S(1)} collective-permute-done((bf16[2,2,128,128]{3,2,1,0:T(8,128)(2,1)S(1)}, bf16[2,2,128,128]{3,2,1,0:T(8,128)(2,1)S(1)}, u32[]{:S(2)}, u32[]{:S(2)}) %collective-permute-start.28) | collective-permute-done | bytes 131104 | tf_op jit(solution)/shard_map/ppermute | solution.py:461
  264.6 9.9 %collective-permute-done.31 = bf16[2,2,128,128]{3,2,1,0:T(8,128)(2,1)S(1)} collective-permute-done((bf16[2,2,128,128]{3,2,1,0:T(8,128)(2,1)S(1)}, bf16[2,2,128,128]{3,2,1,0:T(8,128)(2,1)S(1)}, u32[]{:S(2)}, u32[]{:S(2)}) %collective-permute-start.31) | collective-permute-done | bytes 131104 | tf_op jit(solution)/shard_map/ppermute | solution.py:465
  274.7 5.5 %collect.1 = bf16[9,2,128,128]{3,2,1,0:T(8,128)(2,1)S(1)} custom-call(s32[158]{0:T(256)S(1)} %concatenate.12.meta, bf16[64,2,128,128]{3,2,1,0:T(8,128)(2,1)} %all-to-all-done.3.got, f32[11,2,128,128]{3,2,1,0:T(8,128)S(1)} %copy-done, bf16[1,2,128,128]{3,2,1,0:T(8,128)(2,1)S(1)} %collective-permute-done.29.lower, ...), custom_call_target="tpu_custom_call" | custom-call | tf_op jit(solution)/shard_map/collect/pallas_call | solution.py:330
  280.3 15.8 %all_to_all.25 = bf16[4,2,288,128]{3,2,1,0:T(8,128)(2,1)S(1)} all-to-all(bf16[4,2,288,128]{3,2,1,0:T(8,128)(2,1)S(1)} %copy.111), channel_id=1, replica_groups=mesh['z'=8,'x'=4,'c'=2,'head'=4] {'head'}, dimensions={0} | all-to-all | bytes 1179648 | tf_op jit(solution)/shard_map/all_to_all | solution.py:366
  (158 shorter events, 43.5 us)
Async XLA Ops:
  0.6 6.6 %copy-start.19 = (bf16[288,32,128]{2,1,0:T(8,128)(2,1)S(1)}, bf16[288,32,128]{2,1,0:T(8,128)(2,1)}, u32[]{:S(2)}) copy-start(bf16[288,32,128]{2,1,0:T(8,128)(2,1)} %param.8) | copy-start | bytes 7077892
  2.8 16.3 %all-to-all-start = ((bf16[4,2,288,128]{3,2,1,0:T(8,128)(2,1)}), bf16[4,2,288,128]{3,2,1,0:T(8,128)(2,1)}, u32[]{:S(2)}, u32[]{:S(2)}) async-start(bf16[4,2,288,128]{3,2,1,0:T(8,128)(2,1)} %maximum_bitcast_fusion), calls=%async_computation | async-start | bytes 1179648 | tf_op jit(solution)/shard_map/all_to_all | solution.py:366
  8.7 24.2 %collective-permute-start.2 = (bf16[2304,128]{1,0:T(8,128)(2,1)}, bf16[2304,128]{1,0:T(8,128)(2,1)S(1)}, u32[]{:S(2)}, u32[]{:S(2)}) collective-permute-start(bf16[2304,128]{1,0:T(8,128)(2,1)} %get-tuple-element.125), channel_id=1, source_target_pairs={{0,1},{1,2},{2,3},{3,0},{4,5},{5,6},{6,7},{7,4},{8,9},{9,10},{10,1... | collective-permute-start | bytes 1769480 | tf_op jit(solution)/shard_map/ppermute | solution.py:370
  10.7 22.2 %collective-permute-start.3 = (bf16[2304,128]{1,0:T(8,128)(2,1)}, bf16[2304,128]{1,0:T(8,128)(2,1)S(1)}, u32[]{:S(2)}, u32[]{:S(2)}) collective-permute-start(bf16[2304,128]{1,0:T(8,128)(2,1)} %get-tuple-element.124), channel_id=1, source_target_pairs={{0,3},{1,0},{2,1},{3,2},{4,7},{5,4},{6,5},{7,6},{8,11},{9,8},{10,9... | collective-permute-start | bytes 1769480 | tf_op jit(solution)/shard_map/ppermute | solution.py:370
  19.1 22.9 %copy-start.29 = (f32[2,18,128]{2,0,1:T(2,128)S(1)}, f32[2,18,128]{2,0,1:T(2,128)}, u32[]{:S(2)}) copy-start(f32[2,18,128]{2,0,1:T(2,128)} %get-tuple-element.60) | copy-start | bytes 55300
  19.1 24.9 %copy-start.28 = (f32[2,18,128]{2,0,1:T(2,128)S(1)}, f32[2,18,128]{2,0,1:T(2,128)}, u32[]{:S(2)}) copy-start(f32[2,18,128]{2,0,1:T(2,128)} %get-tuple-element.61) | copy-start | bytes 55300
  20.2 18.5 %collective-permute-start = (bf16[9,2,128,128]{3,2,1,0:T(8,128)(2,1)S(1)}, bf16[9,2,128,128]{3,2,1,0:T(8,128)(2,1)S(1)}, u32[]{:S(2)}, u32[]{:S(2)}) collective-permute-start(bf16[9,2,128,128]{3,2,1,0:T(8,128)(2,1)S(1)} %bitcast.102), channel_id=1, source_target_pairs={{0,32},{32,64},{64,96},{96,128},{128,160},{160,192},{192,224},{224... | collective-permute-start | bytes 1769480 | tf_op jit(solution)/shard_map/ppermute | solution.py:386
  22.2 16.5 %collective-permute-start.1 = (bf16[9,2,128,128]{3,2,1,0:T(8,128)(2,1)S(1)}, bf16[9,2,128,128]{3,2,1,0:T(8,128)(2,1)S(1)}, u32[]{:S(2)}, u32[]{:S(2)}) collective-permute-start(bf16[9,2,128,128]{3,2,1,0:T(8,128)(2,1)S(1)} %bitcast.103), channel_id=1, source_target_pairs={{0,224},{32,0},{64,32},{96,64},{128,96},{160,128},{192,160},{224,1... | collective-permute-start | bytes 1769480 | tf_op jit(solution)/shard_map/ppermute | solution.py:386
  26.2 5.0 %collective-permute-start.4 = (f32[2,18,128]{2,0,1:T(2,128)S(1)}, f32[2,18,128]{2,0,1:T(2,128)S(1)}, u32[]{:S(2)}, u32[]{:S(2)}) collective-permute-start(f32[2,18,128]{2,0,1:T(2,128)S(1)} %get-tuple-element.56), channel_id=1, source_target_pairs={{0,1},{1,2},{2,3},{3,0},{4,5},{5,6},{6,7},{7,4},{8,9},{9,10},{10,1... | collective-permute-start | bytes 55304 | tf_op jit(solution)/shard_map/ppermute | solution.py:370
  31.8 15.9 %collective-permute-start.7 = (bf16[2304,128]{1,0:T(8,128)(2,1)}, bf16[2304,128]{1,0:T(8,128)(2,1)S(1)}, u32[]{:S(2)}, u32[]{:S(2)}) collective-permute-start(bf16[2304,128]{1,0:T(8,128)(2,1)} %get-tuple-element.123), channel_id=1, source_target_pairs={{0,2},{1,3},{2,0},{3,1},{4,6},{5,7},{6,4},{7,5},{8,10},{9,11},{10,... | collective-permute-start | bytes 1769480 | tf_op jit(solution)/shard_map/ppermute | solution.py:370
  32.9 105.5 %copy-start.2 = (bf16[2304,128]{1,0:T(8,128)(2,1)}, bf16[2304,128]{1,0:T(8,128)(2,1)S(1)}, u32[]{:S(2)}) copy-start(bf16[2304,128]{1,0:T(8,128)(2,1)S(1)} %collective-permute-done.3.q3) | copy-start | bytes 1769476
  38.7 17.3 %copy-start.9 = (bf16[9,2,128,128]{3,2,1,0:T(8,128)(2,1)}, bf16[9,2,128,128]{3,2,1,0:T(8,128)(2,1)S(1)}, u32[]{:S(2)}) copy-start(bf16[9,2,128,128]{3,2,1,0:T(8,128)(2,1)S(1)} %collective-permute-done.1.refs_1_) | copy-start | bytes 1769476
  38.7 14.9 %collective-permute-start.5 = (bf16[9,2,128,128]{3,2,1,0:T(8,128)(2,1)S(1)}, bf16[9,2,128,128]{3,2,1,0:T(8,128)(2,1)S(1)}, u32[]{:S(2)}, u32[]{:S(2)}) collective-permute-start(bf16[9,2,128,128]{3,2,1,0:T(8,128)(2,1)S(1)} %collective-permute-done.refs_4_), channel_id=1, source_target_pairs={{0,32},{32,64},{64,96},{96,128},{128,160},{160,192},{192,224},{224... | collective-permute-start | bytes 1769480 | tf_op jit(solution)/shard_map/ppermute | solution.py:386
  38.7 14.9 %collective-permute-start.6 = (bf16[9,2,128,128]{3,2,1,0:T(8,128)(2,1)S(1)}, bf16[9,2,128,128]{3,2,1,0:T(8,128)(2,1)S(1)}, u32[]{:S(2)}, u32[]{:S(2)}) collective-permute-start(bf16[9,2,128,128]{3,2,1,0:T(8,128)(2,1)S(1)} %collective-permute-done.1.refs_1_), channel_id=1, source_target_pairs={{0,224},{32,0},{64,32},{96,64},{128,96},{160,128},{192,160},{224,1... | collective-permute-start | bytes 1769480 | tf_op jit(solution)/shard_map/ppermute | solution.py:386
  42.0 5.4 %collective-permute-start.8 = (f32[2,18,128]{2,0,1:T(2,128)S(1)}, f32[2,18,128]{2,0,1:T(2,128)S(1)}, u32[]{:S(2)}, u32[]{:S(2)}) collective-permute-start(f32[2,18,128]{2,0,1:T(2,128)S(1)} %copy-done.29), channel_id=1, source_target_pairs={{0,2},{1,3},{2,0},{3,1},{4,6},{5,7},{6,4},{7,5},{8,10},{9,11},{10,... | collective-permute-start | bytes 55304 | tf_op jit(solution)/shard_map/ppermute | solution.py:370
  43.9 3.8 %collective-permute-start.9 = (f32[2,18,128]{2,0,1:T(2,128)S(1)}, f32[2,18,128]{2,0,1:T(2,128)S(1)}, u32[]{:S(2)}, u32[]{:S(2)}) collective-permute-start(f32[2,18,128]{2,0,1:T(2,128)S(1)} %copy-done.28), channel_id=1, source_target_pairs={{0,3},{1,0},{2,1},{3,2},{4,7},{5,4},{6,5},{7,6},{8,11},{9,8},{10,9... | collective-permute-start | bytes 55304 | tf_op jit(solution)/shard_map/ppermute | solution.py:370
  47.7 90.7 %copy-start.3 = (bf16[2304,128]{1,0:T(8,128)(2,1)}, bf16[2304,128]{1,0:T(8,128)(2,1)S(1)}, u32[]{:S(2)}) copy-start(bf16[2304,128]{1,0:T(8,128)(2,1)S(1)} %collective-permute-done.7.q2) | copy-start | bytes 1769476
  58.6 48.7 %all-to-all-start.1 = ((bf16[40,2,128,128]{3,2,1,0:T(8,128)(2,1)}), bf16[40,2,128,128]{3,2,1,0:T(8,128)(2,1)}, u32[]{:S(2)}, u32[]{:S(2)}) async-start(bf16[40,2,128,128]{3,2,1,0:T(8,128)(2,1)} %select.20), calls=%async_computation.1 | async-start | bytes 5242880 | tf_op jit(solution)/shard_map/all_to_all | solution.py:366
  66.3 72.1 %copy-start.1 = (bf16[2304,128]{1,0:T(8,128)(2,1)}, bf16[2304,128]{1,0:T(8,128)(2,1)S(1)}, u32[]{:S(2)}) copy-start(bf16[2304,128]{1,0:T(8,128)(2,1)S(1)} %get-tuple-element.122.d0) | copy-start | bytes 1769476
  66.3 29.5 %collective-permute-start.12 = (bf16[2304,128]{1,0:T(8,128)(2,1)}, bf16[2304,128]{1,0:T(8,128)(2,1)}, u32[]{:S(2)}, u32[]{:S(2)}) collective-permute-start(bf16[2304,128]{1,0:T(8,128)(2,1)} %get-tuple-element.121), channel_id=1, source_target_pairs={{0,1},{1,2},{2,3},{3,0},{4,5},{5,6},{6,7},{7,4},{8,9},{9,10},{10,1... | collective-permute-start | bytes 1769480 | tf_op jit(solution)/shard_map/ppermute | solution.py:370
  66.4 29.5 %collective-permute-start.13 = (bf16[2304,128]{1,0:T(8,128)(2,1)}, bf16[2304,128]{1,0:T(8,128)(2,1)}, u32[]{:S(2)}, u32[]{:S(2)}) collective-permute-start(bf16[2304,128]{1,0:T(8,128)(2,1)} %get-tuple-element.120), channel_id=1, source_target_pairs={{0,3},{1,0},{2,1},{3,2},{4,7},{5,4},{6,5},{7,6},{8,11},{9,8},{10,9... | collective-permute-start | bytes 1769480 | tf_op jit(solution)/shard_map/ppermute | solution.py:370
  69.6 32.6 %collective-permute-start.16 = (bf16[2304,128]{1,0:T(8,128)(2,1)}, bf16[2304,128]{1,0:T(8,128)(2,1)}, u32[]{:S(2)}, u32[]{:S(2)}) collective-permute-start(bf16[2304,128]{1,0:T(8,128)(2,1)} %get-tuple-element.119), channel_id=1, source_target_pairs={{0,2},{1,3},{2,0},{3,1},{4,6},{5,7},{6,4},{7,5},{8,10},{9,11},{10,... | collective-permute-start | bytes 1769480 | tf_op jit(solution)/shard_map/ppermute | solution.py:370
  69.9 25.9 %collective-permute-start.10 = (bf16[9,2,128,128]{3,2,1,0:T(8,128)(2,1)}, bf16[9,2,128,128]{3,2,1,0:T(8,128)(2,1)S(1)}, u32[]{:S(2)}, u32[]{:S(2)}) collective-permute-start(bf16[9,2,128,128]{3,2,1,0:T(8,128)(2,1)} %copy-done.10), channel_id=1, source_target_pairs={{0,32},{32,64},{64,96},{96,128},{128,160},{160,192},{192,224},{224... | collective-permute-start | bytes 1769480 | tf_op jit(solution)/shard_map/ppermute | solution.py:386
  71.8 24.0 %collective-permute-start.11 = (bf16[9,2,128,128]{3,2,1,0:T(8,128)(2,1)}, bf16[9,2,128,128]{3,2,1,0:T(8,128)(2,1)S(1)}, u32[]{:S(2)}, u32[]{:S(2)}) collective-permute-start(bf16[9,2,128,128]{3,2,1,0:T(8,128)(2,1)} %copy-done.11), channel_id=1, source_target_pairs={{0,224},{32,0},{64,32},{96,64},{128,96},{160,128},{192,160},{224,1... | collective-permute-start | bytes 1769480 | tf_op jit(solution)/shard_map/ppermute | solution.py:386
  96.7 9.8 %collective-permute-start.14 = (bf16[5,2,128,128]{3,2,1,0:T(8,128)(2,1)S(1)}, bf16[5,2,128,128]{3,2,1,0:T(8,128)(2,1)S(1)}, u32[]{:S(2)}, u32[]{:S(2)}) collective-permute-start(bf16[5,2,128,128]{3,2,1,0:T(8,128)(2,1)S(1)} %slice.50), channel_id=1, source_target_pairs={{0,32},{32,64},{64,96},{96,128},{128,160},{160,192},{192,224},{224... | collective-permute-start | bytes 983048 | tf_op jit(solution)/shard_map/ppermute | solution.py:386
  99.5 6.4 %collective-permute-start.15 = (bf16[4,2,128,128]{3,2,1,0:T(8,128)(2,1)S(1)}, bf16[4,2,128,128]{3,2,1,0:T(8,128)(2,1)S(1)}, u32[]{:S(2)}, u32[]{:S(2)}) collective-permute-start(bf16[4,2,128,128]{3,2,1,0:T(8,128)(2,1)S(1)} %slice.51), channel_id=1, source_target_pairs={{0,224},{32,0},{64,32},{96,64},{128,96},{160,128},{192,160},{224,1... | collective-permute-start | bytes 786440 | tf_op jit(solution)/shard_map/ppermute | solution.py:386
  113.3 25.1 %all-to-all-start.2 = ((bf16[24,2,128,128]{3,2,1,0:T(8,128)(2,1)}), bf16[24,2,128,128]{3,2,1,0:T(8,128)(2,1)}, u32[]{:S(2)}, u32[]{:S(2)}) async-start(bf16[24,2,128,128]{3,2,1,0:T(8,128)(2,1)} %select.21), calls=%async_computation.2 | async-start | bytes 3145728 | tf_op jit(solution)/shard_map/all_to_all | solution.py:366
  118.8 34.9 %collective-permute-start.17 = (bf16[1,2,128,128]{3,2,1,0:T(8,128)(2,1)}, bf16[1,2,128,128]{3,2,1,0:T(8,128)(2,1)}, u32[]{:S(2)}, u32[]{:S(2)}) collective-permute-start(bf16[1,2,128,128]{3,2,1,0:T(8,128)(2,1)} %get-tuple-element.132), channel_id=1, source_target_pairs={{0,4},{4,8},{8,12},{12,16},{16,20},{20,24},{24,28},{28,32},{32,36}... | collective-permute-start | bytes 196616 | tf_op jit(solution)/shard_map/ppermute | solution.py:444
  120.8 32.9 %collective-permute-start.18 = (bf16[1,2,128,128]{3,2,1,0:T(8,128)(2,1)}, bf16[1,2,128,128]{3,2,1,0:T(8,128)(2,1)}, u32[]{:S(2)}, u32[]{:S(2)}) collective-permute-start(bf16[1,2,128,128]{3,2,1,0:T(8,128)(2,1)} %get-tuple-element.131), channel_id=1, source_target_pairs={{4,0},{8,4},{12,8},{16,12},{20,16},{24,20},{28,24},{32,28},{36,32}... | collective-permute-start | bytes 196616 | tf_op jit(solution)/shard_map/ppermute | solution.py:445
  153.7 8.1 %copy-start.23 = (bf16[2,2,128,128]{3,2,1,0:T(8,128)(2,1)S(1)}, bf16[2,2,128,128]{3,2,1,0:T(8,128)(2,1)}, u32[]{:S(2)}) copy-start(bf16[2,2,128,128]{3,2,1,0:T(8,128)(2,1)} %slice.66) | copy-start | bytes 393220
  153.7 120.9 %all-to-all-start.3 = ((bf16[64,2,128,128]{3,2,1,0:T(8,128)(2,1)}), bf16[64,2,128,128]{3,2,1,0:T(8,128)(2,1)}, u32[]{:S(2)}, u32[]{:S(2)}) async-start(bf16[64,2,128,128]{3,2,1,0:T(8,128)(2,1)} %get-tuple-element.99), calls=%async_computation.3 | async-start | bytes 8388608 | tf_op jit(solution)/shard_map/all_to_all | solution.py:366
  161.8 21.5 %copy-start.13 = (f32[2,9,8,128]{3,2,1,0:T(8,128)S(1)}, f32[2,9,8,128]{3,2,1,0:T(8,128)}, u32[]{:S(2)}) copy-start(f32[2,9,8,128]{3,2,1,0:T(8,128)} %copy.109.ld_ref) | copy-start | bytes 221188
  163.1 0.7 collective-permute-start.19
  163.8 13.0 %collective-permute-start.20 = (bf16[4,128,128]{2,1,0:T(8,128)(2,1)S(1)}, bf16[4,128,128]{2,1,0:T(8,128)(2,1)S(1)}, u32[]{:S(2)}, u32[]{:S(2)}) collective-permute-start(bf16[4,128,128]{2,1,0:T(8,128)(2,1)S(1)} %broadcast_select_fusion), channel_id=1, source_target_pairs={{0,8},{4,12},{1,9},{5,13},{2,10},{6,14},{3,11},{7,15},{32,40},{36,... | collective-permute-start | bytes 393224 | tf_op jit(solution)/shard_map/ppermute | solution.py:392
  176.9 6.4 %collective-permute-start.21 = (bf16[4,128,128]{2,1,0:T(8,128)(2,1)S(1)}, bf16[4,128,128]{2,1,0:T(8,128)(2,1)S(1)}, u32[]{:S(2)}, u32[]{:S(2)}) collective-permute-start(bf16[4,128,128]{2,1,0:T(8,128)(2,1)S(1)} %broadcast_select_fusion.1), channel_id=1, source_target_pairs={{0,16},{4,20},{8,24},{12,28},{1,17},{5,21},{9,25},{13,29},{2,18},{... | collective-permute-start | bytes 393224 | tf_op jit(solution)/shard_map/ppermute | solution.py:392
  205.5 30.3 %copy-start.16 = (bf16[2304,128]{1,0:T(8,128)(2,1)}, bf16[2304,128]{1,0:T(8,128)(2,1)S(1)}, u32[]{:S(2)}) copy-start(bf16[2304,128]{1,0:T(8,128)(2,1)S(1)} %get-tuple-element.92) | copy-start | bytes 1769476
  205.5 14.6 %collective-permute-start.25 = (f32[2,2,128,128]{3,2,1,0:T(8,128)S(1)}, f32[2,2,128,128]{3,2,1,0:T(8,128)S(1)}, u32[]{:S(2)}, u32[]{:S(2)}) collective-permute-start(f32[2,2,128,128]{3,2,1,0:T(8,128)S(1)} %get-tuple-element.91), channel_id=1, source_target_pairs={{16,0},{20,4},{24,8},{28,12},{17,1},{21,5},{25,9},{29,13},{18,2},{... | collective-permute-start | bytes 786440 | tf_op jit(solution)/shard_map/ppermute | solution.py:401
  206.8 28.8 %collective-permute-start.22 = (bf16[2304,128]{1,0:T(8,128)(2,1)S(1)}, bf16[2304,128]{1,0:T(8,128)(2,1)S(1)}, u32[]{:S(2)}, u32[]{:S(2)}) collective-permute-start(bf16[2304,128]{1,0:T(8,128)(2,1)S(1)} %get-tuple-element.88), channel_id=1, source_target_pairs={{0,1},{1,2},{2,3},{3,0},{4,5},{5,6},{6,7},{7,4},{8,9},{9,10},{10,1... | collective-permute-start | bytes 1769480 | tf_op jit(solution)/shard_map/ppermute | solution.py:370
  206.9 28.9 %collective-permute-start.23 = (bf16[2304,128]{1,0:T(8,128)(2,1)S(1)}, bf16[2304,128]{1,0:T(8,128)(2,1)S(1)}, u32[]{:S(2)}, u32[]{:S(2)}) collective-permute-start(bf16[2304,128]{1,0:T(8,128)(2,1)S(1)} %get-tuple-element.89), channel_id=1, source_target_pairs={{0,2},{1,3},{2,0},{3,1},{4,6},{5,7},{6,4},{7,5},{8,10},{9,11},{10,... | collective-permute-start | bytes 1769480 | tf_op jit(solution)/shard_map/ppermute | solution.py:370
  214.2 21.7 %collective-permute-start.24 = (bf16[2304,128]{1,0:T(8,128)(2,1)S(1)}, bf16[2304,128]{1,0:T(8,128)(2,1)S(1)}, u32[]{:S(2)}, u32[]{:S(2)}) collective-permute-start(bf16[2304,128]{1,0:T(8,128)(2,1)S(1)} %get-tuple-element.90), channel_id=1, source_target_pairs={{0,3},{1,0},{2,1},{3,2},{4,7},{5,4},{6,5},{7,6},{8,11},{9,8},{10,9... | collective-permute-start | bytes 1769480 | tf_op jit(solution)/shard_map/ppermute | solution.py:370
  220.2 14.7 %collective-permute-start.26 = (f32[2,2,128,128]{3,2,1,0:T(8,128)S(1)}, f32[2,2,128,128]{3,2,1,0:T(8,128)S(1)}, u32[]{:S(2)}, u32[]{:S(2)}) collective-permute-start(f32[2,2,128,128]{3,2,1,0:T(8,128)S(1)} %add.132), channel_id=1, source_target_pairs={{8,0},{12,4},{9,1},{13,5},{10,2},{14,6},{11,3},{15,7},{40,32},{44,... | collective-permute-start | bytes 786440 | tf_op jit(solution)/shard_map/ppermute | solution.py:401
  234.9 0.7 collective-permute-start.27
  241.3 19.4 %collective-permute-start.28 = (bf16[2,2,128,128]{3,2,1,0:T(8,128)(2,1)S(1)}, bf16[2,2,128,128]{3,2,1,0:T(8,128)(2,1)S(1)}, u32[]{:S(2)}, u32[]{:S(2)}) collective-permute-start(bf16[2,2,128,128]{3,2,1,0:T(8,128)(2,1)S(1)} %convert_element_type.28), channel_id=1, source_target_pairs={{128,0},{160,32},{192,64},{224,96},{129,1},{161,33},{193,65},{225,... | collective-permute-start | bytes 393224 | tf_op jit(solution)/shard_map/ppermute | solution.py:461
  242.6 8.8 %collective-permute-start.29 = (bf16[1,2,128,128]{3,2,1,0:T(8,128)(2,1)S(1)}, bf16[1,2,128,128]{3,2,1,0:T(8,128)(2,1)S(1)}, u32[]{:S(2)}, u32[]{:S(2)}) collective-permute-start(bf16[1,2,128,128]{3,2,1,0:T(8,128)(2,1)S(1)} %get-tuple-element.128), channel_id=1, source_target_pairs={{4,0},{8,4},{12,8},{16,12},{20,16},{24,20},{28,24},{32,28},{36,32}... | collective-permute-start | bytes 196616 | tf_op jit(solution)/shard_map/ppermute | solution.py:459
  249.5 5.6 %collective-permute-start.30 = (bf16[1,2,128,128]{3,2,1,0:T(8,128)(2,1)S(1)}, bf16[1,2,128,128]{3,2,1,0:T(8,128)(2,1)S(1)}, u32[]{:S(2)}, u32[]{:S(2)}) collective-permute-start(bf16[1,2,128,128]{3,2,1,0:T(8,128)(2,1)S(1)} %get-tuple-element.127), channel_id=1, source_target_pairs={{0,4},{4,8},{8,12},{12,16},{16,20},{20,24},{24,28},{28,32},{32,36}... | collective-permute-start | bytes 196616 | tf_op jit(solution)/shard_map/ppermute | solution.py:460
  260.7 13.8 %collective-permute-start.31 = (bf16[2,2,128,128]{3,2,1,0:T(8,128)(2,1)S(1)}, bf16[2,2,128,128]{3,2,1,0:T(8,128)(2,1)S(1)}, u32[]{:S(2)}, u32[]{:S(2)}) collective-permute-start(bf16[2,2,128,128]{3,2,1,0:T(8,128)(2,1)S(1)} %fusion), channel_id=1, source_target_pairs={{32,0},{33,1},{34,2},{35,3},{36,4},{37,5},{38,6},{39,7},{40,8},{41... | collective-permute-start | bytes 393224 | tf_op jit(solution)/shard_map/ppermute | solution.py:465
  262.0 12.5 %collective-permute-start.32 = (bf16[2,2,128,128]{3,2,1,0:T(8,128)(2,1)S(1)}, bf16[2,2,128,128]{3,2,1,0:T(8,128)(2,1)S(1)}, u32[]{:S(2)}, u32[]{:S(2)}) collective-permute-start(bf16[2,2,128,128]{3,2,1,0:T(8,128)(2,1)S(1)} %fusion), channel_id=1, source_target_pairs={{64,0},{65,1},{66,2},{67,3},{68,4},{69,5},{70,6},{71,7},{72,8},{73... | collective-permute-start | bytes 393224 | tf_op jit(solution)/shard_map/ppermute | solution.py:465
  263.3 11.2 %collective-permute-start.33 = (bf16[2,2,128,128]{3,2,1,0:T(8,128)(2,1)S(1)}, bf16[2,2,128,128]{3,2,1,0:T(8,128)(2,1)S(1)}, u32[]{:S(2)}, u32[]{:S(2)}) collective-permute-start(bf16[2,2,128,128]{3,2,1,0:T(8,128)(2,1)S(1)} %fusion), channel_id=1, source_target_pairs={{96,0},{97,1},{98,2},{99,3},{100,4},{101,5},{102,6},{103,7},{104,8... | collective-permute-start | bytes 393224 | tf_op jit(solution)/shard_map/ppermute | solution.py:465
  (22 other events, 36.7 us)
